TPU v7x, 128 devices: a whole 4x4x4 slice. The times are simulated.
128 devices in a mesh: space: 16 (over y, x_lo, core), sample: 8 (over z, x_hi).
Axes of the slice: x: 4 (x_hi: 2, x_lo: 2; x = x_hi * 2 + x_lo), y: 4, z: 4, core: 2. Of those that a mesh axis runs over, the one named last changes fastest.
Arguments:
- fields: bfloat16 [8, 64, 20, 8192], P('sample', 'space'), may hold values from -6 to 6
- cotangent: bfloat16 [8, 64, 20, 8192], P('sample', 'space'), may hold values from -6 to 6
- spectral_weight: bfloat16 [2, 20, 20, 4608], P(None, None, None, 'space'), may hold values from -6 to 6
- point_weight: bfloat16 [20, 20], replicated, may hold values from -1.25 to 1.25
- point_bias: float32 [20], replicated, may hold values from -1 to 1
Outputs:
- activated: bfloat16 [8, 64, 20, 8192], P('sample', 'space')
- grad_input: bfloat16 [8, 64, 20, 8192], P('sample', 'space')
- grad_spectral: float32 [2, 20, 20, 4608], P(None, None, None, ('space', 'sample'))
All inputs are finite; a program needn't handle non-finite values.
Results may differ from a plain program's by a relative error of at most 0.001.
Values sent between devices are 32-bit elements; how exact they have to be, the bound alone decides.
No kernel may reach another device: no remote copies, remote signals or barrier semaphores. Data moves between devices by JAX's collectives and lax.ppermute only.
A program may use at most 128 MiB of HBM per device.

v0:
```python
import math

import jax
import jax.numpy as jnp
from jax import lax
from jax.sharding import PartitionSpec as P

NX = 64
NY = 64
NZ = 32
NT = 4
MX = 12
MY = 12
MZ = 8
MT = 4


HIGHEST_PRECISION = lax.Precision.HIGHEST


def in_one_piece(arrays, axis, split_dim, concat_dim, along):
    both = jnp.concatenate(arrays, axis=along)
    result, at, gathered = (
        lax.all_to_all(both, axis, split_axis=split_dim, concat_axis=concat_dim, tiled=True),
        0,
        [],
    )
    for a in arrays:
        gathered.append(lax.slice_in_dim(result, at, at + a.shape[along], axis=along))
        at += a.shape[along]
    return tuple(gathered)


def signed_freq(index, modes):
    return jnp.where(index < modes // 2, index, index - modes)


def line_table(length, modes):
    position = jnp.arange(length, dtype=jnp.int32)[:, None]
    frequency = signed_freq(jnp.arange(modes, dtype=jnp.int32)[None, :], modes)
    angle = jnp.mod(frequency * position, length).astype(jnp.float32) * (2.0 * math.pi / length)
    return (jnp.cos(angle), jnp.sin(angle))


def plane_table(depth, steps, depth_modes, step_modes):
    depth_pos = jnp.arange(depth, dtype=jnp.int32)[:, None, None, None]
    step_pos = jnp.arange(steps, dtype=jnp.int32)[None, :, None, None]
    depth_freq = signed_freq(
        jnp.arange(depth_modes, dtype=jnp.int32)[None, None, :, None], depth_modes
    )
    step_freq = signed_freq(
        jnp.arange(step_modes, dtype=jnp.int32)[None, None, None, :], step_modes
    )
    phase = jnp.mod(
        jnp.mod(depth_freq * depth_pos, depth) * steps
        + jnp.mod(step_freq * step_pos, steps) * depth,
        depth * steps,
    )
    angle = phase.astype(jnp.float32) * (2.0 * math.pi / (depth * steps))
    shape_out = (depth * steps, depth_modes * step_modes)
    return (jnp.cos(angle).reshape(shape_out), jnp.sin(angle).reshape(shape_out))


def contract(pattern, left, table):
    return jnp.einsum(pattern, left, table, precision=HIGHEST_PRECISION)


def forward_pair(real_part, imag_part, cosine, sine, pattern):
    return (
        contract(pattern, real_part, cosine) + contract(pattern, imag_part, sine),
        contract(pattern, imag_part, cosine) - contract(pattern, real_part, sine),
    )


def inverse_pair(real_part, imag_part, cosine, sine, pattern):
    return (
        contract(pattern, real_part, cosine) - contract(pattern, imag_part, sine),
        contract(pattern, imag_part, cosine) + contract(pattern, real_part, sine),
    )


def gelu_slope(values):
    return 0.5 * (1.0 + lax.erf(values * (1.0 / math.sqrt(2.0)))) + values * jnp.exp(
        -0.5 * values * values
    ) * (1.0 / math.sqrt(2.0 * math.pi))


def grad_terms(spec_in, spec_up):
    grad_real = contract("scm,som->com", spec_in[0], spec_up[0]) + contract(
        "scm,som->com", spec_in[1], spec_up[1]
    )
    grad_imag = contract("scm,som->com", spec_in[0], spec_up[1]) - contract(
        "scm,som->com", spec_in[1], spec_up[0]
    )
    return jnp.stack([grad_real, grad_imag])


def shards(fields, cotangent, spectral_weight, point_weight, point_bias):
    batch, slab_rows, channels, columns = fields.shape
    plane_cos, plane_sin = plane_table(NZ, NT, MZ, MT)
    y_cos, y_sin = line_table(NY, MY)
    x_cos, x_sin = line_table(NX, MX)
    plane_modes = MZ * MT
    owned = plane_modes // lax.axis_size("space")
    volume = NX * NY * NZ * NT

    def slab_to_owner(field_in, scale):
        blocked = field_in.reshape(batch, slab_rows, channels, NY, NZ * NT)
        real_part = contract("sxcyn,nq->sxcqy", blocked, plane_cos) * scale
        imag_part = contract("sxcyn,nq->sxcqy", blocked, plane_sin) * -scale
        along_y = forward_pair(real_part, imag_part, y_cos, y_sin, "sxcqy,yk->sxcqk")
        stacked = jnp.stack(along_y).reshape(2, batch, slab_rows, channels, plane_modes * MY)
        received = lax.all_to_all(stacked, "space", split_axis=4, concat_axis=2, tiled=True)
        items = received.shape[3]
        along_x = forward_pair(received[0], received[1], x_cos, x_sin, "sxcm,xk->scmk")
        return jnp.stack(along_x).reshape(2, batch, items, owned * MY * MX)

    def owner_to_slab(spectral_in):
        outputs = spectral_in.shape[2]
        blocked_modes = spectral_in.reshape(2, batch, outputs, owned * MY, MX)
        along_x = inverse_pair(blocked_modes[0], blocked_modes[1], x_cos, x_sin, "somk,xk->sxom")
        stacked = jnp.stack(along_x)
        received = lax.all_to_all(stacked, "space", split_axis=2, concat_axis=4, tiled=True)
        items = received.shape[3]
        split_modes = received.reshape(2, batch, slab_rows, items, plane_modes, MY)
        along_y = inverse_pair(split_modes[0], split_modes[1], y_cos, y_sin, "sxoqk,yk->sxoqy")
        real_out = contract("sxoqy,nq->sxoyn", along_y[0], plane_cos) - contract(
            "sxoqy,nq->sxoyn", along_y[1], plane_sin
        )
        return real_out.reshape(batch, slab_rows, items, NY * NZ * NT)

    weights = spectral_weight.astype(jnp.float32)
    spec_in = slab_to_owner(fields, 1.0)
    mixed_real = contract("com,scm->som", weights[0], spec_in[0]) - contract(
        "com,scm->som", weights[1], spec_in[1]
    )
    mixed_imag = contract("com,scm->som", weights[0], spec_in[1]) + contract(
        "com,scm->som", weights[1], spec_in[0]
    )
    spectral = owner_to_slab(jnp.stack([mixed_real, mixed_imag])) * (1.0 / volume)
    local = jnp.einsum("sxcn,co->sxon", fields, point_weight, preferred_element_type=jnp.float32)
    pre = spectral + local + point_bias[None, None, :, None]
    activated = jax.nn.gelu(pre, approximate=False).astype(jnp.bfloat16)
    upstream = cotangent.astype(jnp.float32) * gelu_slope(pre)
    spec_up = slab_to_owner(upstream, 1.0 / volume)
    back_real = contract("com,som->scm", weights[0], spec_up[0]) + contract(
        "com,som->scm", weights[1], spec_up[1]
    )
    back_imag = contract("com,som->scm", weights[0], spec_up[1]) - contract(
        "com,som->scm", weights[1], spec_up[0]
    )
    back = owner_to_slab(jnp.stack([back_real, back_imag]))
    point_full = point_weight.astype(jnp.float32)
    grad_input = (back + contract("sxon,co->sxcn", upstream, point_full)).astype(jnp.bfloat16)
    all_in, all_up = in_one_piece((spec_in, spec_up), "sample", 3, 1, 0)
    grad_spectral = grad_terms(all_in, all_up)
    return (activated, grad_input, grad_spectral)


def solution(mesh):
    return jax.shard_map(
        shards,
        mesh=mesh,
        in_specs=(
            P("sample", "space", None, None),
            P("sample", "space", None, None),
            P(None, None, None, "space"),
            P(),
            P(),
        ),
        out_specs=(
            P("sample", "space", None, None),
            P("sample", "space", None, None),
            P(None, None, None, ("space", "sample")),
        ),
        check_vma=False,
    )
```

profile of v0, /device:TPU:1, one launch (start us, length us, event | category | flops | bytes accessed | tf_op | source)
XLA Modules:
  0.0 260.9 jit_solution(18208793548036887955)
XLA Ops:
  5.1 3.6 %fusion.23 = f32[4,20,32,64]{3,2,1,0:T(8,128)S(1)} fusion(bf16[4,20,64,128]{3,2,0,1:T(8,128)(2,1)S(1)} %reshape.511, f32[128,32,1,1]{0,1,2,3:T(8,128)S(1)} %reshape.538), kind=kOutput, calls=%fused_computation.45 | convolution fusion | flops 251822080 | bytes 1982464 | tf_op jit(solution)/shard_map/sxcyn,nq->sxcqy/dot_general | solution.py:65
  8.7 3.6 %convolution_bitcast_fusion.2 = f32[4,20,32,64]{3,2,1,0:T(8,128)S(1)} fusion(bf16[4,20,64,128]{3,2,0,1:T(8,128)(2,1)S(1)} %reshape.511, f32[128,32,1,1]{0,1,2,3:T(8,128)S(1)} %reshape.536), kind=kOutput, calls=%fused_computation.43 | convolution fusion | flops 251658240 | bytes 1982464 | tf_op jit(solution)/shard_map/sxcyn,nq->sxcqy/dot_general | solution.py:65
  12.4 5.3 %fusion.93 = f32[4,20,32,12]{2,3,1,0:T(8,128)S(1)} fusion(f32[4,20,32,64]{3,2,1,0:T(8,128)S(1)} %convolution_bitcast_fusion.2, s32[12]{0:T(128)S(1)} %compare_select_fusion.2), kind=kOutput, calls=%fused_computation.162 | convolution fusion | flops 23603712 | bytes 778288 | tf_op jit(solution)/shard_map/sxcqy,yk->sxcqk/dot_general | solution.py:65
  17.6 5.3 %fusion.91 = f32[4,20,32,12]{2,3,1,0:T(8,128)S(1)} fusion(f32[4,20,32,64]{3,2,1,0:T(8,128)S(1)} %fusion.23, s32[12]{0:T(128)S(1)} %compare_select_fusion.2), kind=kOutput, calls=%fused_computation.160 | convolution fusion | flops 23603712 | bytes 778288 | tf_op jit(solution)/shard_map/sxcqy,yk->sxcqk/dot_general | solution.py:65
  22.9 5.3 %convolution_add_fusion.3 = f32[4,20,32,12]{2,3,1,0:T(8,128)S(1)} fusion(f32[4,20,32,12]{2,3,1,0:T(8,128)S(1)} %fusion.93, f32[4,20,32,64]{3,2,1,0:T(8,128)S(1)} %fusion.23, s32[12]{0:T(128)S(1)} %compare_select_fusion.2), kind=kOutput, calls=%fused_computation.49 | convolution fusion | flops 23634432 | bytes 901168 | tf_op jit(solution)/shard_map/sxcqy,yk->sxcqk/dot_general | solution.py:65
  28.2 5.6 %convolution_subtract_fusion.4 = f32[4,20,32,12]{2,3,1,0:T(8,128)S(1)} fusion(f32[4,20,32,12]{2,3,1,0:T(8,128)S(1)} %fusion.91, f32[4,20,32,64]{3,2,1,0:T(8,128)S(1)} %convolution_bitcast_fusion.2, s32[12]{0:T(128)S(1)} %compare_select_fusion.2), kind=kOutput, calls=%fused_computation.48 | convolution fusion | flops 23634432 | bytes 901168 | tf_op jit(solution)/shard_map/sxcqy,yk->sxcqk/dot_general | solution.py:65
  37.8 2.8 %reshape.567 = f32[16,1,3840]{2,1,0:T(1,128)} reshape(f32[384,2,1,4,20]{4,3,2,1,0:T(4,128)S(1)} %bitcast.336) | data formatting | bytes 491520
  40.6 6.9 %all-to-all-start = ((f32[16,1,3840]{2,1,0:T(1,128)}), f32[16,1,3840]{2,1,0:T(1,128)S(1)}, u32[]{:S(2)}, u32[]{:S(2)}) async-start(f32[16,1,3840]{2,1,0:T(1,128)} %reshape.567), calls=%async_computation | async-start | bytes 491520 | tf_op jit(solution)/shard_map/all_to_all | solution.py:113
  49.9 4.7 %all-to-all-done = f32[16,1,3840]{2,1,0:T(1,128)S(1)} async-done(((f32[16,1,3840]{2,1,0:T(1,128)}), f32[16,1,3840]{2,1,0:T(1,128)S(1)}, u32[]{:S(2)}, u32[]{:S(2)}) %all-to-all-start) | async-done | bytes 245792 | tf_op jit(solution)/shard_map/all_to_all | solution.py:113
  69.0 3.0 %reshape.569 = f32[16,1,3840]{2,1,0:T(1,128)} reshape(f32[64,1,20,2,24]{4,3,2,1,0:T(2,128)S(1)} %bitcast.356) | data formatting | bytes 491520
  72.1 4.4 %all-to-all-start.1 = ((f32[16,1,3840]{2,1,0:T(1,128)}), f32[16,1,3840]{2,1,0:T(1,128)S(1)}, u32[]{:S(2)}, u32[]{:S(2)}) async-start(f32[16,1,3840]{2,1,0:T(1,128)} %reshape.569), calls=%async_computation.1 | async-start | bytes 491520 | tf_op jit(solution)/shard_map/all_to_all | solution.py:123
  76.9 6.6 %all-to-all-done.1 = f32[16,1,3840]{2,1,0:T(1,128)S(1)} async-done(((f32[16,1,3840]{2,1,0:T(1,128)}), f32[16,1,3840]{2,1,0:T(1,128)S(1)}, u32[]{:S(2)}, u32[]{:S(2)}) %all-to-all-start.1) | async-done | bytes 245792 | tf_op jit(solution)/shard_map/all_to_all | solution.py:123
  100.9 4.3 %fusion.54 = f32[4,20,64,128]{3,2,1,0:T(8,128)S(1)} fusion(f32[4,20,32,64]{3,2,1,0:T(8,128)S(1)} %convolution_subtract_fusion.2, s32[128,32]{0,1:T(8,128)S(1)} %add.367), kind=kOutput, calls=%fused_computation.120 | convolution fusion | flops 251711488 | bytes 3293184 | tf_op jit(solution)/shard_map/sxoqy,nq->sxoyn/dot_general | solution.py:65
  105.2 4.3 %subtract_multiply_fusion = f32[4,20,64,128]{3,2,1,0:T(8,128)S(1)} fusion(f32[4,20,64,128]{3,2,1,0:T(8,128)S(1)} %fusion.54, f32[4,20,32,64]{3,2,1,0:T(8,128)S(1)} %convolution_add_fusion.1, s32[128,32]{0,1:T(8,128)S(1)} %add.367), kind=kOutput, calls=%fused_computation.32 | convolution fusion | flops 253022208 | bytes 5914624 | tf_op jit(solution)/shard_map/sxoqy,nq->sxoyn/dot_general | solution.py:65
  111.5 11.9 %fusion.11 = (f32[1,4,20,8192]{3,2,1,0:T(8,128)}, bf16[1,4,20,8192]{3,2,1,0:T(8,128)(2,1)}) fusion(bf16[1,4,20,8192]{3,1,2,0:T(4,128)(2,1)} %param.6, f32[20]{0:T(128)S(1)} %copy-done.7, f32[1,4,20,8192]{3,2,1,0:T(8,128)} %reshape.564, bf16[4,20,8192]{2,0,1:T(4,128)(2,1)} %bitcast.366, bf16[20,20]{1,0:T(8,128)(2,1)S(1)} %copy-done), kind=kOutput, calls=%fused_computation.15 | convolution fusion | flops 76677120 | bytes 9175920 | tf_op jit(solution)/shard_map/sxcn,co->sxon/dot_general | solution.py:141
  125.8 7.1 %fusion.22 = f32[4,20,32,64]{3,2,1,0:T(8,128)S(1)} fusion(f32[4,20,64,128]{3,2,1,0:T(8,128)S(1)} %reshape.565, f32[128,32,1,1]{0,1,2,3:T(8,128)S(1)} %reshape.536), kind=kOutput, calls=%fused_computation.40 | convolution fusion | flops 251822080 | bytes 3293184 | tf_op jit(solution)/shard_map/sxcyn,nq->sxcqy/dot_general | solution.py:65
  133.0 7.2 %fusion.21 = f32[4,20,32,64]{3,2,1,0:T(8,128)S(1)} fusion(f32[4,20,64,128]{3,2,1,0:T(8,128)S(1)} %reshape.565, f32[128,32,1,1]{0,1,2,3:T(8,128)S(1)} %reshape.538), kind=kOutput, calls=%fused_computation.38 | convolution fusion | flops 251822080 | bytes 3293184 | tf_op jit(solution)/shard_map/sxcyn,nq->sxcqy/dot_general | solution.py:65
  140.1 5.2 %fusion.83 = f32[4,20,32,12]{2,3,1,0:T(8,128)S(1)} fusion(f32[4,20,32,64]{3,2,1,0:T(8,128)S(1)} %fusion.21, s32[12]{0:T(128)S(1)} %compare_select_fusion.2), kind=kOutput, calls=%fused_computation.152 | convolution fusion | flops 23603712 | bytes 778288 | tf_op jit(solution)/shard_map/sxcqy,yk->sxcqk/dot_general | solution.py:65
  145.4 5.6 %fusion.85 = f32[4,20,32,12]{2,3,1,0:T(8,128)S(1)} fusion(f32[4,20,32,64]{3,2,1,0:T(8,128)S(1)} %fusion.22, s32[12]{0:T(128)S(1)} %compare_select_fusion.2), kind=kOutput, calls=%fused_computation.154 | convolution fusion | flops 23603712 | bytes 778288 | tf_op jit(solution)/shard_map/sxcqy,yk->sxcqk/dot_general | solution.py:65
  151.0 5.3 %convolution_subtract_fusion.3 = f32[4,20,32,12]{2,3,1,0:T(8,128)S(1)} fusion(f32[4,20,32,12]{2,3,1,0:T(8,128)S(1)} %fusion.83, f32[4,20,32,64]{3,2,1,0:T(8,128)S(1)} %fusion.22, s32[12]{0:T(128)S(1)} %compare_select_fusion.2), kind=kOutput, calls=%fused_computation.46 | convolution fusion | flops 23634432 | bytes 901168 | tf_op jit(solution)/shard_map/sxcqy,yk->sxcqk/dot_general | solution.py:65
  156.3 5.3 %convolution_add_fusion.2 = f32[4,20,32,12]{2,3,1,0:T(8,128)S(1)} fusion(f32[4,20,32,12]{2,3,1,0:T(8,128)S(1)} %fusion.85, f32[4,20,32,64]{3,2,1,0:T(8,128)S(1)} %fusion.21, s32[12]{0:T(128)S(1)} %compare_select_fusion.2), kind=kOutput, calls=%fused_computation.47 | convolution fusion | flops 23634432 | bytes 901168 | tf_op jit(solution)/shard_map/sxcqy,yk->sxcqk/dot_general | solution.py:65
  168.3 4.5 %all-to-all-start.2 = ((f32[16,1,3840]{2,1,0:T(1,128)}), f32[16,1,3840]{2,1,0:T(1,128)S(1)}, u32[]{:S(2)}, u32[]{:S(2)}) async-start(f32[16,1,3840]{2,1,0:T(1,128)} %reshape.571), calls=%async_computation.2 | async-start | bytes 491520 | tf_op jit(solution)/shard_map/all_to_all | solution.py:113
  173.1 3.5 %copy.217 = bf16[1,4,20,8192]{3,1,2,0:T(4,128)(2,1)} copy(bf16[1,4,20,8192]{3,2,1,0:T(8,128)(2,1)} %get-tuple-element.28) | data formatting | bytes 2621440
  176.6 3.2 %all-to-all-done.2 = f32[16,1,3840]{2,1,0:T(1,128)S(1)} async-done(((f32[16,1,3840]{2,1,0:T(1,128)}), f32[16,1,3840]{2,1,0:T(1,128)S(1)}, u32[]{:S(2)}, u32[]{:S(2)}) %all-to-all-start.2) | async-done | bytes 245792 | tf_op jit(solution)/shard_map/all_to_all | solution.py:113
  197.9 7.2 %all-to-all-start.4 = ((f32[8,1,2880]{2,1,0:T(1,128)}), f32[8,1,2880]{2,1,0:T(1,128)S(1)}, u32[]{:S(2)}, u32[]{:S(2)}) async-start(f32[8,1,2880]{2,1,0:T(1,128)} %reshape.575), calls=%async_computation.4 | async-start | bytes 188416 | tf_op jit(solution)/shard_map/all_to_all | solution.py:24
  206.0 3.0 %reshape.573 = f32[16,1,3840]{2,1,0:T(1,128)} reshape(f32[64,1,20,2,24]{4,3,2,1,0:T(2,128)S(1)} %bitcast.358) | data formatting | bytes 491520
  209.0 2.9 %all-to-all-done.4 = f32[8,1,2880]{2,1,0:T(1,128)S(1)} async-done(((f32[8,1,2880]{2,1,0:T(1,128)}), f32[8,1,2880]{2,1,0:T(1,128)S(1)}, u32[]{:S(2)}, u32[]{:S(2)}) %all-to-all-start.4) | async-done | bytes 92192 | tf_op jit(solution)/shard_map/all_to_all | solution.py:24
  212.0 6.1 %all-to-all-start.3 = ((f32[16,1,3840]{2,1,0:T(1,128)}), f32[16,1,3840]{2,1,0:T(1,128)S(1)}, u32[]{:S(2)}, u32[]{:S(2)}) async-start(f32[16,1,3840]{2,1,0:T(1,128)} %reshape.573), calls=%async_computation.3 | async-start | bytes 491520 | tf_op jit(solution)/shard_map/all_to_all | solution.py:123
  240.9 4.3 %fusion.52 = f32[4,20,64,128]{3,2,1,0:T(8,128)S(1)} fusion(f32[4,20,32,64]{3,2,1,0:T(8,128)S(1)} %convolution_subtract_fusion.1, s32[128,32]{0,1:T(8,128)S(1)} %add.367), kind=kOutput, calls=%fused_computation.118 | convolution fusion | flops 251711488 | bytes 3293184 | tf_op jit(solution)/shard_map/sxoqy,nq->sxoyn/dot_general | solution.py:65
  245.2 6.1 %convolution_subtract_fusion = f32[4,20,64,128]{3,2,1,0:T(8,128)} fusion(f32[4,20,64,128]{3,2,1,0:T(8,128)S(1)} %fusion.52, f32[4,20,32,64]{3,2,1,0:T(8,128)S(1)} %convolution_add_fusion, s32[128,32]{0,1:T(8,128)S(1)} %add.367), kind=kOutput, calls=%fused_computation.33 | convolution fusion | flops 252366848 | bytes 5914624 | tf_op jit(solution)/shard_map/sxoqy,nq->sxoyn/dot_general | solution.py:65
  251.3 3.4 %reshape.566 = f32[1,4,20,8192]{3,2,1,0:T(8,128)} reshape(f32[4,20,64,128]{3,2,1,0:T(8,128)} %convolution_subtract_fusion) | data formatting | bytes 5242880 | tf_op jit(solution)/shard_map/reshape | solution.py:130
  254.7 3.9 %fusion.3 = bf16[1,4,20,8192]{3,2,1,0:T(8,128)(2,1)S(1)} fusion(f32[1,4,20,8192]{3,2,1,0:T(8,128)} %reshape.566, f32[1,4,20,8192]{3,2,1,0:T(8,128)S(1)} %copy-done.1, bf16[20,20]{1,0:T(8,128)(2,1)S(1)} %copy-done), kind=kOutput, calls=%fused_computation.5 | convolution fusion | flops 158597120 | bytes 6554400 | tf_op jit(solution)/shard_map/sxon,co->sxcn/dot_general | solution.py:65
  (137 shorter events, 97.8 us)
Async XLA Ops:
  0.6 110.9 %copy-start = (bf16[20,20]{1,0:T(8,128)(2,1)S(1)}, bf16[20,20]{1,0:T(8,128)(2,1)}, u32[]{:S(2)}) copy-start(bf16[20,20]{1,0:T(8,128)(2,1)} %param.8) | copy-start | bytes 2404
  0.6 2.9 %copy-start.6 = (bf16[1,4,20,8192]{3,1,2,0:T(4,128)(2,1)S(1)}, bf16[1,4,20,8192]{3,1,2,0:T(4,128)(2,1)}, u32[]{:S(2)}) copy-start(bf16[1,4,20,8192]{3,1,2,0:T(4,128)(2,1)} %param.5) | copy-start | bytes 3932164
  40.6 14.0 %all-to-all-start = ((f32[16,1,3840]{2,1,0:T(1,128)}), f32[16,1,3840]{2,1,0:T(1,128)S(1)}, u32[]{:S(2)}, u32[]{:S(2)}) async-start(f32[16,1,3840]{2,1,0:T(1,128)} %reshape.567), calls=%async_computation | async-start | bytes 491520 | tf_op jit(solution)/shard_map/all_to_all | solution.py:113
  49.9 15.8 %copy-start.2 = (bf16[1,20,20,288]{3,0,2,1:T(2,128)(2,1)}, bf16[1,20,20,288]{3,0,2,1:T(2,128)(2,1)S(1)}, u32[]{:S(2)}) copy-start(bf16[1,20,20,288]{3,0,2,1:T(2,128)(2,1)S(1)} %get-tuple-element.38) | copy-start | bytes 691204
  65.5 2.7 %copy-start.4 = (f32[20,24,12]{2,1,0:T(8,128)}, f32[20,24,12]{2,1,0:T(8,128)S(1)}, u32[]{:S(2)}) copy-start(f32[20,24,12]{2,1,0:T(8,128)S(1)} %copy.160) | copy-start | bytes 69124
  72.1 11.4 %all-to-all-start.1 = ((f32[16,1,3840]{2,1,0:T(1,128)}), f32[16,1,3840]{2,1,0:T(1,128)S(1)}, u32[]{:S(2)}, u32[]{:S(2)}) async-start(f32[16,1,3840]{2,1,0:T(1,128)} %reshape.569), calls=%async_computation.1 | async-start | bytes 491520 | tf_op jit(solution)/shard_map/all_to_all | solution.py:123
  109.6 2.0 copy-start.7
  164.6 8.4 %copy-start.5 = (f32[20,24,12]{2,1,0:T(8,128)S(1)}, f32[20,24,12]{2,1,0:T(8,128)}, u32[]{:S(2)}) copy-start(f32[20,24,12]{2,1,0:T(8,128)} %copy-done.4) | copy-start | bytes 69124
  168.3 11.5 %all-to-all-start.2 = ((f32[16,1,3840]{2,1,0:T(1,128)}), f32[16,1,3840]{2,1,0:T(1,128)S(1)}, u32[]{:S(2)}, u32[]{:S(2)}) async-start(f32[16,1,3840]{2,1,0:T(1,128)} %reshape.571), calls=%async_computation.2 | async-start | bytes 491520 | tf_op jit(solution)/shard_map/all_to_all | solution.py:113
  188.1 2.6 %copy-start.3 = (bf16[1,20,20,288]{3,0,2,1:T(2,128)(2,1)S(1)}, bf16[1,20,20,288]{3,0,2,1:T(2,128)(2,1)}, u32[]{:S(2)}) copy-start(bf16[1,20,20,288]{3,0,2,1:T(2,128)(2,1)} %copy-done.2) | copy-start | bytes 691204
  197.9 14.1 %all-to-all-start.4 = ((f32[8,1,2880]{2,1,0:T(1,128)}), f32[8,1,2880]{2,1,0:T(1,128)S(1)}, u32[]{:S(2)}, u32[]{:S(2)}) async-start(f32[8,1,2880]{2,1,0:T(1,128)} %reshape.575), calls=%async_computation.4 | async-start | bytes 188416 | tf_op jit(solution)/shard_map/all_to_all | solution.py:24
  212.0 13.5 %all-to-all-start.3 = ((f32[16,1,3840]{2,1,0:T(1,128)}), f32[16,1,3840]{2,1,0:T(1,128)S(1)}, u32[]{:S(2)}, u32[]{:S(2)}) async-start(f32[16,1,3840]{2,1,0:T(1,128)} %reshape.573), calls=%async_computation.3 | async-start | bytes 491520 | tf_op jit(solution)/shard_map/all_to_all | solution.py:123
  251.3 3.4 %copy-start.1 = (f32[1,4,20,8192]{3,2,1,0:T(8,128)S(1)}, f32[1,4,20,8192]{3,2,1,0:T(8,128)}, u32[]{:S(2)}) copy-start(f32[1,4,20,8192]{3,2,1,0:T(8,128)} %get-tuple-element.27) | copy-start | bytes 7864324
where the time goes:
time: 265 us; the launch traced here: 261 us
  matrix products  130 us (49%)
  local copies, waits for them, and re-layouts  70.3 us (27%)
  starting transfers between devices  29.1 us (11%)
  waiting for transfers between devices  17.4 us (7%)
  other arithmetic  12.5 us (5%)
    dot_general x45, matrix products, contract(): return jnp.einsum(pattern, left, table, precision=HIGHEST_PRECISION)  118 us
    unnamed x28, local copies, waits for them, and re-layouts  28.2 us
    dot_general x1, matrix products, shards(): jnp.einsum('sxcn,co->sxon', fields, point_weight, preferred_element_type=...  11.9 us
    all_to_all x2, starting transfers between devices, slab_to_owner(): lax.all_to_all(stacked, 'space', split_axis=4, concat_axis=2, tiled=True)  11.4 us
    all_to_all x2, starting transfers between devices, owner_to_slab(): lax.all_to_all(stacked, 'space', split_axis=2, concat_axis=4, tiled=True)  10.5 us
    all_to_all x2, waiting for transfers between devices, slab_to_owner(): lax.all_to_all(stacked, 'space', split_axis=4, concat_axis=2, tiled=True)  7.92 us
    another operation x14, local copies, waits for them, and re-layouts  7.33 us
    all_to_all x1, starting transfers between devices, in_one_piece(): lax.all_to_all(both, axis, split_axis=split_dim, concat_axis=concat_dim,...  7.19 us
  transfers between devices with their start and end apart: 5, of which 4 were waited for; matrix products, arithmetic and copies ran while one was open for 7% of the time, Pallas kernels for 0%

commit v1 on v0

v1 whole, which is shorter than its diff:
```python
import functools
import math

import jax
import jax.numpy as jnp
import ml_dtypes
import numpy as np
from jax import lax
from jax.experimental import pallas as pl
from jax.experimental.pallas import tpu as pltpu
from jax.sharding import PartitionSpec as P

NX, NY, NZ, NT = 64, 64, 32, 4
MX, MY, MZ, MT = 12, 12, 8, 4
C = 20
CP = 24
PLANE = NZ * NT
CELLS = NY * PLANE
KEPT_ROWS = C * MY
SLAB = 4
OWNERS = 16
SAMPLES = 8
BLOCK_MODES = 36
PAIRS = C // 2
CHUNK = 8
VOLUME = NX * NY * NZ * NT
F32, BF16 = jnp.float32, jnp.bfloat16
VMEM_LIMIT = 24 * 1024 * 1024


def signed(index, modes):
    return np.where(index < modes // 2, index, index - modes)


def hi_lo(table):
    hi = table.astype(np.float32).astype(ml_dtypes.bfloat16)
    lo = (table - hi.astype(np.float64)).astype(np.float32).astype(ml_dtypes.bfloat16)
    return hi, lo


def y_table():
    k = signed(np.arange(MY), MY)[:, None]
    theta = 2 * np.pi * ((k * np.arange(NY)[None, :]) % NY) / NY
    eye = np.eye(2)
    return np.concatenate([np.kron(eye, np.cos(theta)), np.kron(eye, -np.sin(theta))], axis=0)


def plane_table():
    z = np.arange(PLANE) // NT
    t = np.arange(PLANE) % NT
    rows = []
    for ql in range(2):
        q = 2 * np.arange(OWNERS) + ql
        fz = signed(q // MT, MZ)[:, None]
        ft = signed(q % MT, MT)[:, None]
        phase = (fz * z * NT + ft * t * NZ) % PLANE
        theta = 2 * np.pi * phase / PLANE
        rows.append(np.concatenate([np.cos(theta), np.sin(theta)], axis=1))
        rows.append(np.concatenate([-np.sin(theta), np.cos(theta)], axis=1))
    return np.concatenate(rows, axis=0)


def x_tables(ql, forward_scale, inverse_scale):
    lane = np.arange(256) + 128 * ql
    f = signed(lane % MX, MX)[None, :]
    theta = 2 * np.pi * ((f * np.arange(NX)[:, None]) % NX) / NX
    cos, sin = np.cos(theta), np.sin(theta)
    forward = np.zeros((NX, 2, 512))
    forward[:, 0] = np.concatenate([cos, -sin], axis=1)
    forward[:, 1] = np.concatenate([sin, cos], axis=1)
    inverse = np.zeros((NX, 2, 512))
    inverse[:, 0] = np.concatenate([cos, -sin], axis=1)
    inverse[:, 1] = np.concatenate([sin, cos], axis=1)
    return forward.reshape(128, 512) * forward_scale, inverse.reshape(128, 512) * inverse_scale


def mode_mask():
    mask = np.zeros((2, 24, 512), np.float32)
    for ql in range(2):
        lane = np.arange(256) + 128 * ql
        code = np.where(lane < 288, lane // MX, -1)
        hit = code[None, :] == (ql * MY + np.arange(24)[:, None] % MY)
        mask[ql] = np.concatenate([hit, hit], axis=1)
    return mask


def group_table():
    g = np.zeros((CP, KEPT_ROWS), np.float32)
    for c in range(C):
        g[c, c * MY : (c + 1) * MY] = 1.0
    return g


def split(value):
    hi = value.astype(BF16)
    return hi, (value - hi.astype(F32)).astype(BF16)


def dot(a, b):
    return lax.dot_general(a, b, (((1,), (0,)), ((), ())), preferred_element_type=F32)


def dot_tn(a, b):
    return lax.dot_general(a, b, (((0,), (0,)), ((), ())), preferred_element_type=F32)


def dot_nt(a, b):
    return lax.dot_general(a, b, (((1,), (1,)), ((), ())), preferred_element_type=F32)


def slab_forward(tile_ref, exact, x, ytab, ztab, out_ref):
    real, imag = [], []
    for p in range(PAIRS):
        cells = tile_ref[p * 128 : (p + 1) * 128, :]
        if exact:
            both = dot(ytab[...], cells.astype(BF16))
            u = both[:48] + both[48:]
        else:
            hi, lo = split(cells)
            both = dot(ytab[...], hi)
            u = both[:48] + both[48:] + dot(ytab[:48], lo)
        real.append(u[:24])
        imag.append(u[24:])
    fill = [jnp.zeros((256 - KEPT_ROWS, 128), F32)]
    rows = jnp.concatenate(
        [jnp.concatenate(real + fill, axis=0), jnp.concatenate(imag + fill, axis=0)], axis=1
    )
    hi, lo = split(rows)
    both = dot_nt(ztab[...], hi)
    out = both[:64] + both[64:] + dot_nt(ztab[:64], lo)
    for ql in range(2):
        for reim in range(2):
            at = (ql * 2 + reim) * 16
            for half in range(2):
                start = (ql * 2 + half) * 8 + x * 2 + reim
                out_ref[pl.ds(start, OWNERS, stride=32), :] = out[at : at + 16, half * 128 : (half + 1) * 128]


def slab_inverse(recv_ref, x, ytab_t, ztab_k, tile_ref):
    parts = []
    for ql in range(2):
        for reim in range(2):
            halves = [
                recv_ref[pl.ds((ql * 2 + half) * 8 + x * 2 + reim, OWNERS, stride=32), :] for half in range(2)
            ]
            parts.append(jnp.concatenate(halves, axis=1))
    hi, lo = split(jnp.concatenate(parts, axis=0))
    h = dot_tn(jnp.concatenate([hi, lo, hi], axis=0), ztab_k[...])
    for p in range(PAIRS):
        pair = h[p * 24 : (p + 1) * 24]
        hi, lo = split(jnp.concatenate([pair[:, :128], pair[:, 128:]], axis=0))
        tile_ref[p * 128 : (p + 1) * 128, :] = dot(ytab_t[...], jnp.concatenate([hi, lo, hi], axis=0))


def forward_kernel(x_ref, ytab, ztab, out_ref, tile_ref):
    x = pl.program_id(0)
    for y in range(NY):
        tile_ref[pl.ds(y, C, stride=NY), :] = x_ref[:, y * 128 : (y + 1) * 128].astype(F32)
    slab_forward(tile_ref, True, x, ytab, ztab, out_ref)


def middle_kernel(
    recv_ref, x_ref, cot_ref, wt_ref, bias_ref, ytab, ztab, ytab_t, ztab_k,
    act_ref, up_ref, out_ref, tile_ref,
):
    x = pl.program_id(0)
    slab_inverse(recv_ref, x, ytab_t, ztab_k, tile_ref)
    wt = wt_ref[...]
    bias = bias_ref[...]

    def step(i, carry):
        base = pl.multiple_of(i * (CHUNK * 128), CHUNK * 128)
        local = dot(wt, x_ref[:, pl.ds(base, CHUNK * 128)])
        for k in range(CHUNK):
            y = i * CHUNK + k
            lanes = pl.ds(pl.multiple_of(base + k * 128, 128), 128)
            pre = tile_ref[pl.ds(y, C, stride=NY), :] + local[:, k * 128 : (k + 1) * 128] + bias
            cdf = 0.5 * (1.0 + lax.erf(pre * (1.0 / math.sqrt(2.0))))
            slope = cdf + pre * jnp.exp(-0.5 * pre * pre) * (1.0 / math.sqrt(2.0 * math.pi))
            act_ref[:, lanes] = (pre * cdf).astype(BF16)
            up = cot_ref[:, lanes].astype(F32) * slope
            up_ref[:, lanes] = up
            tile_ref[pl.ds(y, C, stride=NY), :] = up
        return carry

    lax.fori_loop(0, NY // CHUNK, step, 0)
    slab_forward(tile_ref, False, x, ytab, ztab, out_ref)


def last_kernel(recv_ref, up_ref, w_ref, ytab_t, ztab_k, out_ref, tile_ref):
    x = pl.program_id(0)
    slab_inverse(recv_ref, x, ytab_t, ztab_k, tile_ref)
    w = w_ref[...]

    def step(i, carry):
        base = pl.multiple_of(i * (CHUNK * 128), CHUNK * 128)
        hi, lo = split(up_ref[:, pl.ds(base, CHUNK * 128)])
        local = dot(w, hi) + dot(w, lo)
        for k in range(CHUNK):
            lanes = pl.ds(pl.multiple_of(base + k * 128, 128), 128)
            spectral = tile_ref[pl.ds(i * CHUNK + k, C, stride=NY), :]
            out_ref[:, lanes] = (spectral + local[:, k * 128 : (k + 1) * 128]).astype(BF16)
        return carry

    lax.fori_loop(0, NY // CHUNK, step, 0)


def owner_kernel(adjoint, s_ref, w_ref, dhi, dlo, ihi, ilo, mask_ref, g_ref, gt_ref, out_ref, spec_ref, f_ref, m_ref):
    g = g_ref[...]
    halves = []
    for ql in range(2):
        tiles = [s_ref[:, t * 8 : (t + 1) * 8, :].reshape(128, 128) for t in (2 * ql, 2 * ql + 1)]
        hi, lo = split(jnp.concatenate(tiles, axis=1))
        rep = dot_tn(hi, dhi[ql]) + dot_tn(lo, dhi[ql]) + dot_tn(hi, dlo[ql])
        rep = rep[:KEPT_ROWS].reshape(PAIRS, 24, 512) * mask_ref[ql][None]
        hi, lo = split(rep.reshape(KEPT_ROWS, 512))
        halves.append(dot(g, hi) + dot(g, lo))
    for reim in range(2):
        a = halves[0][:, reim * 256 : (reim + 1) * 256]
        b = halves[1][:, reim * 256 : (reim + 1) * 256]
        f_ref[reim] = jnp.concatenate([a[:, :128], a[:, 128:] + b[:, :128], b[:, 128:]], axis=1)
    for j in range(SAMPLES):
        for reim in range(2):
            spec_ref[j, :, reim * 64 : reim * 64 + BLOCK_MODES] = f_ref[
                reim, :, j * BLOCK_MODES : (j + 1) * BLOCK_MODES
            ]
    m_ref[...] = jnp.zeros_like(m_ref)
    if adjoint:
        fr, fi = f_ref[0, :C, :288], f_ref[1, :C, :288]
        for c in range(C):
            wr, wi = w_ref[c].astype(F32), w_ref[C + c].astype(F32)
            m_ref[0, c : c + 1, :288] = jnp.sum(wr * fr + wi * fi, axis=0, keepdims=True)
            m_ref[1, c : c + 1, :288] = jnp.sum(wr * fi - wi * fr, axis=0, keepdims=True)
    else:
        mr = jnp.zeros((C, 288), F32)
        mi = jnp.zeros((C, 288), F32)
        for c in range(C):
            wr, wi = w_ref[c].astype(F32), w_ref[C + c].astype(F32)
            fr, fi = f_ref[0, c : c + 1, :288], f_ref[1, c : c + 1, :288]
            mr = mr + (wr * fr - wi * fi)
            mi = mi + (wr * fi + wi * fr)
        m_ref[0, :C, :288] = mr
        m_ref[1, :C, :288] = mi
    for ql in range(2):
        lanes = slice(ql * 128, ql * 128 + 256)
        hi, lo = split(jnp.concatenate([m_ref[0, :, lanes], m_ref[1, :, lanes]], axis=1))
        mask = mask_ref[ql][None]
        spread = []
        for part in (hi, lo):
            rows = dot(gt_ref[...], part).reshape(PAIRS, 24, 512) * mask
            rows = jnp.concatenate([rows.reshape(KEPT_ROWS, 512), jnp.zeros((256 - KEPT_ROWS, 512), F32)], axis=0)
            spread.append(rows.astype(BF16))
        hi, lo = spread
        out = dot_nt(ihi[ql], hi) + dot_nt(ihi[ql], lo) + dot_nt(ilo[ql], hi)
        for half in range(2):
            t = 2 * ql + half
            out_ref[:, t * 8 : (t + 1) * 8, :] = out[:, half * 128 : (half + 1) * 128].reshape(OWNERS, 8, 128)


def weight_kernel(a_ref, b_ref, out_ref):
    low = lax.broadcasted_iota(jnp.int32, (CP, 128), 1) < 64
    terms = []
    for s in range(SAMPLES):
        a, b = a_ref[s], b_ref[s]
        turned, b_turned = pltpu.roll(a, 64, 1), pltpu.roll(b, 64, 1)
        terms.append(
            (jnp.where(low, a, turned), jnp.where(low, turned, a), b, jnp.where(low, b_turned, -b_turned))
        )
    for c in range(C):
        total = jnp.zeros((CP, 128), F32)
        for re, im, b, swapped in terms:
            total = total + (re[c : c + 1] * b + im[c : c + 1] * swapped)
        out_ref[0, c] = total[:C, :BLOCK_MODES]
        out_ref[1, c] = total[:C, 64 : 64 + BLOCK_MODES]


def whole(shape):
    return pl.BlockSpec(shape, lambda *_: (0,) * len(shape))


def plane_spec(ndim_lead):
    return pl.BlockSpec((None,) * ndim_lead + (C, CELLS), lambda x: (0,) * (ndim_lead - 1) + (x, 0, 0))


def params():
    return pltpu.CompilerParams(vmem_limit_bytes=VMEM_LIMIT)


def exchange(block):
    return lax.all_to_all(block, "space", split_axis=0, concat_axis=0, tiled=True)


def shards(fields, cotangent, spectral_weight, point_weight, point_bias):
    yhi, ylo = hi_lo(y_table())
    zhi, zlo = hi_lo(plane_table())
    ytab = jnp.asarray(np.concatenate([yhi, ylo], axis=0))
    ztab = jnp.asarray(np.concatenate([zhi, zlo], axis=0))
    ytab_t = jnp.asarray(np.concatenate([yhi.T, yhi.T, ylo.T], axis=1))
    ztab_k = jnp.asarray(np.concatenate([zhi, zhi, zlo], axis=0))
    mask = jnp.asarray(mode_mask())
    g = jnp.asarray(group_table().astype(ml_dtypes.bfloat16))
    gt = jnp.asarray(group_table().T.astype(ml_dtypes.bfloat16))
    flat = (OWNERS * 32, 128)
    slab_out = jax.ShapeDtypeStruct(flat, F32)
    owned_out = jax.ShapeDtypeStruct((OWNERS, 32, 128), F32)
    table_specs = [whole(ytab.shape), whole(ztab.shape)]
    inverse_specs = [whole(ytab_t.shape), whole(ztab_k.shape)]
    tile = pltpu.VMEM((C * NY, 128), F32)

    def owner(received, adjoint):
        scale = 1.0 / VOLUME
        tabs = [x_tables(ql, scale if adjoint else 1.0, 1.0 if adjoint else scale) for ql in range(2)]
        dhi, dlo = hi_lo(np.stack([t[0] for t in tabs]))
        ihi, ilo = hi_lo(np.stack([t[1] for t in tabs]))
        weights = spectral_weight.reshape(2 * C, C, 288)
        return pl.pallas_call(
            functools.partial(owner_kernel, adjoint),
            out_shape=[owned_out, jax.ShapeDtypeStruct((SAMPLES, CP, 128), F32)],
            scratch_shapes=[pltpu.VMEM((2, CP, 384), F32), pltpu.VMEM((2, CP, 384), F32)],
            compiler_params=params(),
            name="owner_up" if adjoint else "owner_in",
        )(received, weights, jnp.asarray(dhi), jnp.asarray(dlo), jnp.asarray(ihi), jnp.asarray(ilo), mask, g, gt)

    sent = pl.pallas_call(
        forward_kernel,
        grid=(SLAB,),
        in_specs=[plane_spec(2)] + table_specs,
        out_specs=whole(flat),
        out_shape=slab_out,
        scratch_shapes=[tile],
        compiler_params=params(),
        name="slab_in",
    )(fields, ytab, ztab)
    mixed, spec_in = owner(exchange(sent.reshape(OWNERS, 32, 128)), False)
    bias = jnp.broadcast_to(point_bias[:, None], (C, 128))
    activated, upstream, sent = pl.pallas_call(
        middle_kernel,
        grid=(SLAB,),
        in_specs=[whole(flat), plane_spec(2), plane_spec(2), whole((C, C)), whole((C, 128))]
        + table_specs
        + inverse_specs,
        out_specs=[plane_spec(2), plane_spec(1), whole(flat)],
        out_shape=[
            jax.ShapeDtypeStruct((1, SLAB, C, CELLS), BF16),
            jax.ShapeDtypeStruct((SLAB, C, CELLS), F32),
            slab_out,
        ],
        scratch_shapes=[tile],
        compiler_params=params(),
        name="slab_mid",
    )(exchange(mixed).reshape(flat), fields, cotangent, point_weight.T, bias, ytab, ztab, ytab_t, ztab_k)
    back, spec_up = owner(exchange(sent.reshape(OWNERS, 32, 128)), True)
    grad_input = pl.pallas_call(
        last_kernel,
        grid=(SLAB,),
        in_specs=[whole(flat), plane_spec(1), whole((C, C))] + inverse_specs,
        out_specs=plane_spec(2),
        out_shape=jax.ShapeDtypeStruct((1, SLAB, C, CELLS), BF16),
        scratch_shapes=[tile],
        compiler_params=params(),
        name="slab_out",
    )(exchange(back).reshape(flat), upstream, point_weight, ytab_t, ztab_k)
    both = jnp.concatenate([spec_in, spec_up], axis=1)
    both = lax.all_to_all(both, "sample", split_axis=0, concat_axis=0, tiled=True)
    grad_spectral = pl.pallas_call(
        weight_kernel,
        out_shape=jax.ShapeDtypeStruct((2, C, C, BLOCK_MODES), F32),
        compiler_params=params(),
        name="weight_grad",
    )(both[:, :CP], both[:, CP:])
    return activated, grad_input, grad_spectral


def solution(mesh):
    return jax.shard_map(
        shards,
        mesh=mesh,
        in_specs=(
            P("sample", "space", None, None),
            P("sample", "space", None, None),
            P(None, None, None, "space"),
            P(),
            P(),
        ),
        out_specs=(
            P("sample", "space", None, None),
            P("sample", "space", None, None),
            P(None, None, None, ("space", "sample")),
        ),
        check_vma=False,
    )
```

time: 265 us -> 109 us (0.41); the launches traced: 261 us -> 108 us
  matrix products: 130 us -> 0 us
  local copies, waits for them, and re-layouts: 70.3 us -> 23.3 us
  Pallas kernels: 0 us -> 30.4 us
  blocking collectives: 0 us -> 25.2 us
  other arithmetic: 12.5 us -> 0.01 us
  starting transfers between devices: 29.1 us -> 17.6 us
  waiting for transfers between devices: 17.4 us -> 10.8 us
    dot_general x46 -> x0, matrix products: 130 us -> none  [the longest x45 118 us: contract(): return jnp.einsum(pattern, left, table, precision=HIGHEST_PRECISION)]
    pallas_call x0 -> x6, Pallas kernels: none -> 30.4 us  [the longest x1 12.5 us: shards(): pl.pallas_call(middle_kernel, grid=(SLAB,), in_specs=[whole(flat), plane_...]
    all_to_all x0 -> x2, blocking collectives: none -> 25.2 us  [the longest x1 14.4 us: shards(): lax.all_to_all(both, 'sample', split_axis=0, concat_axis=0, tiled=True)]
    another operation x28 -> x0, local copies, waits for them, and re-layouts: 15.8 us -> none
    all_to_all x5 -> x3, starting transfers between devices: 29.1 us -> 17.6 us  [exchange(): lax.all_to_all(block, 'space', split_axis=0, concat_axis=0, tiled=True)]
    slice x13 -> x1, local copies, waits for them, and re-layouts: 10.7 us -> 0.01 us  [shards(): both[:, CP:]]
    all_to_all x5 -> x3, waiting for transfers between devices: 17.4 us -> 10.8 us  [exchange(): lax.all_to_all(block, 'space', split_axis=0, concat_axis=0, tiled=True)]
    all_to_all x6 -> x0, local copies, waits for them, and re-layouts: 6 us -> none  [the longest x3 5.3 us: slab_to_owner(): lax.all_to_all(stacked, 'space', split_axis=4, concat_axis=2, tiled=True)]
  transfers between devices with their start and end apart: 5 -> 3, of which waited for: 4 -> 3; matrix products, arithmetic and copies ran while one was open for 7% -> 10% of each run, Pallas kernels for 0% -> 0%
where the time goes in v1:
time: 109 us; the launch traced here: 108 us
  Pallas kernels  30.4 us (28%)
  blocking collectives  25.2 us (23%)
  local copies, waits for them, and re-layouts  23.3 us (21%)
  starting transfers between devices  17.6 us (16%)
  waiting for transfers between devices  10.8 us (10%)
    unnamed x59, local copies, waits for them, and re-layouts  22.6 us
    all_to_all x3, starting transfers between devices, exchange(): lax.all_to_all(block, 'space', split_axis=0, concat_axis=0, tiled=True)  17.6 us
    all_to_all x1, blocking collectives, shards(): lax.all_to_all(both, 'sample', split_axis=0, concat_axis=0, tiled=True)  14.4 us
    pallas_call x1, Pallas kernels, shards(): pl.pallas_call(middle_kernel, grid=(SLAB,), in_specs=[whole(flat), plane_...  12.5 us
    all_to_all x3, waiting for transfers between devices, exchange(): lax.all_to_all(block, 'space', split_axis=0, concat_axis=0, tiled=True)  10.8 us
    all_to_all x1, blocking collectives, exchange(): lax.all_to_all(block, 'space', split_axis=0, concat_axis=0, tiled=True)  10.8 us
    pallas_call x1, Pallas kernels, shards(): pl.pallas_call(last_kernel, grid=(SLAB,), in_specs=[whole(flat), plane_sp...  7.67 us
    pallas_call x2, Pallas kernels, owner(): pl.pallas_call(functools.partial(owner_kernel, adjoint), out_shape=[owned...  5.9 us
  transfers between devices with their start and end apart: 3, of which 3 were waited for; matrix products, arithmetic and copies ran while one was open for 10% of the time, Pallas kernels for 0%

profile of v1, /device:TPU:1, one launch (start us, length us, event | category | flops | bytes accessed | tf_op | source)
XLA Modules:
  0.0 108.2 jit_solution(11001926404950742385)
XLA Ops:
  0.6 0.0 copy-start.17
  0.7 2.1 %copy.23.x_ref = bf16[1,4,20,8192]{3,2,1,0:T(8,128)(2,1)S(1)} copy(bf16[1,4,20,8192]{3,1,2,0:T(4,128)(2,1)} %param.20) | data formatting | bytes 2621440 | tf_op args[0]
  2.8 3.9 %slab_in.1 = f32[512,128]{1,0:T(8,128)} custom-call(bf16[1,4,20,8192]{3,2,1,0:T(8,128)(2,1)S(1)} %copy.23.x_ref, bf16[96,128]{1,0:T(8,128)(2,1)S(1)} %copy-done.17, bf16[128,256]{1,0:T(8,128)(2,1)S(1)} %copy-done.12), custom_call_target="tpu_custom_call" | custom-call | tf_op jit(solution)/shard_map/slab_in/pallas_call | solution.py:324
  6.8 6.9 %all-to-all-start = ((f32[16,32,128]{2,1,0:T(8,128)}), f32[16,32,128]{2,1,0:T(8,128)}, u32[]{:S(2)}, u32[]{:S(2)}) async-start(f32[16,32,128]{2,1,0:T(8,128)} %bitcast), calls=%async_computation | async-start | bytes 524288 | tf_op jit(solution)/shard_map/all_to_all | solution.py:290
  13.7 1.2 %copy.24 = bf16[2,20,20,288]{3,2,1,0:T(8,128)(2,1)S(1)} copy(bf16[2,20,20,288]{3,0,2,1:T(2,128)(2,1)} %param.22) | data formatting | bytes 921600 | tf_op args[2]
  14.9 6.1 %all-to-all-done.s_ref = f32[16,32,128]{2,1,0:T(8,128)} async-done(((f32[16,32,128]{2,1,0:T(8,128)}), f32[16,32,128]{2,1,0:T(8,128)}, u32[]{:S(2)}, u32[]{:S(2)}) %all-to-all-start) | async-done | bytes 262176 | tf_op jit(solution)/shard_map/all_to_all | solution.py:290
  21.0 3.1 %owner_in.1 = (f32[16,32,128]{2,1,0:T(8,128)S(1)}, f32[8,24,128]{2,1,0:T(8,128)S(1)}) custom-call(f32[16,32,128]{2,1,0:T(8,128)} %all-to-all-done.s_ref, bf16[40,20,288]{2,1,0:T(8,128)(2,1)S(1)} %bitcast.6, bf16[2,128,512]{2,1,0:T(8,128)(2,1)S(1)} %copy-done.7, bf16[2,128,512]{2,1,0:T(8,128)(2,1)S(1)} %copy-done.6, bf16[2,128,512]{2,1,0:T(8,128)(2,1)S(1)} %copy-done.5, ...), custom_call_target="tpu_custom_call" | custom-call | tf_op jit(solution)/shard_map/owner_in/pallas_call | solution.py:316
  24.1 0.7 copy-done.14
  24.8 0.6 copy-done.19
  25.4 4.9 %all-to-all-start.1 = ((f32[16,32,128]{2,1,0:T(8,128)}), f32[16,32,128]{2,1,0:T(8,128)}, u32[]{:S(2)}, u32[]{:S(2)}) async-start(f32[16,32,128]{2,1,0:T(8,128)} %copy-done.14), calls=%async_computation.1 | async-start | bytes 524288 | tf_op jit(solution)/shard_map/all_to_all | solution.py:290
  30.3 1.4 %copy.25 = bf16[20,20]{0,1:T(8,128)(2,1)} copy(bf16[20,20]{1,0:T(8,128)(2,1)} %w_ref.1) | data formatting | bytes 1600 | tf_op args[3]
  31.7 3.2 %copy.27.cot_ref = bf16[1,4,20,8192]{3,2,1,0:T(8,128)(2,1)} copy(bf16[1,4,20,8192]{3,1,2,0:T(4,128)(2,1)} %param.21) | data formatting | bytes 2621440 | tf_op args[1]
  35.0 2.7 %all-to-all-done.1 = f32[16,32,128]{2,1,0:T(8,128)} async-done(((f32[16,32,128]{2,1,0:T(8,128)}), f32[16,32,128]{2,1,0:T(8,128)}, u32[]{:S(2)}, u32[]{:S(2)}) %all-to-all-start.1) | async-done | bytes 262176 | tf_op jit(solution)/shard_map/all_to_all | solution.py:290
  37.7 0.7 broadcast_in_dim.2.bias_ref
  38.4 1.4 %copy-done = bf16[1,4,20,8192]{3,2,1,0:T(8,128)(2,1)S(1)} copy-done((bf16[1,4,20,8192]{3,2,1,0:T(8,128)(2,1)S(1)}, bf16[1,4,20,8192]{3,2,1,0:T(8,128)(2,1)}, u32[]{:S(2)}) %copy-start) | copy-done | bytes 1310744
  39.8 0.8 copy-done.10
  40.6 0.8 copy-done.13
  41.5 0.7 copy-done.18
  42.2 0.7 copy-done.23
  42.9 12.5 %slab_mid.1 = (bf16[1,4,20,8192]{3,2,1,0:T(8,128)(2,1)S(1)}, f32[4,20,8192]{2,1,0:T(8,128)S(1)}, f32[512,128]{1,0:T(8,128)S(1)}) custom-call(f32[512,128]{1,0:T(8,128)} %bitcast.2.recv_ref, bf16[1,4,20,8192]{3,2,1,0:T(8,128)(2,1)S(1)} %copy.23.x_ref, bf16[1,4,20,8192]{3,2,1,0:T(8,128)(2,1)S(1)} %copy-done, bf16[20,20]{1,0:T(8,128)(2,1)S(1)} %bitcast.10, ...), custom_call_target="tpu_custom_call" | custom-call | tf_op jit(solution)/shard_map/slab_mid/pallas_call | solution.py:336
  55.4 1.1 %copy-done.3 = bf16[1,4,20,8192]{3,2,1,0:T(8,128)(2,1)} copy-done((bf16[1,4,20,8192]{3,2,1,0:T(8,128)(2,1)}, bf16[1,4,20,8192]{3,2,1,0:T(8,128)(2,1)S(1)}, u32[]{:S(2)}) %copy-start.3) | copy-done | bytes 1310744
  56.5 10.8 %all_to_all.25.s_ref = f32[16,32,128]{2,1,0:T(8,128)S(1)} all-to-all(f32[16,32,128]{2,1,0:T(8,128)S(1)} %bitcast.9), channel_id=1, replica_groups=mesh['space'=16,'sample'=8] {'space'}, dimensions={0} | all-to-all | bytes 524288 | tf_op jit(solution)/shard_map/all_to_all | solution.py:290
  67.3 2.8 %owner_up.1 = (f32[16,32,128]{2,1,0:T(8,128)}, f32[8,24,128]{2,1,0:T(8,128)S(1)}) custom-call(f32[16,32,128]{2,1,0:T(8,128)S(1)} %all_to_all.25.s_ref, bf16[40,20,288]{2,1,0:T(8,128)(2,1)S(1)} %bitcast.7, bf16[2,128,512]{2,1,0:T(8,128)(2,1)S(1)} %copy-done.5, bf16[2,128,512]{2,1,0:T(8,128)(2,1)S(1)} %copy-done.4, bf16[2,128,512]{2,1,0:T(8,128)(2,1)S(1)} %copy-done.7, ...), custom_call_target="tpu_custom_call" | custom-call | tf_op jit(solution)/shard_map/owner_up/pallas_call | solution.py:316
  70.1 14.4 %all_to_all.26 = f32[8,48,128]{2,1,0:T(8,128)} all-to-all(f32[8,48,128]{2,1,0:T(8,128)S(1)} %pad_maximum_fusion), channel_id=1, replica_groups=mesh['space'=16,'sample'=8] {'sample'}, dimensions={0} | all-to-all | bytes 393216 | tf_op jit(solution)/shard_map/all_to_all | solution.py:364
  84.6 5.8 %all-to-all-start.3 = ((f32[16,32,128]{2,1,0:T(8,128)}), f32[16,32,128]{2,1,0:T(8,128)S(1)}, u32[]{:S(2)}, u32[]{:S(2)}) async-start(f32[16,32,128]{2,1,0:T(8,128)} %get-tuple-element.13), calls=%async_computation.3 | async-start | bytes 524288 | tf_op jit(solution)/shard_map/all_to_all | solution.py:290
  90.3 3.6 %copy.28 = bf16[1,4,20,8192]{3,1,2,0:T(4,128)(2,1)} copy(bf16[1,4,20,8192]{3,2,1,0:T(8,128)(2,1)} %copy-done.3) | data formatting | bytes 2621440
  94.0 0.5 weight_grad.1
  94.5 1.1 copy.30
  95.5 2.0 %all-to-all-done.3 = f32[16,32,128]{2,1,0:T(8,128)S(1)} async-done(((f32[16,32,128]{2,1,0:T(8,128)}), f32[16,32,128]{2,1,0:T(8,128)S(1)}, u32[]{:S(2)}, u32[]{:S(2)}) %all-to-all-start.3) | async-done | bytes 262176 | tf_op jit(solution)/shard_map/all_to_all | solution.py:290
  97.6 0.8 copy-done.11
  98.4 7.7 %slab_out.1 = bf16[1,4,20,8192]{3,2,1,0:T(8,128)(2,1)S(1)} custom-call(f32[512,128]{1,0:T(8,128)S(1)} %bitcast.8, f32[4,20,8192]{2,1,0:T(8,128)S(1)} %copy-done.2, bf16[20,20]{1,0:T(8,128)(2,1)S(1)} %copy-done.24, bf16[128,144]{1,0:T(8,128)(2,1)S(1)} %copy-done.11, bf16[192,256]{1,0:T(8,128)(2,1)S(1)} %copy-done.9), custom_call_target="tpu_custom_call" | custom-call | tf_op jit(solution)/shard_map/slab_out/pallas_call | solution.py:353
  106.1 2.1 %copy.29 = bf16[1,4,20,8192]{3,1,2,0:T(4,128)(2,1)} copy(bf16[1,4,20,8192]{3,2,1,0:T(8,128)(2,1)S(1)} %slab_out.1) | data formatting | bytes 2621440
  (44 shorter events, 0.1 us)
Async XLA Ops:
  0.6 2.1 %copy-start.12 = (bf16[128,256]{1,0:T(8,128)(2,1)S(1)}, bf16[128,256]{1,0:T(8,128)(2,1)}, u32[]{:S(2)}) copy-start(bf16[128,256]{1,0:T(8,128)(2,1)} %constant.23.clone.ztab) | copy-start | bytes 196612
  0.6 2.1 %copy-start.17 = (bf16[96,128]{1,0:T(8,128)(2,1)S(1)}, bf16[96,128]{1,0:T(8,128)(2,1)}, u32[]{:S(2)}) copy-start(bf16[96,128]{1,0:T(8,128)(2,1)} %constant.22.clone.ytab) | copy-start | bytes 73732
  2.8 18.2 %copy-start.4 = (bf16[2,128,512]{2,1,0:T(8,128)(2,1)S(1)}, bf16[2,128,512]{2,1,0:T(8,128)(2,1)}, u32[]{:S(2)}) copy-start(bf16[2,128,512]{2,1,0:T(8,128)(2,1)} %constant.32.clone.ilo.dlo) | copy-start | bytes 786436
  2.8 18.2 %copy-start.5 = (bf16[2,128,512]{2,1,0:T(8,128)(2,1)S(1)}, bf16[2,128,512]{2,1,0:T(8,128)(2,1)}, u32[]{:S(2)}) copy-start(bf16[2,128,512]{2,1,0:T(8,128)(2,1)} %constant.31.clone.ihi.dhi) | copy-start | bytes 786436
  2.8 18.2 %copy-start.6 = (bf16[2,128,512]{2,1,0:T(8,128)(2,1)S(1)}, bf16[2,128,512]{2,1,0:T(8,128)(2,1)}, u32[]{:S(2)}) copy-start(bf16[2,128,512]{2,1,0:T(8,128)(2,1)} %constant.30.clone.dlo.ilo) | copy-start | bytes 786436
  2.8 18.2 %copy-start.7 = (bf16[2,128,512]{2,1,0:T(8,128)(2,1)S(1)}, bf16[2,128,512]{2,1,0:T(8,128)(2,1)}, u32[]{:S(2)}) copy-start(bf16[2,128,512]{2,1,0:T(8,128)(2,1)} %constant.29.clone.dhi.ihi) | copy-start | bytes 786436
  2.8 18.2 %copy-start.8 = (f32[2,24,512]{2,1,0:T(8,128)S(1)}, f32[2,24,512]{2,1,0:T(8,128)}, u32[]{:S(2)}) copy-start(f32[2,24,512]{2,1,0:T(8,128)} %constant.26.clone.mask_ref) | copy-start | bytes 294916
  2.8 18.2 %copy-start.15 = (bf16[240,24]{1,0:T(8,128)(2,1)S(1)}, bf16[240,24]{1,0:T(8,128)(2,1)}, u32[]{:S(2)}) copy-start(bf16[240,24]{1,0:T(8,128)(2,1)} %constant.28.clone.gt_ref) | copy-start | bytes 34564
  2.8 18.2 %copy-start.21 = (bf16[24,240]{1,0:T(8,128)(2,1)S(1)}, bf16[24,240]{1,0:T(8,128)(2,1)}, u32[]{:S(2)}) copy-start(bf16[24,240]{1,0:T(8,128)(2,1)} %constant.27.clone.g_ref) | copy-start | bytes 34564
  6.8 14.2 %all-to-all-start = ((f32[16,32,128]{2,1,0:T(8,128)}), f32[16,32,128]{2,1,0:T(8,128)}, u32[]{:S(2)}, u32[]{:S(2)}) async-start(f32[16,32,128]{2,1,0:T(8,128)} %bitcast), calls=%async_computation | async-start | bytes 524288 | tf_op jit(solution)/shard_map/all_to_all | solution.py:290
  24.1 0.7 copy-start.14
  24.8 0.6 copy-start.19
  25.4 12.2 %all-to-all-start.1 = ((f32[16,32,128]{2,1,0:T(8,128)}), f32[16,32,128]{2,1,0:T(8,128)}, u32[]{:S(2)}, u32[]{:S(2)}) async-start(f32[16,32,128]{2,1,0:T(8,128)} %copy-done.14), calls=%async_computation.1 | async-start | bytes 524288 | tf_op jit(solution)/shard_map/all_to_all | solution.py:290
  30.3 8.1 %copy-start.9 = (bf16[192,256]{1,0:T(8,128)(2,1)S(1)}, bf16[192,256]{1,0:T(8,128)(2,1)}, u32[]{:S(2)}) copy-start(bf16[192,256]{1,0:T(8,128)(2,1)} %constant.25.clone.ztab_k) | copy-start | bytes 294916
  38.4 1.4 %copy-start = (bf16[1,4,20,8192]{3,2,1,0:T(8,128)(2,1)S(1)}, bf16[1,4,20,8192]{3,2,1,0:T(8,128)(2,1)}, u32[]{:S(2)}) copy-start(bf16[1,4,20,8192]{3,2,1,0:T(8,128)(2,1)} %copy.27.cot_ref) | copy-start | bytes 3932164
  39.8 0.8 copy-start.10
  40.6 0.8 copy-start.13
  41.5 0.7 copy-start.18
  42.2 0.7 copy-start.23
  42.9 24.4 %copy-start.16 = (bf16[240,24]{1,0:T(8,128)(2,1)S(1)}, bf16[240,24]{1,0:T(8,128)(2,1)}, u32[]{:S(2)}) copy-start(bf16[240,24]{1,0:T(8,128)(2,1)} %constant.28.clone.gt_ref) | copy-start | bytes 34564
  42.9 24.4 %copy-start.22 = (bf16[24,240]{1,0:T(8,128)(2,1)S(1)}, bf16[24,240]{1,0:T(8,128)(2,1)}, u32[]{:S(2)}) copy-start(bf16[24,240]{1,0:T(8,128)(2,1)} %constant.27.clone.g_ref) | copy-start | bytes 34564
  55.4 1.2 %copy-start.3 = (bf16[1,4,20,8192]{3,2,1,0:T(8,128)(2,1)}, bf16[1,4,20,8192]{3,2,1,0:T(8,128)(2,1)S(1)}, u32[]{:S(2)}) copy-start(bf16[1,4,20,8192]{3,2,1,0:T(8,128)(2,1)S(1)} %get-tuple-element.17) | copy-start | bytes 3932164
  56.5 28.0 %copy-start.1 = (f32[4,20,8192]{2,1,0:T(8,128)}, f32[4,20,8192]{2,1,0:T(8,128)S(1)}, u32[]{:S(2)}) copy-start(f32[4,20,8192]{2,1,0:T(8,128)S(1)} %get-tuple-element.14.up_ref) | copy-start | bytes 7864324
  56.5 13.6 %copy-start.20 = (f32[8,24,128]{2,1,0:T(8,128)S(1)}, f32[8,24,128]{2,1,0:T(8,128)}, u32[]{:S(2)}) copy-start(f32[8,24,128]{2,1,0:T(8,128)} %copy-done.19) | copy-start | bytes 294916
  84.6 13.0 %all-to-all-start.3 = ((f32[16,32,128]{2,1,0:T(8,128)}), f32[16,32,128]{2,1,0:T(8,128)S(1)}, u32[]{:S(2)}, u32[]{:S(2)}) async-start(f32[16,32,128]{2,1,0:T(8,128)} %get-tuple-element.13), calls=%async_computation.3 | async-start | bytes 524288 | tf_op jit(solution)/shard_map/all_to_all | solution.py:290
  90.3 3.6 %copy-start.25 = (f32[8,48,128]{2,1,0:T(8,128)S(1)}, f32[8,48,128]{2,1,0:T(8,128)}, u32[]{:S(2)}) copy-start(f32[8,48,128]{2,1,0:T(8,128)} %all_to_all.26) | copy-start | bytes 589828
  90.3 7.2 %copy-start.2 = (f32[4,20,8192]{2,1,0:T(8,128)S(1)}, f32[4,20,8192]{2,1,0:T(8,128)}, u32[]{:S(2)}) copy-start(f32[4,20,8192]{2,1,0:T(8,128)} %copy-done.1) | copy-start | bytes 7864324
  94.0 3.6 %copy-start.24 = (bf16[20,20]{1,0:T(8,128)(2,1)S(1)}, bf16[20,20]{1,0:T(8,128)(2,1)}, u32[]{:S(2)}) copy-start(bf16[20,20]{1,0:T(8,128)(2,1)} %w_ref.1) | copy-start | bytes 2404
  97.6 0.8 copy-start.11

commit v2 on v1

v2 whole, which is shorter than its diff:
```python
import functools
import math

import jax
import jax.numpy as jnp
import ml_dtypes
import numpy as np
from jax import lax
from jax.experimental import pallas as pl
from jax.experimental.pallas import tpu as pltpu
from jax.sharding import PartitionSpec as P

NX, NY, NZ, NT = 64, 64, 32, 4
MX, MY, MZ, MT = 12, 12, 8, 4
C = 20
CP = 24
PLANE = NZ * NT
CELLS = NY * PLANE
KEPT_ROWS = C * MY
SLAB = 4
OWNERS = 16
SAMPLES = 8
BLOCK_MODES = 36
PAIRS = C // 2
CHUNK = 64
STEPS = C // 4
ROWS = C * SLAB * NY
PAIR_ROWS = 2 * SLAB * NY
QUAD_ROWS = 2 * PAIR_ROWS
QUARTER = 2 * SLAB * 24
MIX = 16
VOLUME = NX * NY * NZ * NT
F32, BF16 = jnp.float32, jnp.bfloat16
MIB = 1024 * 1024


def signed(index, modes):
    return np.where(index < modes // 2, index, index - modes)


def hi_lo(table):
    hi = table.astype(np.float32).astype(ml_dtypes.bfloat16)
    lo = (table - hi.astype(np.float64)).astype(np.float32).astype(ml_dtypes.bfloat16)
    return hi, lo


def y_table():
    k = signed(np.arange(MY), MY)[:, None]
    theta = 2 * np.pi * ((k * np.arange(NY)[None, :]) % NY) / NY
    eye2, eye4 = np.eye(2), np.eye(SLAB)
    parts = [np.einsum("ab,pq,ky->apkqyb", eye4, eye2, t) for t in (np.cos(theta), -np.sin(theta))]
    return np.stack(parts).reshape(QUARTER, PAIR_ROWS)


def plane_table():
    z = np.arange(PLANE) // NT
    t = np.arange(PLANE) % NT
    rows = []
    for ql in range(2):
        q = 2 * np.arange(OWNERS) + ql
        fz = signed(q // MT, MZ)[:, None]
        ft = signed(q % MT, MT)[:, None]
        phase = (fz * z * NT + ft * t * NZ) % PLANE
        theta = 2 * np.pi * phase / PLANE
        rows.append(np.concatenate([np.cos(theta), np.sin(theta)], axis=1))
        rows.append(np.concatenate([-np.sin(theta), np.cos(theta)], axis=1))
    return np.concatenate(rows, axis=0)


def x_tables(ql, forward_scale, inverse_scale):
    lane = np.arange(256) + 128 * ql
    f = signed(lane % MX, MX)[None, :]
    theta = 2 * np.pi * ((f * np.arange(NX)[:, None]) % NX) / NX
    cos, sin = np.cos(theta), np.sin(theta)
    forward = np.zeros((NX, 2, 512))
    forward[:, 0] = np.concatenate([cos, -sin], axis=1)
    forward[:, 1] = np.concatenate([sin, cos], axis=1)
    inverse = np.zeros((NX, 2, 512))
    inverse[:, 0] = np.concatenate([cos, -sin], axis=1)
    inverse[:, 1] = np.concatenate([sin, cos], axis=1)
    return forward.reshape(128, 512) * forward_scale, inverse.reshape(128, 512) * inverse_scale


def mode_mask():
    mask = np.zeros((2, 24, 512), np.float32)
    for ql in range(2):
        lane = np.arange(256) + 128 * ql
        code = np.where(lane < 288, lane // MX, -1)
        hit = code[None, :] == (ql * MY + np.arange(24)[:, None] % MY)
        mask[ql] = np.concatenate([hit, hit], axis=1)
    return mask


def group_table():
    g = np.zeros((CP, KEPT_ROWS), np.float32)
    for c in range(C):
        g[c, c * MY : (c + 1) * MY] = 1.0
    return g


def split(value):
    hi = value.astype(BF16)
    return hi, (value - hi.astype(F32)).astype(BF16)


def dot(a, b):
    return lax.dot_general(a, b, (((1,), (0,)), ((), ())), preferred_element_type=F32)


def dot_tn(a, b):
    return lax.dot_general(a, b, (((0,), (0,)), ((), ())), preferred_element_type=F32)


def dot_nt(a, b):
    return lax.dot_general(a, b, (((1,), (1,)), ((), ())), preferred_element_type=F32)


def forward_y(quad, left, right, ytab, u_ref):
    u = dot(ytab[...], jnp.concatenate([left[0], right[0]], axis=1))
    u = u[:QUARTER] + u[QUARTER:]
    if len(left) > 1:
        u = u + dot(ytab[:QUARTER], jnp.concatenate([left[1], right[1]], axis=1))
    for side in range(2):
        rows = slice(quad * 48 + side * 24, quad * 48 + side * 24 + 24)
        for reim in range(2):
            for x in range(SLAB):
                at = (reim * SLAB + x) * 24
                u_ref[x, rows, reim * 128 : (reim + 1) * 128] = u[at : at + 24, side * 128 : (side + 1) * 128]


def forward_plane(u_ref, ztab, out_ref):
    for x in range(SLAB):
        u_ref[x, KEPT_ROWS:, :] = jnp.zeros((256 - KEPT_ROWS, 256), F32)
        hi, lo = split(u_ref[x])
        both = dot_nt(ztab[...], hi)
        out = both[:64] + both[64:] + dot_nt(ztab[:64], lo)
        for ql in range(2):
            for reim in range(2):
                at = (ql * 2 + reim) * 16
                for half in range(2):
                    start = (ql * 2 + half) * 8 + x * 2 + reim
                    out_ref[pl.ds(start, OWNERS, stride=32), :] = out[at : at + 16, half * 128 : (half + 1) * 128]


def inverse_plane(recv_ref, ztab_k, h_ref):
    for x in range(SLAB):
        parts = []
        for ql in range(2):
            for reim in range(2):
                halves = [
                    recv_ref[pl.ds((ql * 2 + half) * 8 + x * 2 + reim, OWNERS, stride=32), :] for half in range(2)
                ]
                parts.append(jnp.concatenate(halves, axis=1))
        hi, lo = split(jnp.concatenate(parts, axis=0))
        h_ref[x] = dot_tn(jnp.concatenate([hi, lo, hi], axis=0), ztab_k[...])


def inverse_y(quad, h_ref, ytab_t):
    pieces = []
    for reim in range(2):
        for x in range(SLAB):
            sides = [
                h_ref[x, quad * 48 + side * 24 : quad * 48 + side * 24 + 24, reim * 128 : (reim + 1) * 128]
                for side in range(2)
            ]
            pieces.append(jnp.concatenate(sides, axis=1))
    hi, lo = split(jnp.concatenate(pieces, axis=0))
    return dot(ytab_t[...], jnp.concatenate([hi, lo, hi], axis=0))


def quad_rows(quad):
    return pl.ds(quad * QUAD_ROWS, QUAD_ROWS)


def fetch(source, target, sems, first):
    copies = [
        pltpu.make_async_copy(source.at[quad_rows(q)], target.at[quad_rows(q)], sems.at[first + q])
        for q in range(STEPS)
    ]
    for copy in copies:
        copy.start()
    return copies


def forward_kernel(x_hbm, ytab_hbm, ztab_hbm, out_ref, x_ref, ytab, ztab, u_ref, sems):
    tables = [
        pltpu.make_async_copy(ytab_hbm, ytab, sems.at[STEPS]),
        pltpu.make_async_copy(ztab_hbm, ztab, sems.at[STEPS + 1]),
    ]
    tables[0].start()
    copies = fetch(x_hbm, x_ref, sems, 0)
    tables[1].start()
    tables[0].wait()
    for quad in range(STEPS):
        copies[quad].wait()
        at = quad * QUAD_ROWS
        left, right = x_ref[at : at + PAIR_ROWS, :], x_ref[at + PAIR_ROWS : at + QUAD_ROWS, :]
        forward_y(quad, [left], [right], ytab, u_ref)
    tables[1].wait()
    forward_plane(u_ref, ztab, out_ref)


def middle_kernel(
    recv_ref, local_hbm, cot_hbm, ytab, ztab, ytab_t, ztab_k,
    act_hbm, up_hbm, out_ref,
    local_ref, cot_ref, act_ref, up_ref, h_ref, u_ref, pre_ref, hi_ref, lo_ref, sems,
):
    local_copies = fetch(local_hbm, local_ref, sems, 0)
    cot_copies = fetch(cot_hbm, cot_ref, sems, STEPS)
    stores = []
    inverse_plane(recv_ref, ztab_k, h_ref)
    for quad in range(STEPS):
        pre_ref[...] = inverse_y(quad, h_ref, ytab_t)
        local_copies[quad].wait()
        cot_copies[quad].wait()
        for side in range(2):
            lanes = slice(side * 128, (side + 1) * 128)
            for i in range(PAIR_ROWS // CHUNK):
                near = slice(i * CHUNK, (i + 1) * CHUNK)
                at = quad * QUAD_ROWS + side * PAIR_ROWS + i * CHUNK
                rows = slice(at, at + CHUNK)
                pre = pre_ref[near, lanes] + local_ref[rows, :]
                cdf = 0.5 * (1.0 + lax.erf(pre * (1.0 / math.sqrt(2.0))))
                slope = cdf + pre * jnp.exp(-0.5 * pre * pre) * (1.0 / math.sqrt(2.0 * math.pi))
                act_ref[rows, :] = (pre * cdf).astype(BF16)
                up = cot_ref[rows, :].astype(F32) * slope
                up_ref[rows, :] = up
                hi_ref[near, lanes], lo_ref[near, lanes] = split(up)
        for k, (source, target) in enumerate(((act_ref, act_hbm), (up_ref, up_hbm))):
            store = pltpu.make_async_copy(
                source.at[quad_rows(quad)], target.at[quad_rows(quad)], sems.at[(2 + k) * STEPS + quad]
            )
            store.start()
            stores.append(store)
        sides = [[ref[:, side * 128 : (side + 1) * 128] for ref in (hi_ref, lo_ref)] for side in range(2)]
        forward_y(quad, sides[0], sides[1], ytab, u_ref)
    forward_plane(u_ref, ztab, out_ref)
    for store in stores:
        store.wait()


def last_kernel(recv_ref, local_hbm, ytab_t, ztab_k, out_hbm, token_ref, local_ref, out_ref, h_ref, sems):
    token_ref[...] = jnp.zeros_like(token_ref)
    local_copies = fetch(local_hbm, local_ref, sems, 0)
    stores = []
    inverse_plane(recv_ref, ztab_k, h_ref)
    for quad in range(STEPS):
        spectral = inverse_y(quad, h_ref, ytab_t)
        local_copies[quad].wait()
        for side in range(2):
            at = quad * QUAD_ROWS + side * PAIR_ROWS
            rows = slice(at, at + PAIR_ROWS)
            out_ref[rows, :] = (spectral[:, side * 128 : (side + 1) * 128] + local_ref[rows, :]).astype(BF16)
        store = pltpu.make_async_copy(
            out_ref.at[quad_rows(quad)], out_hbm.at[quad_rows(quad)], sems.at[STEPS + quad]
        )
        store.start()
        stores.append(store)
    for store in stores:
        store.wait()


def point_kernel(transposed, x_ref, w_ref, *rest):
    bias_ref, out_ref, token_ref = rest if len(rest) == 3 else (None, *rest)
    token_ref[...] = jnp.zeros_like(token_ref)
    size = C * MIX
    row = lax.broadcasted_iota(jnp.int32, (size, C), 0)
    spread = (row // MIX == lax.broadcasted_iota(jnp.int32, (size, C), 1)).astype(F32)
    offset = jnp.sum(spread * bias_ref[...], axis=1, keepdims=True) if bias_ref is not None else 0.0
    spread = spread.astype(BF16)
    wide = (dot_nt if transposed else dot)(spread, w_ref[...]).astype(BF16)
    wide = dot_nt(wide, spread)
    row = lax.broadcasted_iota(jnp.int32, (size, size), 0)
    column = lax.broadcasted_iota(jnp.int32, (size, size), 1)
    wide = jnp.where(row % MIX == column % MIX, wide, 0.0).astype(BF16)
    for block in range(SLAB * NY // (2 * MIX)):
        sides = []
        for side in range(2):
            at = (2 * block + side) * MIX
            sides.append(
                jnp.concatenate([x_ref[c * SLAB * NY + at : c * SLAB * NY + at + MIX, :] for c in range(C)], axis=0)
            )
        both = jnp.concatenate(sides, axis=1)
        if both.dtype == BF16:
            out = dot(wide, both)
        else:
            hi, lo = split(both)
            out = dot(wide, hi) + dot(wide, lo)
        out = out + offset
        for side in range(2):
            at = (2 * block + side) * MIX
            for c in range(C):
                out_ref[c * SLAB * NY + at : c * SLAB * NY + at + MIX, :] = out[
                    c * MIX : (c + 1) * MIX, side * 128 : (side + 1) * 128
                ]


def owner_kernel(adjoint, s_ref, w_ref, dhi, dlo, ihi, ilo, mask_ref, g_ref, gt_ref, *rest):
    if adjoint:
        first_ref, _, out_ref, *send_refs = rest[:8]
        f_ref, m_ref, turn_ref, b_ref = rest[8:]
        send_refs = send_refs[:4] + [send_refs[4].at[k] for k in range(4)]
    else:
        out_ref, spec_hbm, f_ref, m_ref, turn_ref, spec_ref, sem = rest
        store = pltpu.make_async_copy(spec_ref, spec_hbm, sem)
    g = g_ref[...]
    halves = []
    for ql in range(2):
        tiles = [s_ref[:, t * 8 : (t + 1) * 8, :].reshape(128, 128) for t in (2 * ql, 2 * ql + 1)]
        hi, lo = split(jnp.concatenate(tiles, axis=1))
        rep = dot_tn(hi, dhi[ql]) + dot_tn(lo, dhi[ql]) + dot_tn(hi, dlo[ql])
        rep = rep[:KEPT_ROWS].reshape(PAIRS, 24, 512) * mask_ref[ql][None]
        hi, lo = split(rep.reshape(KEPT_ROWS, 512))
        halves.append(dot(g, hi) + dot(g, lo))
    for reim in range(2):
        a = halves[0][:, reim * 256 : (reim + 1) * 256]
        b = halves[1][:, reim * 256 : (reim + 1) * 256]
        f_ref[reim] = jnp.concatenate([a[:, :128], a[:, 128:] + b[:, :128], b[:, 128:]], axis=1)
    for reim in range(2):
        for t in range(3):
            turn_ref[t, pl.ds(reim, CP, stride=2), :] = f_ref[reim, :, t * 128 : (t + 1) * 128]
    turned = jnp.concatenate([turn_ref[t, : 2 * C, :] for t in range(3)], axis=1)
    for j in range(SAMPLES):
        block = turned[:, j * BLOCK_MODES : (j + 1) * BLOCK_MODES]
        if adjoint:
            b_ref[j, :, 64 : 64 + BLOCK_MODES] = block
            b_ref[j, :, :BLOCK_MODES] = first_ref[j, :, :BLOCK_MODES]
        else:
            spec_ref[j, :, :BLOCK_MODES] = block
    if adjoint:
        me = lax.axis_index("sample")
        for d in range(SAMPLES):
            send_refs[d][...] = b_ref[jnp.bitwise_xor(me, d)]
    else:
        store.start()
    m_ref[...] = jnp.zeros_like(m_ref)
    if adjoint:
        fr, fi = f_ref[0, :C, :288], f_ref[1, :C, :288]
        for c in range(C):
            wr, wi = w_ref[c].astype(F32), w_ref[C + c].astype(F32)
            m_ref[0, c : c + 1, :288] = jnp.sum(wr * fr + wi * fi, axis=0, keepdims=True)
            m_ref[1, c : c + 1, :288] = jnp.sum(wr * fi - wi * fr, axis=0, keepdims=True)
    else:
        mr = jnp.zeros((C, 288), F32)
        mi = jnp.zeros((C, 288), F32)
        for c in range(C):
            wr, wi = w_ref[c].astype(F32), w_ref[C + c].astype(F32)
            fr, fi = f_ref[0, c : c + 1, :288], f_ref[1, c : c + 1, :288]
            mr = mr + (wr * fr - wi * fi)
            mi = mi + (wr * fi + wi * fr)
        m_ref[0, :C, :288] = mr
        m_ref[1, :C, :288] = mi
    for ql in range(2):
        lanes = slice(ql * 128, ql * 128 + 256)
        hi, lo = split(jnp.concatenate([m_ref[0, :, lanes], m_ref[1, :, lanes]], axis=1))
        mask = mask_ref[ql][None]
        spread = []
        for part in (hi, lo):
            rows = dot(gt_ref[...], part).reshape(PAIRS, 24, 512) * mask
            rows = jnp.concatenate([rows.reshape(KEPT_ROWS, 512), jnp.zeros((256 - KEPT_ROWS, 512), F32)], axis=0)
            spread.append(rows.astype(BF16))
        hi, lo = spread
        out = dot_nt(ihi[ql], hi) + dot_nt(ihi[ql], lo) + dot_nt(ilo[ql], hi)
        for half in range(2):
            t = 2 * ql + half
            out_ref[:, t * 8 : (t + 1) * 8, :] = out[:, half * 128 : (half + 1) * 128].reshape(OWNERS, 8, 128)
    if not adjoint:
        store.wait()


def weight_kernel(*refs):
    own_ref, far_ref, near_refs, (out_ref, a_ref) = refs[0], refs[1], refs[2:5], refs[6:]
    even = lax.broadcasted_iota(jnp.int32, (2 * C, 128), 0) % 2 == 0
    terms = []
    for s, ref in enumerate([own_ref, far_ref.at[0]] + [ref.at[k] for ref in near_refs for k in range(2)]):
        block = ref[...]
        a_ref[s] = block
        b = pltpu.roll(block, 64, 1)
        below, above = pltpu.roll(b, 2 * C - 1, 0), pltpu.roll(b, 1, 0)
        terms.append((b, jnp.where(even, below, -above)))
    for c in range(C):
        total = jnp.zeros((2 * C, 128), F32)
        for s, (b, swapped) in enumerate(terms):
            total = total + (a_ref[s, 2 * c : 2 * c + 1, :] * b + a_ref[s, 2 * c + 1 : 2 * c + 2, :] * swapped)
        out_ref[c * 2 * C : (c + 1) * 2 * C, :] = total[:, :BLOCK_MODES]


def whole(shape):
    return pl.BlockSpec(shape, lambda *_: (0,) * len(shape))


def pinned():
    return pl.BlockSpec(memory_space=pltpu.HBM)


def params(limit):
    return pltpu.CompilerParams(vmem_limit_bytes=int(limit * MIB))


def cost(us):
    return pl.CostEstimate(flops=int(us * 4e8), bytes_accessed=int(us * 3e6), transcendentals=0)


def exchange(block):
    return lax.all_to_all(block, "space", split_axis=0, concat_axis=0, tiled=True)


def shards(fields, cotangent, spectral_weight, point_weight, point_bias):
    yhi, ylo = hi_lo(y_table())
    zhi, zlo = hi_lo(plane_table())
    ytab = jnp.asarray(np.concatenate([yhi, ylo], axis=0))
    ztab = jnp.asarray(np.concatenate([zhi, zlo], axis=0))
    ytab_t = jnp.asarray(np.concatenate([yhi.T, yhi.T, ylo.T], axis=1))
    ztab_k = jnp.asarray(np.concatenate([zhi, zhi, zlo], axis=0))
    mask = jnp.asarray(mode_mask())
    g = jnp.asarray(group_table().astype(ml_dtypes.bfloat16))
    gt = jnp.asarray(group_table().T.astype(ml_dtypes.bfloat16))
    flat = (OWNERS * 32, 128)
    slab_out = jax.ShapeDtypeStruct(flat, F32)
    owned_out = jax.ShapeDtypeStruct((OWNERS, 32, 128), F32)
    rows_out = [jax.ShapeDtypeStruct((ROWS, 128), dtype) for dtype in (BF16, F32)]
    table_specs = [whole(ytab.shape), whole(ztab.shape)]
    inverse_specs = [whole(ytab_t.shape), whole(ztab_k.shape)]
    planes = pltpu.VMEM((SLAB, 256, 256), F32)

    def owner(received, adjoint, *first):
        scale = 1.0 / VOLUME
        tabs = [x_tables(ql, scale if adjoint else 1.0, 1.0 if adjoint else scale) for ql in range(2)]
        dhi, dlo = hi_lo(np.stack([t[0] for t in tabs]))
        ihi, ilo = hi_lo(np.stack([t[1] for t in tabs]))
        weights = spectral_weight.reshape(2 * C, C, 288)
        if adjoint:
            spec_shapes = [(2 * C, 128)] * 4 + [(4, 2 * C, 128)]
        else:
            spec_shapes = [(SAMPLES, 2 * C, 128)]
        scratch = [pltpu.VMEM((2, CP, 384), F32), pltpu.VMEM((2, CP, 384), F32), pltpu.VMEM((3, 2 * CP, 128), F32)]
        scratch.append(pltpu.VMEM((SAMPLES, 2 * C, 128), F32))
        if not adjoint:
            scratch.append(pltpu.SemaphoreType.DMA)
        return pl.pallas_call(
            functools.partial(owner_kernel, adjoint),
            out_shape=[owned_out] + [jax.ShapeDtypeStruct(shape, F32) for shape in spec_shapes],
            scratch_shapes=scratch,
            **({} if adjoint else {"out_specs": [whole(owned_out.shape), pinned()]}),
            compiler_params=params(52),
            cost_estimate=cost(3),
            name="owner_up" if adjoint else "owner_in",
        )(received, weights, *map(jnp.asarray, (dhi, dlo, ihi, ilo)), mask, g, gt, *first)

    def as_rows(array):
        return jnp.transpose(array.reshape(SLAB, C, NY, PLANE), (1, 2, 0, 3)).reshape(ROWS, PLANE)

    def as_planes(rows):
        return jnp.transpose(rows.reshape(C, NY, SLAB, PLANE), (2, 0, 1, 3)).reshape(1, SLAB, C, CELLS)

    def point(values, transposed, *bias):
        return pl.pallas_call(
            functools.partial(point_kernel, transposed),
            out_shape=[rows_out[1], jax.ShapeDtypeStruct((8, 128), F32)],
            compiler_params=params(24),
            cost_estimate=cost(4),
            name="point_in" if transposed else "point_up",
        )(values, point_weight, *bias)

    field_rows = as_rows(fields)
    sems = pltpu.SemaphoreType.DMA
    sent = pl.pallas_call(
        forward_kernel,
        in_specs=[pinned()] * 3,
        out_shape=slab_out,
        scratch_shapes=[
            pltpu.VMEM((ROWS, 128), BF16), pltpu.VMEM(ytab.shape, BF16), pltpu.VMEM(ztab.shape, BF16),
            planes, sems((STEPS + 2,)),
        ],
        compiler_params=params(56),
        cost_estimate=cost(3),
        name="slab_in",
    )(field_rows, ytab, ztab)
    mixed, spec_in = owner(exchange(sent.reshape(OWNERS, 32, 128)), False)
    local, _ = point(field_rows, True, point_bias[None, :])
    activated, upstream, sent = pl.pallas_call(
        middle_kernel,
        in_specs=[whole(flat), pinned(), pinned()] + table_specs + inverse_specs,
        out_specs=[pinned(), pinned(), whole(flat)],
        out_shape=rows_out + [slab_out],
        scratch_shapes=[pltpu.VMEM((ROWS, 128), dtype) for dtype in (F32, BF16, BF16, F32)]
        + [planes, planes, pltpu.VMEM((PAIR_ROWS, 256), F32)]
        + [pltpu.VMEM((PAIR_ROWS, 256), BF16)] * 2
        + [sems((4 * STEPS,))],
        compiler_params=params(52),
        cost_estimate=cost(8),
        name="slab_mid",
    )(exchange(mixed).reshape(flat), local, as_rows(cotangent), ytab, ztab, ytab_t, ztab_k)
    local, token = point(upstream, False)
    back, *sends = owner(exchange(sent.reshape(OWNERS, 32, 128)), True, spec_in, token)
    grad_input, done = pl.pallas_call(
        last_kernel,
        in_specs=[whole(flat), pinned()] + inverse_specs,
        out_specs=[pinned(), whole((8, 128))],
        out_shape=[rows_out[0], jax.ShapeDtypeStruct((8, 128), F32)],
        scratch_shapes=[pltpu.VMEM((ROWS, 128), dtype) for dtype in (F32, BF16)] + [planes, sems((2 * STEPS,))],
        compiler_params=params(52),
        cost_estimate=cost(20),
        name="slab_out",
    )(exchange(back).reshape(flat), local, ytab_t, ztab_k)

    def swap(block, bits):
        return lax.ppermute(block, "sample", [(s, s ^ bits) for s in range(SAMPLES)])

    far = swap(sends[4], 4)
    near = [swap(jnp.stack([sends[d], far[d]]), d) for d in range(1, 4)]
    grad_spectral = pl.pallas_call(
        weight_kernel,
        out_shape=jax.ShapeDtypeStruct((2 * C * C, BLOCK_MODES), F32),
        scratch_shapes=[pltpu.VMEM((SAMPLES, 2 * C, 128), F32)],
        compiler_params=params(8),
        cost_estimate=cost(1),
        name="weight_grad",
    )(sends[0], far, *near, done)
    grad_spectral = jnp.transpose(grad_spectral.reshape(C, C, 2, BLOCK_MODES), (2, 0, 1, 3))
    return as_planes(activated), as_planes(grad_input), grad_spectral


def solution(mesh):
    return jax.shard_map(
        shards,
        mesh=mesh,
        in_specs=(
            P("sample", "space", None, None),
            P("sample", "space", None, None),
            P(None, None, None, "space"),
            P(),
            P(),
        ),
        out_specs=(
            P("sample", "space", None, None),
            P("sample", "space", None, None),
            P(None, None, None, ("space", "sample")),
        ),
        check_vma=False,
    )
```

time: 109 us -> 81.3 us (0.75)
  blocking collectives: 25.2 us -> 0 us
  local copies, waits for them, and re-layouts: 23.3 us -> 5.77 us
  starting transfers between devices: 17.6 us -> 28.1 us
  waiting for transfers between devices: 10.8 us -> 16.1 us
    all_to_all x2 -> x0, blocking collectives: 25.2 us -> none  [the longest x1 14.4 us: shards(): lax.all_to_all(both, 'sample', split_axis=0, concat_axis=0, tiled=True)]
    unnamed x59 -> x45, local copies, waits for them, and re-layouts: 22.6 us -> 5.77 us
    ppermute x0 -> x4, starting transfers between devices: none -> 7.83 us  [swap(): lax.ppermute(block, 'sample', [(s, s ^ bits) for s in range(SAMPLES)])]
    all_to_all x3 -> x4, waiting for transfers between devices: 10.8 us -> 16.1 us  [exchange(): lax.all_to_all(block, 'space', split_axis=0, concat_axis=0, tiled=True)]
    pallas_call x4 -> x6, Pallas kernels: 24.5 us -> 21.3 us  [the longest x1 8.73 us: shards(): pl.pallas_call(middle_kernel, in_specs=[whole(flat), pinned(), pinned()]...]
    all_to_all x3 -> x4, starting transfers between devices: 17.6 us -> 20.3 us  [exchange(): lax.all_to_all(block, 'space', split_axis=0, concat_axis=0, tiled=True)]
    pallas_call x2, Pallas kernels: 5.9 us -> 8.35 us  [owner(): pl.pallas_call(functools.partial(owner_kernel, adjoint), out_shape=[owned...]
  transfers between devices with their start and end apart: 3 -> 8, of which waited for: 3 -> 4; matrix products, arithmetic and copies ran while one was open for 10% -> 1% of each run, Pallas kernels for 0% -> 9%
where the time goes in v2:
time: 81.3 us; the launch traced here: 80.6 us
  Pallas kernels  29.7 us (37%)
  starting transfers between devices  28.1 us (35%)
  waiting for transfers between devices  16.1 us (20%)
  local copies, waits for them, and re-layouts  5.77 us (7%)
  between operations  0.96 us (1%)
    all_to_all x4, starting transfers between devices, exchange(): lax.all_to_all(block, 'space', split_axis=0, concat_axis=0, tiled=True)  20.3 us
    all_to_all x4, waiting for transfers between devices, exchange(): lax.all_to_all(block, 'space', split_axis=0, concat_axis=0, tiled=True)  16.1 us
    pallas_call x1, Pallas kernels, shards(): pl.pallas_call(middle_kernel, in_specs=[whole(flat), pinned(), pinned()]...  8.73 us
    pallas_call x2, Pallas kernels, owner(): pl.pallas_call(functools.partial(owner_kernel, adjoint), out_shape=[owned...  8.35 us
    ppermute x4, starting transfers between devices, swap(): lax.ppermute(block, 'sample', [(s, s ^ bits) for s in range(SAMPLES)])  7.83 us
    unnamed x45, local copies, waits for them, and re-layouts  5.77 us
    pallas_call x1, Pallas kernels, shards(): pl.pallas_call(forward_kernel, in_specs=[pinned()] * 3, out_shape=slab_ou...  4.2 us
    pallas_call x1, Pallas kernels, shards(): pl.pallas_call(last_kernel, in_specs=[whole(flat), pinned()] + inverse_sp...  4.15 us
  transfers between devices with their start and end apart: 8, of which 4 were waited for; matrix products, arithmetic and copies ran while one was open for 1% of the time, Pallas kernels for 9%

profile of v2, /device:TPU:1, one launch (start us, length us, event | category | flops | bytes accessed | tf_op | source)
XLA Modules:
  0.0 80.6 jit_solution(13492736644836024369)
XLA Ops:
  0.6 4.2 %slab_in.1 = f32[512,128]{1,0:T(8,128)} custom-call(bf16[5120,128]{1,0:T(8,128)(2,1)} %bitcast.37, bf16[384,512]{1,0:T(8,128)(2,1)} %constant.22.clone.ytab_hbm.ytab, bf16[128,256]{1,0:T(8,128)(2,1)} %constant.23.clone.ztab_hbm.ztab), custom_call_target="tpu_custom_call" | custom-call | flops 1200000000 | bytes 9000000 | tf_op jit(solution)/shard_map/slab_in/pallas_call | solution.py:467
  4.8 0.0 copy-start.5
  4.9 0.0 copy-start.7
  4.9 0.0 copy-start.8
  4.9 0.0 copy-start.11
  4.9 0.0 copy-start.13
  4.9 0.0 copy-start.15
  4.9 7.1 %all-to-all-start = ((f32[16,32,128]{2,1,0:T(8,128)}), f32[16,32,128]{2,1,0:T(8,128)S(1)}, u32[]{:S(2)}, u32[]{:S(2)}) async-start(f32[16,32,128]{2,1,0:T(8,128)} %bitcast.42), calls=%async_computation | async-start | bytes 524288 | tf_op jit(solution)/shard_map/all_to_all | solution.py:405
  12.0 1.0 %copy.24 = bf16[2,20,20,288]{3,2,1,0:T(8,128)(2,1)} copy(bf16[2,20,20,288]{3,0,2,1:T(2,128)(2,1)S(1)} %copy-done.21) | data formatting | bytes 921600 | tf_op args[2]
  13.0 6.2 %all-to-all-done.s_ref = f32[16,32,128]{2,1,0:T(8,128)S(1)} async-done(((f32[16,32,128]{2,1,0:T(8,128)}), f32[16,32,128]{2,1,0:T(8,128)S(1)}, u32[]{:S(2)}, u32[]{:S(2)}) %all-to-all-start) | async-done | bytes 262176 | tf_op jit(solution)/shard_map/all_to_all | solution.py:405
  19.3 4.3 %owner_in.1 = (f32[16,32,128]{2,1,0:T(8,128)}, f32[8,40,128]{2,1,0:T(8,128)S(1)}) custom-call(f32[16,32,128]{2,1,0:T(8,128)S(1)} %all-to-all-done.s_ref, bf16[40,20,288]{2,1,0:T(8,128)(2,1)} %bitcast.40, bf16[2,128,512]{2,1,0:T(8,128)(2,1)S(1)} %copy-done.8, bf16[2,128,512]{2,1,0:T(8,128)(2,1)S(1)} %copy-done.7, bf16[2,128,512]{2,1,0:T(8,128)(2,1)S(1)} %copy-done.6, ...), custom_call_target="tpu_custom_call" | custom-call | flops 1200000000 | bytes 9000000 | tf_op jit(solution)/shard_map/owner_in/pallas_call | solution.py:440
  23.6 4.3 %all-to-all-start.1 = ((f32[16,32,128]{2,1,0:T(8,128)}), f32[16,32,128]{2,1,0:T(8,128)S(1)}, u32[]{:S(2)}, u32[]{:S(2)}) async-start(f32[16,32,128]{2,1,0:T(8,128)} %get-tuple-element.19), calls=%async_computation.1 | async-start | bytes 524288 | tf_op jit(solution)/shard_map/all_to_all | solution.py:405
  28.0 0.0 copy-start.3
  28.0 0.0 copy-start.4
  28.0 1.1 %point_in.1 = (f32[5120,128]{1,0:T(8,128)S(1)}, f32[8,128]{1,0:T(8,128)}) custom-call(bf16[5120,128]{1,0:T(8,128)(2,1)S(1)} %bitcast.38, bf16[20,20]{1,0:T(8,128)(2,1)S(1)} %copy-done.1, f32[1,20]{1,0:T(1,128)S(1)} %bitcast.39), custom_call_target="tpu_custom_call" | custom-call | flops 1600000000 | bytes 12000000 | tf_op jit(solution)/shard_map/point_in/pallas_call | solution.py:457
  29.1 1.5 %copy-done.18 = f32[5120,128]{1,0:T(8,128)} copy-done((f32[5120,128]{1,0:T(8,128)}, f32[5120,128]{1,0:T(8,128)S(1)}, u32[]{:S(2)}) %copy-start.18) | copy-done | bytes 2621464
  30.6 4.6 %all-to-all-done.1 = f32[16,32,128]{2,1,0:T(8,128)S(1)} async-done(((f32[16,32,128]{2,1,0:T(8,128)}), f32[16,32,128]{2,1,0:T(8,128)S(1)}, u32[]{:S(2)}, u32[]{:S(2)}) %all-to-all-start.1) | async-done | bytes 262176 | tf_op jit(solution)/shard_map/all_to_all | solution.py:405
  35.2 8.7 %slab_mid.1 = (bf16[5120,128]{1,0:T(8,128)(2,1)}, f32[5120,128]{1,0:T(8,128)}, f32[512,128]{1,0:T(8,128)}) custom-call(f32[512,128]{1,0:T(8,128)S(1)} %bitcast.33, f32[5120,128]{1,0:T(8,128)} %copy-done.18, bf16[5120,128]{1,0:T(8,128)(2,1)} %bitcast.43, bf16[384,512]{1,0:T(8,128)(2,1)S(1)} %copy-done.4, bf16[128,256]{1,0:T(8,128)(2,1)S(1)} %copy-done.12, ...), custom_call_target="tpu_custom_call" | custom-call | flops 3200000000 | bytes 24000000 | tf_op jit(solution)/shard_map/slab_mid/pallas_call | solution.py:481
  43.9 4.3 %all-to-all-start.2 = ((f32[16,32,128]{2,1,0:T(8,128)}), f32[16,32,128]{2,1,0:T(8,128)S(1)}, u32[]{:S(2)}, u32[]{:S(2)}) async-start(f32[16,32,128]{2,1,0:T(8,128)} %bitcast.15), calls=%async_computation.2 | async-start | bytes 524288 | tf_op jit(solution)/shard_map/all_to_all | solution.py:405
  48.3 1.7 %copy-done.17 = f32[5120,128]{1,0:T(8,128)S(1)} copy-done((f32[5120,128]{1,0:T(8,128)S(1)}, f32[5120,128]{1,0:T(8,128)}, u32[]{:S(2)}) %copy-start.17) | copy-done | bytes 2621464
  50.0 1.8 %point_up.1 = (f32[5120,128]{1,0:T(8,128)S(1)}, f32[8,128]{1,0:T(8,128)S(1)}) custom-call(f32[5120,128]{1,0:T(8,128)S(1)} %copy-done.17, bf16[20,20]{1,0:T(8,128)(2,1)S(1)} %copy-done.1), custom_call_target="tpu_custom_call" | custom-call | flops 1600000000 | bytes 12000000 | tf_op jit(solution)/shard_map/point_up/pallas_call | solution.py:457
  51.8 1.5 %copy-done.16 = f32[5120,128]{1,0:T(8,128)} copy-done((f32[5120,128]{1,0:T(8,128)}, f32[5120,128]{1,0:T(8,128)S(1)}, u32[]{:S(2)}) %copy-start.16) | copy-done | bytes 2621464
  53.3 2.2 %all-to-all-done.2.s_ref = f32[16,32,128]{2,1,0:T(8,128)S(1)} async-done(((f32[16,32,128]{2,1,0:T(8,128)}), f32[16,32,128]{2,1,0:T(8,128)S(1)}, u32[]{:S(2)}, u32[]{:S(2)}) %all-to-all-start.2) | async-done | bytes 262176 | tf_op jit(solution)/shard_map/all_to_all | solution.py:405
  55.5 4.0 %owner_up.1 = (f32[16,32,128]{2,1,0:T(8,128)}, f32[40,128]{1,0:T(8,128)S(1)}, f32[40,128]{1,0:T(8,128)S(1)}, f32[40,128]{1,0:T(8,128)S(1)}, f32[40,128]{1,0:T(8,128)S(1)}, /*index=5*/f32[4,40,128]{2,1,0:T(8,128)S(1)}) custom-call(f32[16,32,128]{2,1,0:T(8,128)S(1)} %all-to-all-done.2.s_ref, bf16[40,20,288]{2,1,0:T(8,128)(2,1)} %bitcast.41, ...), custom_call_target="tpu_custom_call" | custom-call | flops 1200000000 | bytes 9000000 | tf_op jit(solution)/shard_map/owner_up/pallas_call | solution.py:440
  59.5 3.6 %collective-permute-start = (f32[4,40,128]{2,1,0:T(8,128)S(1)}, f32[4,40,128]{2,1,0:T(8,128)S(1)}, u32[]{:S(2)}, u32[]{:S(2)}) collective-permute-start(f32[4,40,128]{2,1,0:T(8,128)S(1)} %get-tuple-element.30), channel_id=1, source_target_pairs={{0,4},{1,5},{2,6},{3,7},{4,0},{5,1},{6,2},{7,3},{8,12},{9,13},{10,... | collective-permute-start | bytes 245768 | tf_op jit(solution)/shard_map/ppermute | solution.py:508
  63.1 4.6 %all-to-all-start.3 = ((f32[16,32,128]{2,1,0:T(8,128)}), f32[16,32,128]{2,1,0:T(8,128)S(1)}, u32[]{:S(2)}, u32[]{:S(2)}) async-start(f32[16,32,128]{2,1,0:T(8,128)} %get-tuple-element.26), calls=%async_computation.3 | async-start | bytes 524288 | tf_op jit(solution)/shard_map/all_to_all | solution.py:405
  67.7 2.5 %collective-permute-start.1 = (f32[2,40,128]{2,1,0:T(8,128)S(1)}, f32[2,40,128]{2,1,0:T(8,128)S(1)}, u32[]{:S(2)}, u32[]{:S(2)}) collective-permute-start(f32[2,40,128]{2,1,0:T(8,128)S(1)} %pad_maximum_fusion), channel_id=1, source_target_pairs={{0,1},{1,0},{2,3},{3,2},{4,5},{5,4},{6,7},{7,6},{8,9},{9,8},{10,11... | collective-permute-start | bytes 122888 | tf_op jit(solution)/shard_map/ppermute | solution.py:508
  70.3 0.7 collective-permute-start.2
  71.0 1.0 %collective-permute-start.3 = (f32[2,40,128]{2,1,0:T(8,128)S(1)}, f32[2,40,128]{2,1,0:T(8,128)S(1)}, u32[]{:S(2)}, u32[]{:S(2)}) collective-permute-start(f32[2,40,128]{2,1,0:T(8,128)S(1)} %pad_maximum_fusion.2), channel_id=1, source_target_pairs={{0,3},{1,2},{2,1},{3,0},{4,7},{5,6},{6,5},{7,4},{8,11},{9,10},{10,... | collective-permute-start | bytes 122888 | tf_op jit(solution)/shard_map/ppermute | solution.py:508
  72.0 3.1 %all-to-all-done.3 = f32[16,32,128]{2,1,0:T(8,128)S(1)} async-done(((f32[16,32,128]{2,1,0:T(8,128)}), f32[16,32,128]{2,1,0:T(8,128)S(1)}, u32[]{:S(2)}, u32[]{:S(2)}) %all-to-all-start.3) | async-done | bytes 262176 | tf_op jit(solution)/shard_map/all_to_all | solution.py:405
  75.1 4.2 %slab_out.1 = (bf16[5120,128]{1,0:T(8,128)(2,1)}, f32[8,128]{1,0:T(8,128)S(1)}) custom-call(f32[512,128]{1,0:T(8,128)S(1)} %bitcast.32, f32[5120,128]{1,0:T(8,128)} %copy-done.16, bf16[512,576]{1,0:T(8,128)(2,1)S(1)} %copy-done.3, bf16[192,256]{1,0:T(8,128)(2,1)S(1)} %copy-done.10), custom_call_target="tpu_custom_call" | custom-call | flops 8000000000 | bytes 60000000 | tf_op jit(solution)/shard_map/slab_out/pallas_call | solution.py:496
  79.3 1.4 %weight_grad.1 = f32[800,36]{1,0:T(8,128)} custom-call(f32[40,128]{1,0:T(8,128)S(1)} %get-tuple-element.29.refs_0_, f32[4,40,128]{2,1,0:T(8,128)S(1)} %collective-permute-done.refs_1_, f32[2,40,128]{2,1,0:T(8,128)S(1)} %collective-permute-done.1.refs_2_, f32[2,40,128]{2,1,0:T(8,128)S(1)} %collective-permute-done.2.refs_3_, ...), custom_call_target="tpu_custom_call" | custom-call | flops 400000000 | bytes 3000000 | tf_op jit(solution)/shard_map/weight_grad/pallas_call | solution.py:512
  (41 shorter events, 0.1 us)
Async XLA Ops:
  0.6 11.4 %copy-start.21 = (bf16[2,20,20,288]{3,0,2,1:T(2,128)(2,1)S(1)}, bf16[2,20,20,288]{3,0,2,1:T(2,128)(2,1)}, u32[]{:S(2)}) copy-start(bf16[2,20,20,288]{3,0,2,1:T(2,128)(2,1)} %param.22) | copy-start | bytes 1382404
  4.8 14.3 %copy-start.5 = (bf16[2,128,512]{2,1,0:T(8,128)(2,1)S(1)}, bf16[2,128,512]{2,1,0:T(8,128)(2,1)}, u32[]{:S(2)}) copy-start(bf16[2,128,512]{2,1,0:T(8,128)(2,1)} %constant.32.clone.ilo.dlo) | copy-start | bytes 786436
  4.9 14.3 %copy-start.6 = (bf16[2,128,512]{2,1,0:T(8,128)(2,1)S(1)}, bf16[2,128,512]{2,1,0:T(8,128)(2,1)}, u32[]{:S(2)}) copy-start(bf16[2,128,512]{2,1,0:T(8,128)(2,1)} %constant.31.clone.ihi.dhi) | copy-start | bytes 786436
  4.9 14.3 %copy-start.7 = (bf16[2,128,512]{2,1,0:T(8,128)(2,1)S(1)}, bf16[2,128,512]{2,1,0:T(8,128)(2,1)}, u32[]{:S(2)}) copy-start(bf16[2,128,512]{2,1,0:T(8,128)(2,1)} %constant.30.clone.dlo.ilo) | copy-start | bytes 786436
  4.9 14.3 %copy-start.8 = (bf16[2,128,512]{2,1,0:T(8,128)(2,1)S(1)}, bf16[2,128,512]{2,1,0:T(8,128)(2,1)}, u32[]{:S(2)}) copy-start(bf16[2,128,512]{2,1,0:T(8,128)(2,1)} %constant.29.clone.dhi.ihi) | copy-start | bytes 786436
  4.9 14.3 %copy-start.11 = (f32[2,24,512]{2,1,0:T(8,128)S(1)}, f32[2,24,512]{2,1,0:T(8,128)}, u32[]{:S(2)}) copy-start(f32[2,24,512]{2,1,0:T(8,128)} %constant.26.clone.mask_ref) | copy-start | bytes 294916
  4.9 14.3 %copy-start.13 = (bf16[240,24]{1,0:T(8,128)(2,1)S(1)}, bf16[240,24]{1,0:T(8,128)(2,1)}, u32[]{:S(2)}) copy-start(bf16[240,24]{1,0:T(8,128)(2,1)} %constant.28.clone.gt_ref) | copy-start | bytes 34564
  4.9 14.3 %copy-start.15 = (bf16[24,240]{1,0:T(8,128)(2,1)S(1)}, bf16[24,240]{1,0:T(8,128)(2,1)}, u32[]{:S(2)}) copy-start(bf16[24,240]{1,0:T(8,128)(2,1)} %constant.27.clone.g_ref) | copy-start | bytes 34564
  4.9 14.2 %all-to-all-start = ((f32[16,32,128]{2,1,0:T(8,128)}), f32[16,32,128]{2,1,0:T(8,128)S(1)}, u32[]{:S(2)}, u32[]{:S(2)}) async-start(f32[16,32,128]{2,1,0:T(8,128)} %bitcast.42), calls=%async_computation | async-start | bytes 524288 | tf_op jit(solution)/shard_map/all_to_all | solution.py:405
  19.2 8.7 %copy-start = (bf16[1,4,20,8192]{3,1,2,0:T(4,128)(2,1)S(1)}, bf16[1,4,20,8192]{3,1,2,0:T(4,128)(2,1)}, u32[]{:S(2)}) copy-start(bf16[1,4,20,8192]{3,1,2,0:T(4,128)(2,1)} %param.20) | copy-start | bytes 3932164
  19.2 8.7 %copy-start.1 = (bf16[20,20]{1,0:T(8,128)(2,1)S(1)}, bf16[20,20]{1,0:T(8,128)(2,1)}, u32[]{:S(2)}) copy-start(bf16[20,20]{1,0:T(8,128)(2,1)} %w_ref.3) | copy-start | bytes 2404
  19.2 8.7 %copy-start.2 = (f32[20]{0:T(128)S(1)}, f32[20]{0:T(128)}, u32[]{:S(2)}) copy-start(f32[20]{0:T(128)} %param.24) | copy-start | bytes 244
  23.6 4.3 %copy-start.19 = (f32[8,40,128]{2,1,0:T(8,128)}, f32[8,40,128]{2,1,0:T(8,128)S(1)}, u32[]{:S(2)}) copy-start(f32[8,40,128]{2,1,0:T(8,128)S(1)} %get-tuple-element.23.rest_0_) | copy-start | bytes 491524
  23.6 11.5 %all-to-all-start.1 = ((f32[16,32,128]{2,1,0:T(8,128)}), f32[16,32,128]{2,1,0:T(8,128)S(1)}, u32[]{:S(2)}, u32[]{:S(2)}) async-start(f32[16,32,128]{2,1,0:T(8,128)} %get-tuple-element.19), calls=%async_computation.1 | async-start | bytes 524288 | tf_op jit(solution)/shard_map/all_to_all | solution.py:405
  28.0 7.2 %copy-start.3 = (bf16[512,576]{1,0:T(8,128)(2,1)S(1)}, bf16[512,576]{1,0:T(8,128)(2,1)}, u32[]{:S(2)}) copy-start(bf16[512,576]{1,0:T(8,128)(2,1)} %constant.24.clone.ytab_t) | copy-start | bytes 1769476
  28.0 7.2 %copy-start.4 = (bf16[384,512]{1,0:T(8,128)(2,1)S(1)}, bf16[384,512]{1,0:T(8,128)(2,1)}, u32[]{:S(2)}) copy-start(bf16[384,512]{1,0:T(8,128)(2,1)} %constant.22.clone.ytab_hbm.ytab) | copy-start | bytes 1179652
  28.0 7.2 %copy-start.10 = (bf16[192,256]{1,0:T(8,128)(2,1)S(1)}, bf16[192,256]{1,0:T(8,128)(2,1)}, u32[]{:S(2)}) copy-start(bf16[192,256]{1,0:T(8,128)(2,1)} %constant.25.clone.ztab_k) | copy-start | bytes 294916
  28.0 7.2 %copy-start.12 = (bf16[128,256]{1,0:T(8,128)(2,1)S(1)}, bf16[128,256]{1,0:T(8,128)(2,1)}, u32[]{:S(2)}) copy-start(bf16[128,256]{1,0:T(8,128)(2,1)} %constant.23.clone.ztab_hbm.ztab) | copy-start | bytes 196612
  29.1 1.5 %copy-start.18 = (f32[5120,128]{1,0:T(8,128)}, f32[5120,128]{1,0:T(8,128)S(1)}, u32[]{:S(2)}) copy-start(f32[5120,128]{1,0:T(8,128)S(1)} %get-tuple-element.20.local_hbm) | copy-start | bytes 7864324
  43.9 11.6 %all-to-all-start.2 = ((f32[16,32,128]{2,1,0:T(8,128)}), f32[16,32,128]{2,1,0:T(8,128)S(1)}, u32[]{:S(2)}, u32[]{:S(2)}) async-start(f32[16,32,128]{2,1,0:T(8,128)} %bitcast.15), calls=%async_computation.2 | async-start | bytes 524288 | tf_op jit(solution)/shard_map/all_to_all | solution.py:405
  48.2 1.7 %copy-start.17 = (f32[5120,128]{1,0:T(8,128)S(1)}, f32[5120,128]{1,0:T(8,128)}, u32[]{:S(2)}) copy-start(f32[5120,128]{1,0:T(8,128)} %get-tuple-element.24.x_ref) | copy-start | bytes 7864324
  50.0 5.5 %copy-start.9 = (bf16[2,128,512]{2,1,0:T(8,128)(2,1)S(1)}, bf16[2,128,512]{2,1,0:T(8,128)(2,1)}, u32[]{:S(2)}) copy-start(bf16[2,128,512]{2,1,0:T(8,128)(2,1)} %constant.29.clone.dhi.ihi) | copy-start | bytes 786436
  50.0 5.5 %copy-start.14 = (bf16[240,24]{1,0:T(8,128)(2,1)S(1)}, bf16[240,24]{1,0:T(8,128)(2,1)}, u32[]{:S(2)}) copy-start(bf16[240,24]{1,0:T(8,128)(2,1)} %constant.28.clone.gt_ref) | copy-start | bytes 34564
  50.0 5.5 %copy-start.20 = (f32[8,40,128]{2,1,0:T(8,128)S(1)}, f32[8,40,128]{2,1,0:T(8,128)}, u32[]{:S(2)}) copy-start(f32[8,40,128]{2,1,0:T(8,128)} %copy-done.19) | copy-start | bytes 491524
  51.8 1.5 %copy-start.16 = (f32[5120,128]{1,0:T(8,128)}, f32[5120,128]{1,0:T(8,128)S(1)}, u32[]{:S(2)}) copy-start(f32[5120,128]{1,0:T(8,128)S(1)} %get-tuple-element.27.local_hbm) | copy-start | bytes 7864324
  59.5 8.2 %collective-permute-start = (f32[4,40,128]{2,1,0:T(8,128)S(1)}, f32[4,40,128]{2,1,0:T(8,128)S(1)}, u32[]{:S(2)}, u32[]{:S(2)}) collective-permute-start(f32[4,40,128]{2,1,0:T(8,128)S(1)} %get-tuple-element.30), channel_id=1, source_target_pairs={{0,4},{1,5},{2,6},{3,7},{4,0},{5,1},{6,2},{7,3},{8,12},{9,13},{10,... | collective-permute-start | bytes 245768 | tf_op jit(solution)/shard_map/ppermute | solution.py:508
  63.1 12.0 %all-to-all-start.3 = ((f32[16,32,128]{2,1,0:T(8,128)}), f32[16,32,128]{2,1,0:T(8,128)S(1)}, u32[]{:S(2)}, u32[]{:S(2)}) async-start(f32[16,32,128]{2,1,0:T(8,128)} %get-tuple-element.26), calls=%async_computation.3 | async-start | bytes 524288 | tf_op jit(solution)/shard_map/all_to_all | solution.py:405
  67.7 11.5 %collective-permute-start.1 = (f32[2,40,128]{2,1,0:T(8,128)S(1)}, f32[2,40,128]{2,1,0:T(8,128)S(1)}, u32[]{:S(2)}, u32[]{:S(2)}) collective-permute-start(f32[2,40,128]{2,1,0:T(8,128)S(1)} %pad_maximum_fusion), channel_id=1, source_target_pairs={{0,1},{1,0},{2,3},{3,2},{4,5},{5,4},{6,7},{7,6},{8,9},{9,8},{10,11... | collective-permute-start | bytes 122888 | tf_op jit(solution)/shard_map/ppermute | solution.py:508
  70.3 9.0 %collective-permute-start.2 = (f32[2,40,128]{2,1,0:T(8,128)S(1)}, f32[2,40,128]{2,1,0:T(8,128)S(1)}, u32[]{:S(2)}, u32[]{:S(2)}) collective-permute-start(f32[2,40,128]{2,1,0:T(8,128)S(1)} %pad_maximum_fusion.1), channel_id=1, source_target_pairs={{0,2},{1,3},{2,0},{3,1},{4,6},{5,7},{6,4},{7,5},{8,10},{9,11},{10,... | collective-permute-start | bytes 122888 | tf_op jit(solution)/shard_map/ppermute | solution.py:508
  71.0 8.2 %collective-permute-start.3 = (f32[2,40,128]{2,1,0:T(8,128)S(1)}, f32[2,40,128]{2,1,0:T(8,128)S(1)}, u32[]{:S(2)}, u32[]{:S(2)}) collective-permute-start(f32[2,40,128]{2,1,0:T(8,128)S(1)} %pad_maximum_fusion.2), channel_id=1, source_target_pairs={{0,3},{1,2},{2,1},{3,0},{4,7},{5,6},{6,5},{7,4},{8,11},{9,10},{10,... | collective-permute-start | bytes 122888 | tf_op jit(solution)/shard_map/ppermute | solution.py:508

commit v3 on v2

--- a/solution.py
+++ b/solution.py
@@ -24,10 +24,12 @@
 PAIRS = C // 2
 CHUNK = 64
 STEPS = C // 4
+FAR = 1
+NEAR = (0, 2, 4, 6)
 ROWS = C * SLAB * NY
-PAIR_ROWS = 2 * SLAB * NY
-QUAD_ROWS = 2 * PAIR_ROWS
-QUARTER = 2 * SLAB * 24
+QUAD_ROWS = 4 * SLAB * NY
+LAST_SINE = (12, 0)
+CELL_ROWS = SLAB * NY
 MIX = 16
 VOLUME = NX * NY * NZ * NT
 F32, BF16 = jnp.float32, jnp.bfloat16
@@ -45,11 +47,15 @@
 
 
 def y_table():
-    k = signed(np.arange(MY), MY)[:, None]
-    theta = 2 * np.pi * ((k * np.arange(NY)[None, :]) % NY) / NY
-    eye2, eye4 = np.eye(2), np.eye(SLAB)
-    parts = [np.einsum("ab,pq,ky->apkqyb", eye4, eye2, t) for t in (np.cos(theta), -np.sin(theta))]
-    return np.stack(parts).reshape(QUARTER, PAIR_ROWS)
+    angle = 2 * np.pi * np.arange(NY) / NY
+    rows = np.zeros((2, 16, NY))
+    for parity in range(2):
+        for k in range(7):
+            rows[parity, 4 * parity + k] = np.cos(k * angle)
+        for k in range(1, 6):
+            rows[parity, 4 * parity + 6 + k] = -np.sin(k * angle)
+        rows[parity, LAST_SINE[parity]] = np.sin(6 * angle)
+    return np.einsum("prv,xz->pxrvz", rows, np.eye(SLAB)).reshape(2, 16 * SLAB, NY * SLAB)
 
 
 def plane_table():
@@ -67,27 +73,28 @@
     return np.concatenate(rows, axis=0)
 
 
-def x_tables(ql, forward_scale, inverse_scale):
+def x_table(ql):
     lane = np.arange(256) + 128 * ql
     f = signed(lane % MX, MX)[None, :]
     theta = 2 * np.pi * ((f * np.arange(NX)[:, None]) % NX) / NX
     cos, sin = np.cos(theta), np.sin(theta)
-    forward = np.zeros((NX, 2, 512))
-    forward[:, 0] = np.concatenate([cos, -sin], axis=1)
-    forward[:, 1] = np.concatenate([sin, cos], axis=1)
-    inverse = np.zeros((NX, 2, 512))
-    inverse[:, 0] = np.concatenate([cos, -sin], axis=1)
-    inverse[:, 1] = np.concatenate([sin, cos], axis=1)
-    return forward.reshape(128, 512) * forward_scale, inverse.reshape(128, 512) * inverse_scale
+    rows = [np.concatenate([cos, -sin], axis=1), np.concatenate([sin, cos], axis=1)]
+    return np.stack(rows, axis=1).reshape(2 * NX, 512)
 
 
 def mode_mask():
+    fold = np.zeros((MY, MY), np.float32)
+    fold[0, 0] = fold[6, 6] = 1.0
+    for k in range(1, 6):
+        fold[k, k] = fold[k, MY - k] = fold[6 + k, k] = 1.0
+        fold[6 + k, MY - k] = -1.0
     mask = np.zeros((2, 24, 512), np.float32)
     for ql in range(2):
         lane = np.arange(256) + 128 * ql
         code = np.where(lane < 288, lane // MX, -1)
-        hit = code[None, :] == (ql * MY + np.arange(24)[:, None] % MY)
-        mask[ql] = np.concatenate([hit, hit], axis=1)
+        here = code // MY == ql
+        half = np.where(here[None, :], fold[np.arange(24) % MY][:, code % MY], 0.0)
+        mask[ql] = np.concatenate([half, half], axis=1)
     return mask
 
 
@@ -115,17 +122,30 @@
     return lax.dot_general(a, b, (((1,), (1,)), ((), ())), preferred_element_type=F32)
 
 
-def forward_y(quad, left, right, ytab, u_ref):
-    u = dot(ytab[...], jnp.concatenate([left[0], right[0]], axis=1))
-    u = u[:QUARTER] + u[QUARTER:]
-    if len(left) > 1:
-        u = u + dot(ytab[:QUARTER], jnp.concatenate([left[1], right[1]], axis=1))
-    for side in range(2):
-        rows = slice(quad * 48 + side * 24, quad * 48 + side * 24 + 24)
-        for reim in range(2):
+def folded_rows(parity):
+    return lax.broadcasted_iota(jnp.int32, (16, 128), 0) - 4 * parity
+
+
+def forward_y(quad, cells, ytab, u_ref):
+    for parity in range(2):
+        first = 4 * quad + parity
+        left, right = cells(first), cells(first + 2)
+        table = ytab[parity]
+        u = dot(table, jnp.concatenate([left[0], right[0]], axis=1))
+        u = u[:64] + u[64:]
+        if len(left) > 1:
+            u = u + dot(table[:64], jnp.concatenate([left[1], right[1]], axis=1))
+        k = folded_rows(parity)
+        kept = slice(4 * parity, 4 * parity + MY)
+        for side in range(2):
+            at = (first + 2 * side) * MY
             for x in range(SLAB):
-                at = (reim * SLAB + x) * 24
-                u_ref[x, rows, reim * 128 : (reim + 1) * 128] = u[at : at + 24, side * 128 : (side + 1) * 128]
+                group = u[x * 16 : (x + 1) * 16, side * 128 : (side + 1) * 128]
+                sine = group[LAST_SINE[parity] : LAST_SINE[parity] + 1]
+                real = jnp.where(k <= 6, group, 0.0)
+                imag = jnp.where(k >= 7, group, jnp.where(k == 6, sine, 0.0))
+                u_ref[x, at : at + MY, :128] = real[kept]
+                u_ref[x, at : at + MY, 128:] = imag[kept]
 
 
 def forward_plane(u_ref, ztab, out_ref):
@@ -156,16 +176,24 @@
 
 
 def inverse_y(quad, h_ref, ytab_t):
-    pieces = []
-    for reim in range(2):
-        for x in range(SLAB):
-            sides = [
-                h_ref[x, quad * 48 + side * 24 : quad * 48 + side * 24 + 24, reim * 128 : (reim + 1) * 128]
-                for side in range(2)
-            ]
-            pieces.append(jnp.concatenate(sides, axis=1))
-    hi, lo = split(jnp.concatenate(pieces, axis=0))
-    return dot(ytab_t[...], jnp.concatenate([hi, lo, hi], axis=0))
+    out = [None] * 4
+    for parity in range(2):
+        k = folded_rows(parity)
+        last = LAST_SINE[parity] - 4 * parity
+        sides = []
+        for side in range(2):
+            at = (4 * quad + parity + 2 * side) * MY - 4 * parity
+            groups = []
+            for x in range(SLAB):
+                imag = h_ref[x, at : at + 16, 128:]
+                sine = imag[4 * parity + 6 : 4 * parity + 7]
+                group = jnp.where(k <= 6, h_ref[x, at : at + 16, :128], imag)
+                groups.append(jnp.where(k == last, sine, group))
+            sides.append(jnp.concatenate(groups, axis=0))
+        hi, lo = split(jnp.concatenate(sides, axis=1))
+        both = dot(ytab_t[parity], jnp.concatenate([hi, lo, hi], axis=0))
+        out[parity], out[parity + 2] = both[:, :128], both[:, 128:]
+    return out
 
 
 def quad_rows(quad):
@@ -177,8 +205,6 @@
         pltpu.make_async_copy(source.at[quad_rows(q)], target.at[quad_rows(q)], sems.at[first + q])
         for q in range(STEPS)
     ]
-    for copy in copies:
-        copy.start()
     return copies
 
 
@@ -187,15 +213,13 @@
         pltpu.make_async_copy(ytab_hbm, ytab, sems.at[STEPS]),
         pltpu.make_async_copy(ztab_hbm, ztab, sems.at[STEPS + 1]),
     ]
-    tables[0].start()
     copies = fetch(x_hbm, x_ref, sems, 0)
-    tables[1].start()
+    for copy in [copies[0], tables[0]] + copies[1:] + [tables[1]]:
+        copy.start()
     tables[0].wait()
     for quad in range(STEPS):
         copies[quad].wait()
-        at = quad * QUAD_ROWS
-        left, right = x_ref[at : at + PAIR_ROWS, :], x_ref[at + PAIR_ROWS : at + QUAD_ROWS, :]
-        forward_y(quad, [left], [right], ytab, u_ref)
+        forward_y(quad, lambda c: [x_ref[c * CELL_ROWS : (c + 1) * CELL_ROWS, :]], ytab, u_ref)
     tables[1].wait()
     forward_plane(u_ref, ztab, out_ref)
 
@@ -207,50 +231,73 @@
 ):
     local_copies = fetch(local_hbm, local_ref, sems, 0)
     cot_copies = fetch(cot_hbm, cot_ref, sems, STEPS)
+    for pair in zip(local_copies, cot_copies):
+        for copy in pair:
+            copy.start()
     stores = []
     inverse_plane(recv_ref, ztab_k, h_ref)
     for quad in range(STEPS):
-        pre_ref[...] = inverse_y(quad, h_ref, ytab_t)
+        for k, block in enumerate(inverse_y(quad, h_ref, ytab_t)):
+            pre_ref[k * CELL_ROWS : (k + 1) * CELL_ROWS, :] = block
         local_copies[quad].wait()
         cot_copies[quad].wait()
-        for side in range(2):
-            lanes = slice(side * 128, (side + 1) * 128)
-            for i in range(PAIR_ROWS // CHUNK):
-                near = slice(i * CHUNK, (i + 1) * CHUNK)
-                at = quad * QUAD_ROWS + side * PAIR_ROWS + i * CHUNK
-                rows = slice(at, at + CHUNK)
-                pre = pre_ref[near, lanes] + local_ref[rows, :]
-                cdf = 0.5 * (1.0 + lax.erf(pre * (1.0 / math.sqrt(2.0))))
-                slope = cdf + pre * jnp.exp(-0.5 * pre * pre) * (1.0 / math.sqrt(2.0 * math.pi))
-                act_ref[rows, :] = (pre * cdf).astype(BF16)
-                up = cot_ref[rows, :].astype(F32) * slope
-                up_ref[rows, :] = up
-                hi_ref[near, lanes], lo_ref[near, lanes] = split(up)
+        for i in range(QUAD_ROWS // CHUNK):
+            near = slice(i * CHUNK, (i + 1) * CHUNK)
+            rows = slice(quad * QUAD_ROWS + i * CHUNK, quad * QUAD_ROWS + (i + 1) * CHUNK)
+            pre = pre_ref[near, :] + local_ref[rows, :]
+            cdf = 0.5 * (1.0 + lax.erf(pre * (1.0 / math.sqrt(2.0))))
+            slope = cdf + pre * jnp.exp(-0.5 * pre * pre) * (1.0 / math.sqrt(2.0 * math.pi))
+            act_ref[rows, :] = (pre * cdf).astype(BF16)
+            up = cot_ref[rows, :].astype(F32) * slope
+            up_ref[rows, :] = up
+            hi_ref[near, :], lo_ref[near, :] = split(up)
         for k, (source, target) in enumerate(((act_ref, act_hbm), (up_ref, up_hbm))):
             store = pltpu.make_async_copy(
                 source.at[quad_rows(quad)], target.at[quad_rows(quad)], sems.at[(2 + k) * STEPS + quad]
             )
             store.start()
             stores.append(store)
-        sides = [[ref[:, side * 128 : (side + 1) * 128] for ref in (hi_ref, lo_ref)] for side in range(2)]
-        forward_y(quad, sides[0], sides[1], ytab, u_ref)
+        def parts(c):
+            rows = slice((c - 4 * quad) * CELL_ROWS, (c - 4 * quad + 1) * CELL_ROWS)
+            return [hi_ref[rows, :], lo_ref[rows, :]]
+
+        forward_y(quad, parts, ytab, u_ref)
     forward_plane(u_ref, ztab, out_ref)
     for store in stores:
         store.wait()
 
 
+def weight_kernel(own_ref, far_ref, near1_ref, near2_ref, near3_ref, _, grad_ref, a_ref):
+    near_refs = [near1_ref, near2_ref, near3_ref]
+    even = lax.broadcasted_iota(jnp.int32, (2 * C, 128), 0) % 2 == 0
+    terms = []
+    for s, ref in enumerate([own_ref, far_ref.at[0]] + [ref.at[k] for ref in near_refs for k in range(2)]):
+        block = ref[...]
+        a_ref[s] = block
+        b = pltpu.roll(block, 64, 1)
+        below, above = pltpu.roll(b, 2 * C - 1, 0), pltpu.roll(b, 1, 0)
+        terms.append((b, jnp.where(even, below, -above)))
+    for c in range(C):
+        total = jnp.zeros((2 * C, 128), F32)
+        for s, (b, swapped) in enumerate(terms):
+            total = total + (a_ref[s, 2 * c : 2 * c + 1, :] * b + a_ref[s, 2 * c + 1 : 2 * c + 2, :] * swapped)
+        grad_ref[c * 2 * C : (c + 1) * 2 * C, :] = total[:, :BLOCK_MODES]
+
+
 def last_kernel(recv_ref, local_hbm, ytab_t, ztab_k, out_hbm, token_ref, local_ref, out_ref, h_ref, sems):
     token_ref[...] = jnp.zeros_like(token_ref)
     local_copies = fetch(local_hbm, local_ref, sems, 0)
+    for copy in local_copies:
+        copy.start()
     stores = []
     inverse_plane(recv_ref, ztab_k, h_ref)
     for quad in range(STEPS):
         spectral = inverse_y(quad, h_ref, ytab_t)
         local_copies[quad].wait()
-        for side in range(2):
-            at = quad * QUAD_ROWS + side * PAIR_ROWS
-            rows = slice(at, at + PAIR_ROWS)
-            out_ref[rows, :] = (spectral[:, side * 128 : (side + 1) * 128] + local_ref[rows, :]).astype(BF16)
+        for k in range(4):
+            at = (4 * quad + k) * CELL_ROWS
+            rows = slice(at, at + CELL_ROWS)
+            out_ref[rows, :] = (spectral[k] + local_ref[rows, :]).astype(BF16)
         store = pltpu.make_async_copy(
             out_ref.at[quad_rows(quad)], out_hbm.at[quad_rows(quad)], sems.at[STEPS + quad]
         )
@@ -295,7 +342,10 @@
                 ]
 
 
-def owner_kernel(adjoint, s_ref, w_ref, dhi, dlo, ihi, ilo, mask_ref, g_ref, gt_ref, *rest):
+def owner_kernel(adjoint, s_ref, w_hbm, xhi, xlo, mask_ref, g_ref, *rest):
+    *rest, w_ref, w_sem = rest
+    fetch_w = pltpu.make_async_copy(w_hbm, w_ref, w_sem)
+    fetch_w.start()
     if adjoint:
         first_ref, _, out_ref, *send_refs = rest[:8]
         f_ref, m_ref, turn_ref, b_ref = rest[8:]
@@ -308,14 +358,16 @@
     for ql in range(2):
         tiles = [s_ref[:, t * 8 : (t + 1) * 8, :].reshape(128, 128) for t in (2 * ql, 2 * ql + 1)]
         hi, lo = split(jnp.concatenate(tiles, axis=1))
-        rep = dot_tn(hi, dhi[ql]) + dot_tn(lo, dhi[ql]) + dot_tn(hi, dlo[ql])
+        top = xhi[ql]
+        rep = dot_tn(jnp.concatenate([hi, lo], axis=0), jnp.concatenate([top, top], axis=0)) + dot_tn(hi, xlo[ql])
         rep = rep[:KEPT_ROWS].reshape(PAIRS, 24, 512) * mask_ref[ql][None]
         hi, lo = split(rep.reshape(KEPT_ROWS, 512))
         halves.append(dot(g, hi) + dot(g, lo))
     for reim in range(2):
         a = halves[0][:, reim * 256 : (reim + 1) * 256]
         b = halves[1][:, reim * 256 : (reim + 1) * 256]
-        f_ref[reim] = jnp.concatenate([a[:, :128], a[:, 128:] + b[:, :128], b[:, 128:]], axis=1)
+        joined = jnp.concatenate([a[:, :128], a[:, 128:] + b[:, :128], b[:, 128:]], axis=1)
+        f_ref[reim] = joined * (1.0 / VOLUME) if adjoint else joined
     for reim in range(2):
         for t in range(3):
             turn_ref[t, pl.ds(reim, CP, stride=2), :] = f_ref[reim, :, t * 128 : (t + 1) * 128]
@@ -330,10 +382,11 @@
     if adjoint:
         me = lax.axis_index("sample")
         for d in range(SAMPLES):
-            send_refs[d][...] = b_ref[jnp.bitwise_xor(me, d)]
+            send_refs[d][...] = b_ref[jnp.bitwise_xor(me, NEAR[d % 4] + FAR * (d // 4))]
     else:
         store.start()
     m_ref[...] = jnp.zeros_like(m_ref)
+    fetch_w.wait()
     if adjoint:
         fr, fi = f_ref[0, :C, :288], f_ref[1, :C, :288]
         for c in range(C):
@@ -348,19 +401,22 @@
             fr, fi = f_ref[0, c : c + 1, :288], f_ref[1, c : c + 1, :288]
             mr = mr + (wr * fr - wi * fi)
             mi = mi + (wr * fi + wi * fr)
-        m_ref[0, :C, :288] = mr
-        m_ref[1, :C, :288] = mi
+        m_ref[0, :C, :288] = mr * (1.0 / VOLUME)
+        m_ref[1, :C, :288] = mi * (1.0 / VOLUME)
+    upper = lax.broadcasted_iota(jnp.int32, (24, 256), 0) < MY
     for ql in range(2):
         lanes = slice(ql * 128, ql * 128 + 256)
-        hi, lo = split(jnp.concatenate([m_ref[0, :, lanes], m_ref[1, :, lanes]], axis=1))
-        mask = mask_ref[ql][None]
-        spread = []
-        for part in (hi, lo):
-            rows = dot(gt_ref[...], part).reshape(PAIRS, 24, 512) * mask
-            rows = jnp.concatenate([rows.reshape(KEPT_ROWS, 512), jnp.zeros((256 - KEPT_ROWS, 512), F32)], axis=0)
-            spread.append(rows.astype(BF16))
-        hi, lo = spread
-        out = dot_nt(ihi[ql], hi) + dot_nt(ihi[ql], lo) + dot_nt(ilo[ql], hi)
+        mask = mask_ref[ql]
+        rows = []
+        for c in range(0, C, 2):
+            pair = []
+            for reim in range(2):
+                even, odd = m_ref[reim, c : c + 1, lanes], m_ref[reim, c + 1 : c + 2, lanes]
+                pair.append(jnp.where(upper, even, odd))
+            rows.append(jnp.concatenate(pair, axis=1) * mask)
+        rows.append(jnp.zeros((256 - KEPT_ROWS, 512), F32))
+        hi, lo = split(jnp.concatenate(rows, axis=0))
+        out = dot_nt(xhi[ql], hi) + dot_nt(xhi[ql], lo) + dot_nt(xlo[ql], hi)
         for half in range(2):
             t = 2 * ql + half
             out_ref[:, t * 8 : (t + 1) * 8, :] = out[:, half * 128 : (half + 1) * 128].reshape(OWNERS, 8, 128)
@@ -368,23 +424,6 @@
         store.wait()
 
 
-def weight_kernel(*refs):
-    own_ref, far_ref, near_refs, (out_ref, a_ref) = refs[0], refs[1], refs[2:5], refs[6:]
-    even = lax.broadcasted_iota(jnp.int32, (2 * C, 128), 0) % 2 == 0
-    terms = []
-    for s, ref in enumerate([own_ref, far_ref.at[0]] + [ref.at[k] for ref in near_refs for k in range(2)]):
-        block = ref[...]
-        a_ref[s] = block
-        b = pltpu.roll(block, 64, 1)
-        below, above = pltpu.roll(b, 2 * C - 1, 0), pltpu.roll(b, 1, 0)
-        terms.append((b, jnp.where(even, below, -above)))
-    for c in range(C):
-        total = jnp.zeros((2 * C, 128), F32)
-        for s, (b, swapped) in enumerate(terms):
-            total = total + (a_ref[s, 2 * c : 2 * c + 1, :] * b + a_ref[s, 2 * c + 1 : 2 * c + 2, :] * swapped)
-        out_ref[c * 2 * C : (c + 1) * 2 * C, :] = total[:, :BLOCK_MODES]
-
-
 def whole(shape):
     return pl.BlockSpec(shape, lambda *_: (0,) * len(shape))
 
@@ -408,13 +447,14 @@
 def shards(fields, cotangent, spectral_weight, point_weight, point_bias):
     yhi, ylo = hi_lo(y_table())
     zhi, zlo = hi_lo(plane_table())
-    ytab = jnp.asarray(np.concatenate([yhi, ylo], axis=0))
+    ytab = jnp.asarray(np.concatenate([yhi, ylo], axis=1))
     ztab = jnp.asarray(np.concatenate([zhi, zlo], axis=0))
-    ytab_t = jnp.asarray(np.concatenate([yhi.T, yhi.T, ylo.T], axis=1))
+    yhi_t, ylo_t = (np.swapaxes(t, 1, 2) for t in (yhi, ylo))
+    ytab_t = jnp.asarray(np.concatenate([yhi_t, yhi_t, ylo_t], axis=2))
     ztab_k = jnp.asarray(np.concatenate([zhi, zhi, zlo], axis=0))
     mask = jnp.asarray(mode_mask())
     g = jnp.asarray(group_table().astype(ml_dtypes.bfloat16))
-    gt = jnp.asarray(group_table().T.astype(ml_dtypes.bfloat16))
+    xhi, xlo = map(jnp.asarray, hi_lo(np.stack([x_table(ql) for ql in range(2)])))
     flat = (OWNERS * 32, 128)
     slab_out = jax.ShapeDtypeStruct(flat, F32)
     owned_out = jax.ShapeDtypeStruct((OWNERS, 32, 128), F32)
@@ -424,10 +464,6 @@
     planes = pltpu.VMEM((SLAB, 256, 256), F32)
 
     def owner(received, adjoint, *first):
-        scale = 1.0 / VOLUME
-        tabs = [x_tables(ql, scale if adjoint else 1.0, 1.0 if adjoint else scale) for ql in range(2)]
-        dhi, dlo = hi_lo(np.stack([t[0] for t in tabs]))
-        ihi, ilo = hi_lo(np.stack([t[1] for t in tabs]))
         weights = spectral_weight.reshape(2 * C, C, 288)
         if adjoint:
             spec_shapes = [(2 * C, 128)] * 4 + [(4, 2 * C, 128)]
@@ -435,17 +471,20 @@
             spec_shapes = [(SAMPLES, 2 * C, 128)]
         scratch = [pltpu.VMEM((2, CP, 384), F32), pltpu.VMEM((2, CP, 384), F32), pltpu.VMEM((3, 2 * CP, 128), F32)]
         scratch.append(pltpu.VMEM((SAMPLES, 2 * C, 128), F32))
+        operands = [received, weights, xhi, xlo, mask, g, *first]
+        in_specs = [pinned() if k == 1 else whole(o.shape) for k, o in enumerate(operands)]
         if not adjoint:
             scratch.append(pltpu.SemaphoreType.DMA)
         return pl.pallas_call(
             functools.partial(owner_kernel, adjoint),
             out_shape=[owned_out] + [jax.ShapeDtypeStruct(shape, F32) for shape in spec_shapes],
-            scratch_shapes=scratch,
+            in_specs=in_specs,
+            scratch_shapes=scratch + [pltpu.VMEM((2 * C, C, 288), BF16), pltpu.SemaphoreType.DMA],
             **({} if adjoint else {"out_specs": [whole(owned_out.shape), pinned()]}),
             compiler_params=params(52),
             cost_estimate=cost(3),
             name="owner_up" if adjoint else "owner_in",
-        )(received, weights, *map(jnp.asarray, (dhi, dlo, ihi, ilo)), mask, g, gt, *first)
+        )(*operands)
 
     def as_rows(array):
         return jnp.transpose(array.reshape(SLAB, C, NY, PLANE), (1, 2, 0, 3)).reshape(ROWS, PLANE)
@@ -484,8 +523,8 @@
         out_specs=[pinned(), pinned(), whole(flat)],
         out_shape=rows_out + [slab_out],
         scratch_shapes=[pltpu.VMEM((ROWS, 128), dtype) for dtype in (F32, BF16, BF16, F32)]
-        + [planes, planes, pltpu.VMEM((PAIR_ROWS, 256), F32)]
-        + [pltpu.VMEM((PAIR_ROWS, 256), BF16)] * 2
+        + [planes, planes, pltpu.VMEM((QUAD_ROWS, 128), F32)]
+        + [pltpu.VMEM((QUAD_ROWS, 128), BF16)] * 2
         + [sems((4 * STEPS,))],
         compiler_params=params(52),
         cost_estimate=cost(8),
@@ -493,6 +532,11 @@
     )(exchange(mixed).reshape(flat), local, as_rows(cotangent), ytab, ztab, ytab_t, ztab_k)
     local, token = point(upstream, False)
     back, *sends = owner(exchange(sent.reshape(OWNERS, 32, 128)), True, spec_in, token)
+    def swap(block, bits):
+        return lax.ppermute(block, "sample", [(s, s ^ bits) for s in range(SAMPLES)])
+
+    far = swap(sends[4], FAR)
+    near = [swap(jnp.stack([sends[k], far[k]]), NEAR[k]) for k in range(1, 4)]
     grad_input, done = pl.pallas_call(
         last_kernel,
         in_specs=[whole(flat), pinned()] + inverse_specs,
@@ -503,12 +547,6 @@
         cost_estimate=cost(20),
         name="slab_out",
     )(exchange(back).reshape(flat), local, ytab_t, ztab_k)
-
-    def swap(block, bits):
-        return lax.ppermute(block, "sample", [(s, s ^ bits) for s in range(SAMPLES)])
-
-    far = swap(sends[4], 4)
-    near = [swap(jnp.stack([sends[d], far[d]]), d) for d in range(1, 4)]
     grad_spectral = pl.pallas_call(
         weight_kernel,
         out_shape=jax.ShapeDtypeStruct((2 * C * C, BLOCK_MODES), F32),

time: 81.3 us -> 73 us (0.90)
  Pallas kernels: 29.7 us -> 22.7 us
  waiting for transfers between devices: 16.1 us -> 15.1 us
    pallas_call x1, Pallas kernels: 8.73 us -> 5.96 us  [shards(): pl.pallas_call(middle_kernel, in_specs=[whole(flat), pinned(), pinned()]...]
    pallas_call x2, Pallas kernels: 8.35 us -> 6.34 us  [owner(): pl.pallas_call(functools.partial(owner_kernel, adjoint), out_shape=[owned...]
    pallas_call x1, Pallas kernels: 4.15 us -> 2.86 us  [shards(): pl.pallas_call(last_kernel, in_specs=[whole(flat), pinned()] + inverse_sp...]
    all_to_all x4, waiting for transfers between devices: 16.1 us -> 15.1 us  [exchange(): lax.all_to_all(block, 'space', split_axis=0, concat_axis=0, tiled=True)]
    pallas_call x1, Pallas kernels: 4.2 us -> 3.3 us  [shards(): pl.pallas_call(forward_kernel, in_specs=[pinned()] * 3, out_shape=slab_ou...]
    unnamed x45 -> x31, local copies, waits for them, and re-layouts: 5.77 us -> 5.76 us
  transfers between devices with their start and end apart: 8 -> 8, of which waited for: 4 -> 4; matrix products, arithmetic and copies ran while one was open for 1% -> 1% of each run, Pallas kernels for 9% -> 8%
where the time goes in v3:
time: 73 us; the launch traced here: 72.4 us
  starting transfers between devices  27.9 us (38%)
  Pallas kernels  22.7 us (31%)
  waiting for transfers between devices  15.1 us (21%)
  local copies, waits for them, and re-layouts  5.77 us (8%)
  between operations  0.9 us (1%)
    all_to_all x4, starting transfers between devices, exchange(): lax.all_to_all(block, 'space', split_axis=0, concat_axis=0, tiled=True)  20.3 us
    all_to_all x4, waiting for transfers between devices, exchange(): lax.all_to_all(block, 'space', split_axis=0, concat_axis=0, tiled=True)  15.1 us
    ppermute x4, starting transfers between devices, swap(): lax.ppermute(block, 'sample', [(s, s ^ bits) for s in range(SAMPLES)])  7.56 us
    pallas_call x2, Pallas kernels, owner(): pl.pallas_call(functools.partial(owner_kernel, adjoint), out_shape=[owned...  6.34 us
    pallas_call x1, Pallas kernels, shards(): pl.pallas_call(middle_kernel, in_specs=[whole(flat), pinned(), pinned()]...  5.96 us
    unnamed x31, local copies, waits for them, and re-layouts  5.76 us
    pallas_call x1, Pallas kernels, shards(): pl.pallas_call(forward_kernel, in_specs=[pinned()] * 3, out_shape=slab_ou...  3.3 us
    pallas_call x1, Pallas kernels, shards(): pl.pallas_call(last_kernel, in_specs=[whole(flat), pinned()] + inverse_sp...  2.86 us
  transfers between devices with their start and end apart: 8, of which 4 were waited for; matrix products, arithmetic and copies ran while one was open for 1% of the time, Pallas kernels for 8%

profile of v3, /device:TPU:1, one launch (start us, length us, event | category | flops | bytes accessed | tf_op | source)
XLA Modules:
  0.0 72.4 jit_solution(8654049609990813689)
XLA Ops:
  0.6 3.3 %slab_in.1 = f32[512,128]{1,0:T(8,128)} custom-call(bf16[5120,128]{1,0:T(8,128)(2,1)} %bitcast.37, bf16[2,128,256]{2,1,0:T(8,128)(2,1)} %constant.16.clone.ytab_hbm.ytab, bf16[128,256]{1,0:T(8,128)(2,1)} %constant.17.clone.ztab_hbm.ztab), custom_call_target="tpu_custom_call" | custom-call | flops 1200000000 | bytes 9000000 | tf_op jit(solution)/shard_map/slab_in/pallas_call | solution.py:506
  4.0 0.0 copy-start.4
  4.0 0.0 copy-start.5
  4.0 0.0 copy-start.8
  4.0 0.0 copy-start.10
  4.0 7.1 %all-to-all-start = ((f32[16,32,128]{2,1,0:T(8,128)}), f32[16,32,128]{2,1,0:T(8,128)S(1)}, u32[]{:S(2)}, u32[]{:S(2)}) async-start(f32[16,32,128]{2,1,0:T(8,128)} %bitcast.42), calls=%async_computation | async-start | bytes 524288 | tf_op jit(solution)/shard_map/all_to_all | solution.py:444
  11.1 1.0 %copy.17 = bf16[2,20,20,288]{3,2,1,0:T(8,128)(2,1)} copy(bf16[2,20,20,288]{3,0,2,1:T(2,128)(2,1)S(1)} %copy-done.14) | data formatting | bytes 921600 | tf_op args[2]
  12.0 6.2 %all-to-all-done.s_ref = f32[16,32,128]{2,1,0:T(8,128)S(1)} async-done(((f32[16,32,128]{2,1,0:T(8,128)}), f32[16,32,128]{2,1,0:T(8,128)S(1)}, u32[]{:S(2)}, u32[]{:S(2)}) %all-to-all-start) | async-done | bytes 262176 | tf_op jit(solution)/shard_map/all_to_all | solution.py:444
  18.3 0.0 copy-start
  18.3 2.9 %owner_in.1 = (f32[16,32,128]{2,1,0:T(8,128)}, f32[8,40,128]{2,1,0:T(8,128)S(1)}) custom-call(f32[16,32,128]{2,1,0:T(8,128)S(1)} %all-to-all-done.s_ref, bf16[40,20,288]{2,1,0:T(8,128)(2,1)} %bitcast.40, bf16[2,128,512]{2,1,0:T(8,128)(2,1)S(1)} %copy-done.5, bf16[2,128,512]{2,1,0:T(8,128)(2,1)S(1)} %copy-done.4, f32[2,24,512]{2,1,0:T(8,128)S(1)} %copy-done.8, ...), custom_call_target="tpu_custom_call" | custom-call | flops 1200000000 | bytes 9000000 | tf_op jit(solution)/shard_map/owner_in/pallas_call | solution.py:478
  21.2 4.3 %all-to-all-start.1 = ((f32[16,32,128]{2,1,0:T(8,128)}), f32[16,32,128]{2,1,0:T(8,128)S(1)}, u32[]{:S(2)}, u32[]{:S(2)}) async-start(f32[16,32,128]{2,1,0:T(8,128)} %get-tuple-element.19), calls=%async_computation.1 | async-start | bytes 524288 | tf_op jit(solution)/shard_map/all_to_all | solution.py:444
  25.5 0.0 copy-start.3
  25.5 0.0 copy-start.6
  25.5 0.0 copy-start.7
  25.5 0.0 copy-start.9
  25.6 1.1 %point_in.1 = (f32[5120,128]{1,0:T(8,128)S(1)}, f32[8,128]{1,0:T(8,128)}) custom-call(bf16[5120,128]{1,0:T(8,128)(2,1)S(1)} %bitcast.38, bf16[20,20]{1,0:T(8,128)(2,1)S(1)} %copy-done.1, f32[1,20]{1,0:T(1,128)S(1)} %bitcast.39), custom_call_target="tpu_custom_call" | custom-call | flops 1600000000 | bytes 12000000 | tf_op jit(solution)/shard_map/point_in/pallas_call | solution.py:496
  26.7 1.5 %copy-done.13 = f32[5120,128]{1,0:T(8,128)} copy-done((f32[5120,128]{1,0:T(8,128)}, f32[5120,128]{1,0:T(8,128)S(1)}, u32[]{:S(2)}) %copy-start.13) | copy-done | bytes 2621464
  28.2 4.6 %all-to-all-done.1 = f32[16,32,128]{2,1,0:T(8,128)S(1)} async-done(((f32[16,32,128]{2,1,0:T(8,128)}), f32[16,32,128]{2,1,0:T(8,128)S(1)}, u32[]{:S(2)}, u32[]{:S(2)}) %all-to-all-start.1) | async-done | bytes 262176 | tf_op jit(solution)/shard_map/all_to_all | solution.py:444
  32.7 6.0 %slab_mid.1 = (bf16[5120,128]{1,0:T(8,128)(2,1)}, f32[5120,128]{1,0:T(8,128)}, f32[512,128]{1,0:T(8,128)}) custom-call(f32[512,128]{1,0:T(8,128)S(1)} %bitcast.33, f32[5120,128]{1,0:T(8,128)} %copy-done.13, bf16[5120,128]{1,0:T(8,128)(2,1)} %bitcast.43, bf16[2,128,256]{2,1,0:T(8,128)(2,1)S(1)} %copy-done.6, bf16[128,256]{1,0:T(8,128)(2,1)S(1)} %copy-done.9, ...), custom_call_target="tpu_custom_call" | custom-call | flops 3200000000 | bytes 24000000 | tf_op jit(solution)/shard_map/slab_mid/pallas_call | solution.py:520
  38.7 4.3 %all-to-all-start.2 = ((f32[16,32,128]{2,1,0:T(8,128)}), f32[16,32,128]{2,1,0:T(8,128)S(1)}, u32[]{:S(2)}, u32[]{:S(2)}) async-start(f32[16,32,128]{2,1,0:T(8,128)} %bitcast.15), calls=%async_computation.2 | async-start | bytes 524288 | tf_op jit(solution)/shard_map/all_to_all | solution.py:444
  43.0 1.7 %copy-done.12 = f32[5120,128]{1,0:T(8,128)S(1)} copy-done((f32[5120,128]{1,0:T(8,128)S(1)}, f32[5120,128]{1,0:T(8,128)}, u32[]{:S(2)}) %copy-start.12) | copy-done | bytes 2621464
  44.8 1.8 %point_up.1 = (f32[5120,128]{1,0:T(8,128)S(1)}, f32[8,128]{1,0:T(8,128)S(1)}) custom-call(f32[5120,128]{1,0:T(8,128)S(1)} %copy-done.12, bf16[20,20]{1,0:T(8,128)(2,1)S(1)} %copy-done.1), custom_call_target="tpu_custom_call" | custom-call | flops 1600000000 | bytes 12000000 | tf_op jit(solution)/shard_map/point_up/pallas_call | solution.py:496
  46.6 1.5 %copy-done.11 = f32[5120,128]{1,0:T(8,128)} copy-done((f32[5120,128]{1,0:T(8,128)}, f32[5120,128]{1,0:T(8,128)S(1)}, u32[]{:S(2)}) %copy-start.11) | copy-done | bytes 2621464
  48.0 2.2 %all-to-all-done.2.s_ref = f32[16,32,128]{2,1,0:T(8,128)S(1)} async-done(((f32[16,32,128]{2,1,0:T(8,128)}), f32[16,32,128]{2,1,0:T(8,128)S(1)}, u32[]{:S(2)}, u32[]{:S(2)}) %all-to-all-start.2) | async-done | bytes 262176 | tf_op jit(solution)/shard_map/all_to_all | solution.py:444
  50.3 3.5 %owner_up.1 = (f32[16,32,128]{2,1,0:T(8,128)}, f32[40,128]{1,0:T(8,128)S(1)}, f32[40,128]{1,0:T(8,128)S(1)}, f32[40,128]{1,0:T(8,128)S(1)}, f32[40,128]{1,0:T(8,128)S(1)}, /*index=5*/f32[4,40,128]{2,1,0:T(8,128)S(1)}) custom-call(f32[16,32,128]{2,1,0:T(8,128)S(1)} %all-to-all-done.2.s_ref, bf16[40,20,288]{2,1,0:T(8,128)(2,1)} %bitcast.41, ...), custom_call_target="tpu_custom_call" | custom-call | flops 1200000000 | bytes 9000000 | tf_op jit(solution)/shard_map/owner_up/pallas_call | solution.py:478
  53.7 2.5 %collective-permute-start = (f32[4,40,128]{2,1,0:T(8,128)S(1)}, f32[4,40,128]{2,1,0:T(8,128)S(1)}, u32[]{:S(2)}, u32[]{:S(2)}) collective-permute-start(f32[4,40,128]{2,1,0:T(8,128)S(1)} %get-tuple-element.30), channel_id=1, source_target_pairs={{0,1},{1,0},{2,3},{3,2},{4,5},{5,4},{6,7},{7,6},{8,9},{9,8},{10,11... | collective-permute-start | bytes 245768 | tf_op jit(solution)/shard_map/ppermute | solution.py:536
  56.3 4.6 %all-to-all-start.3 = ((f32[16,32,128]{2,1,0:T(8,128)}), f32[16,32,128]{2,1,0:T(8,128)S(1)}, u32[]{:S(2)}, u32[]{:S(2)}) async-start(f32[16,32,128]{2,1,0:T(8,128)} %get-tuple-element.26), calls=%async_computation.3 | async-start | bytes 524288 | tf_op jit(solution)/shard_map/all_to_all | solution.py:444
  60.9 1.7 %collective-permute-start.1 = (f32[2,40,128]{2,1,0:T(8,128)S(1)}, f32[2,40,128]{2,1,0:T(8,128)S(1)}, u32[]{:S(2)}, u32[]{:S(2)}) collective-permute-start(f32[2,40,128]{2,1,0:T(8,128)S(1)} %pad_maximum_fusion), channel_id=1, source_target_pairs={{0,2},{1,3},{2,0},{3,1},{4,6},{5,7},{6,4},{7,5},{8,10},{9,11},{10,... | collective-permute-start | bytes 122888 | tf_op jit(solution)/shard_map/ppermute | solution.py:536
  62.6 3.3 %collective-permute-start.2 = (f32[2,40,128]{2,1,0:T(8,128)S(1)}, f32[2,40,128]{2,1,0:T(8,128)S(1)}, u32[]{:S(2)}, u32[]{:S(2)}) collective-permute-start(f32[2,40,128]{2,1,0:T(8,128)S(1)} %pad_maximum_fusion.1), channel_id=1, source_target_pairs={{0,4},{1,5},{2,6},{3,7},{4,0},{5,1},{6,2},{7,3},{8,12},{9,13},{10,... | collective-permute-start | bytes 122888 | tf_op jit(solution)/shard_map/ppermute | solution.py:536
  66.0 2.1 %all-to-all-done.3 = f32[16,32,128]{2,1,0:T(8,128)S(1)} async-done(((f32[16,32,128]{2,1,0:T(8,128)}), f32[16,32,128]{2,1,0:T(8,128)S(1)}, u32[]{:S(2)}, u32[]{:S(2)}) %all-to-all-start.3) | async-done | bytes 262176 | tf_op jit(solution)/shard_map/all_to_all | solution.py:444
  68.1 2.9 %slab_out.1 = (bf16[5120,128]{1,0:T(8,128)(2,1)}, f32[8,128]{1,0:T(8,128)S(1)}) custom-call(f32[512,128]{1,0:T(8,128)S(1)} %bitcast.32, f32[5120,128]{1,0:T(8,128)} %copy-done.11, bf16[2,256,192]{2,1,0:T(8,128)(2,1)S(1)} %copy-done.3, bf16[192,256]{1,0:T(8,128)(2,1)S(1)} %copy-done.7), custom_call_target="tpu_custom_call" | custom-call | flops 8000000000 | bytes 60000000 | tf_op jit(solution)/shard_map/slab_out/pallas_call | solution.py:540
  71.0 1.4 %weight_grad.1 = f32[800,36]{1,0:T(8,128)} custom-call(f32[40,128]{1,0:T(8,128)S(1)} %get-tuple-element.29.own_ref, f32[4,40,128]{2,1,0:T(8,128)S(1)} %collective-permute-done.far_ref, f32[2,40,128]{2,1,0:T(8,128)S(1)} %collective-permute-done.1.near1_ref, f32[2,40,128]{2,1,0:T(8,128)S(1)} %collective-permute-done.2.near2_ref, ...), custom_call_target="tpu_custom_call" | custom-call | flops 400000000 | bytes 3000000 | tf_op jit(solution)/shard_map/weight_grad/pallas_call | solution.py:550
  (27 shorter events, 0.1 us)
Async XLA Ops:
  0.6 10.4 %copy-start.14 = (bf16[2,20,20,288]{3,0,2,1:T(2,128)(2,1)S(1)}, bf16[2,20,20,288]{3,0,2,1:T(2,128)(2,1)}, u32[]{:S(2)}) copy-start(bf16[2,20,20,288]{3,0,2,1:T(2,128)(2,1)} %param.15) | copy-start | bytes 1382404
  4.0 14.3 %copy-start.4 = (bf16[2,128,512]{2,1,0:T(8,128)(2,1)S(1)}, bf16[2,128,512]{2,1,0:T(8,128)(2,1)}, u32[]{:S(2)}) copy-start(bf16[2,128,512]{2,1,0:T(8,128)(2,1)} %constant.23.clone.xlo) | copy-start | bytes 786436
  4.0 14.3 %copy-start.5 = (bf16[2,128,512]{2,1,0:T(8,128)(2,1)S(1)}, bf16[2,128,512]{2,1,0:T(8,128)(2,1)}, u32[]{:S(2)}) copy-start(bf16[2,128,512]{2,1,0:T(8,128)(2,1)} %constant.22.clone.xhi) | copy-start | bytes 786436
  4.0 14.3 %copy-start.8 = (f32[2,24,512]{2,1,0:T(8,128)S(1)}, f32[2,24,512]{2,1,0:T(8,128)}, u32[]{:S(2)}) copy-start(f32[2,24,512]{2,1,0:T(8,128)} %constant.20.clone.mask_ref) | copy-start | bytes 294916
  4.0 14.3 %copy-start.10 = (bf16[24,240]{1,0:T(8,128)(2,1)S(1)}, bf16[24,240]{1,0:T(8,128)(2,1)}, u32[]{:S(2)}) copy-start(bf16[24,240]{1,0:T(8,128)(2,1)} %constant.21.clone.g_ref) | copy-start | bytes 34564
  4.0 14.2 %all-to-all-start = ((f32[16,32,128]{2,1,0:T(8,128)}), f32[16,32,128]{2,1,0:T(8,128)S(1)}, u32[]{:S(2)}, u32[]{:S(2)}) async-start(f32[16,32,128]{2,1,0:T(8,128)} %bitcast.42), calls=%async_computation | async-start | bytes 524288 | tf_op jit(solution)/shard_map/all_to_all | solution.py:444
  18.3 7.2 %copy-start = (bf16[1,4,20,8192]{3,1,2,0:T(4,128)(2,1)S(1)}, bf16[1,4,20,8192]{3,1,2,0:T(4,128)(2,1)}, u32[]{:S(2)}) copy-start(bf16[1,4,20,8192]{3,1,2,0:T(4,128)(2,1)} %param.13) | copy-start | bytes 3932164
  18.3 7.2 %copy-start.1 = (bf16[20,20]{1,0:T(8,128)(2,1)S(1)}, bf16[20,20]{1,0:T(8,128)(2,1)}, u32[]{:S(2)}) copy-start(bf16[20,20]{1,0:T(8,128)(2,1)} %w_ref.3) | copy-start | bytes 2404
  18.3 7.2 %copy-start.2 = (f32[20]{0:T(128)S(1)}, f32[20]{0:T(128)}, u32[]{:S(2)}) copy-start(f32[20]{0:T(128)} %param.17) | copy-start | bytes 244
  21.2 11.5 %all-to-all-start.1 = ((f32[16,32,128]{2,1,0:T(8,128)}), f32[16,32,128]{2,1,0:T(8,128)S(1)}, u32[]{:S(2)}, u32[]{:S(2)}) async-start(f32[16,32,128]{2,1,0:T(8,128)} %get-tuple-element.19), calls=%async_computation.1 | async-start | bytes 524288 | tf_op jit(solution)/shard_map/all_to_all | solution.py:444
  25.5 7.2 %copy-start.3 = (bf16[2,256,192]{2,1,0:T(8,128)(2,1)S(1)}, bf16[2,256,192]{2,1,0:T(8,128)(2,1)}, u32[]{:S(2)}) copy-start(bf16[2,256,192]{2,1,0:T(8,128)(2,1)} %constant.18.clone.ytab_t) | copy-start | bytes 589828
  25.5 7.2 %copy-start.6 = (bf16[2,128,256]{2,1,0:T(8,128)(2,1)S(1)}, bf16[2,128,256]{2,1,0:T(8,128)(2,1)}, u32[]{:S(2)}) copy-start(bf16[2,128,256]{2,1,0:T(8,128)(2,1)} %constant.16.clone.ytab_hbm.ytab) | copy-start | bytes 393220
  25.5 7.2 %copy-start.7 = (bf16[192,256]{1,0:T(8,128)(2,1)S(1)}, bf16[192,256]{1,0:T(8,128)(2,1)}, u32[]{:S(2)}) copy-start(bf16[192,256]{1,0:T(8,128)(2,1)} %constant.19.clone.ztab_k) | copy-start | bytes 294916
  25.5 7.2 %copy-start.9 = (bf16[128,256]{1,0:T(8,128)(2,1)S(1)}, bf16[128,256]{1,0:T(8,128)(2,1)}, u32[]{:S(2)}) copy-start(bf16[128,256]{1,0:T(8,128)(2,1)} %constant.17.clone.ztab_hbm.ztab) | copy-start | bytes 196612
  26.7 1.5 %copy-start.13 = (f32[5120,128]{1,0:T(8,128)}, f32[5120,128]{1,0:T(8,128)S(1)}, u32[]{:S(2)}) copy-start(f32[5120,128]{1,0:T(8,128)S(1)} %get-tuple-element.20.local_hbm) | copy-start | bytes 7864324
  38.7 11.6 %all-to-all-start.2 = ((f32[16,32,128]{2,1,0:T(8,128)}), f32[16,32,128]{2,1,0:T(8,128)S(1)}, u32[]{:S(2)}, u32[]{:S(2)}) async-start(f32[16,32,128]{2,1,0:T(8,128)} %bitcast.15), calls=%async_computation.2 | async-start | bytes 524288 | tf_op jit(solution)/shard_map/all_to_all | solution.py:444
  43.0 1.7 %copy-start.12 = (f32[5120,128]{1,0:T(8,128)S(1)}, f32[5120,128]{1,0:T(8,128)}, u32[]{:S(2)}) copy-start(f32[5120,128]{1,0:T(8,128)} %get-tuple-element.24.x_ref) | copy-start | bytes 7864324
  46.5 1.5 %copy-start.11 = (f32[5120,128]{1,0:T(8,128)}, f32[5120,128]{1,0:T(8,128)S(1)}, u32[]{:S(2)}) copy-start(f32[5120,128]{1,0:T(8,128)S(1)} %get-tuple-element.27.local_hbm) | copy-start | bytes 7864324
  53.7 7.1 %collective-permute-start = (f32[4,40,128]{2,1,0:T(8,128)S(1)}, f32[4,40,128]{2,1,0:T(8,128)S(1)}, u32[]{:S(2)}, u32[]{:S(2)}) collective-permute-start(f32[4,40,128]{2,1,0:T(8,128)S(1)} %get-tuple-element.30), channel_id=1, source_target_pairs={{0,1},{1,0},{2,3},{3,2},{4,5},{5,4},{6,7},{7,6},{8,9},{9,8},{10,11... | collective-permute-start | bytes 245768 | tf_op jit(solution)/shard_map/ppermute | solution.py:536
  56.3 11.8 %all-to-all-start.3 = ((f32[16,32,128]{2,1,0:T(8,128)}), f32[16,32,128]{2,1,0:T(8,128)S(1)}, u32[]{:S(2)}, u32[]{:S(2)}) async-start(f32[16,32,128]{2,1,0:T(8,128)} %get-tuple-element.26), calls=%async_computation.3 | async-start | bytes 524288 | tf_op jit(solution)/shard_map/all_to_all | solution.py:444
  60.9 10.1 %collective-permute-start.1 = (f32[2,40,128]{2,1,0:T(8,128)S(1)}, f32[2,40,128]{2,1,0:T(8,128)S(1)}, u32[]{:S(2)}, u32[]{:S(2)}) collective-permute-start(f32[2,40,128]{2,1,0:T(8,128)S(1)} %pad_maximum_fusion), channel_id=1, source_target_pairs={{0,2},{1,3},{2,0},{3,1},{4,6},{5,7},{6,4},{7,5},{8,10},{9,11},{10,... | collective-permute-start | bytes 122888 | tf_op jit(solution)/shard_map/ppermute | solution.py:536
  62.6 8.3 %collective-permute-start.2 = (f32[2,40,128]{2,1,0:T(8,128)S(1)}, f32[2,40,128]{2,1,0:T(8,128)S(1)}, u32[]{:S(2)}, u32[]{:S(2)}) collective-permute-start(f32[2,40,128]{2,1,0:T(8,128)S(1)} %pad_maximum_fusion.1), channel_id=1, source_target_pairs={{0,4},{1,5},{2,6},{3,7},{4,0},{5,1},{6,2},{7,3},{8,12},{9,13},{10,... | collective-permute-start | bytes 122888 | tf_op jit(solution)/shard_map/ppermute | solution.py:536
  66.0 5.0 %collective-permute-start.3 = (f32[2,40,128]{2,1,0:T(8,128)S(1)}, f32[2,40,128]{2,1,0:T(8,128)S(1)}, u32[]{:S(2)}, u32[]{:S(2)}) collective-permute-start(f32[2,40,128]{2,1,0:T(8,128)S(1)} %pad_maximum_fusion.2), channel_id=1, source_target_pairs={{0,6},{1,7},{2,4},{3,5},{4,2},{5,3},{6,0},{7,1},{8,14},{9,15},{10,... | collective-permute-start | bytes 122888 | tf_op jit(solution)/shard_map/ppermute | solution.py:536

commit v4 on v3

--- a/solution.py
+++ b/solution.py
@@ -343,15 +343,15 @@
 
 
 def owner_kernel(adjoint, s_ref, w_hbm, xhi, xlo, mask_ref, g_ref, *rest):
-    *rest, w_ref, w_sem = rest
+    *rest, w_ref, w_sem, out_ref, out_sems = rest
     fetch_w = pltpu.make_async_copy(w_hbm, w_ref, w_sem)
     fetch_w.start()
     if adjoint:
-        first_ref, _, out_ref, *send_refs = rest[:8]
+        first_ref, _, out_hbm, *send_refs = rest[:8]
         f_ref, m_ref, turn_ref, b_ref = rest[8:]
         send_refs = send_refs[:4] + [send_refs[4].at[k] for k in range(4)]
     else:
-        out_ref, spec_hbm, f_ref, m_ref, turn_ref, spec_ref, sem = rest
+        out_hbm, spec_hbm, f_ref, m_ref, turn_ref, spec_ref, sem = rest
         store = pltpu.make_async_copy(spec_ref, spec_hbm, sem)
     g = g_ref[...]
     halves = []
@@ -403,6 +403,7 @@
             mi = mi + (wr * fi + wi * fr)
         m_ref[0, :C, :288] = mr * (1.0 / VOLUME)
         m_ref[1, :C, :288] = mi * (1.0 / VOLUME)
+    sent = []
     upper = lax.broadcasted_iota(jnp.int32, (24, 256), 0) < MY
     for ql in range(2):
         lanes = slice(ql * 128, ql * 128 + 256)
@@ -416,10 +417,16 @@
             rows.append(jnp.concatenate(pair, axis=1) * mask)
         rows.append(jnp.zeros((256 - KEPT_ROWS, 512), F32))
         hi, lo = split(jnp.concatenate(rows, axis=0))
-        out = dot_nt(xhi[ql], hi) + dot_nt(xhi[ql], lo) + dot_nt(xlo[ql], hi)
+        both = dot_nt(jnp.concatenate([xhi[ql], xlo[ql]], axis=0), hi)
+        out = both[:128] + both[128:] + dot_nt(xhi[ql], lo)
         for half in range(2):
             t = 2 * ql + half
             out_ref[:, t * 8 : (t + 1) * 8, :] = out[:, half * 128 : (half + 1) * 128].reshape(OWNERS, 8, 128)
+        part = (slice(None), pl.ds(ql * 16, 16), slice(None))
+        sent.append(pltpu.make_async_copy(out_ref.at[part], out_hbm.at[part], out_sems.at[ql]))
+        sent[ql].start()
+    for copy in sent:
+        copy.wait()
     if not adjoint:
         store.wait()
 
@@ -479,8 +486,10 @@
             functools.partial(owner_kernel, adjoint),
             out_shape=[owned_out] + [jax.ShapeDtypeStruct(shape, F32) for shape in spec_shapes],
             in_specs=in_specs,
-            scratch_shapes=scratch + [pltpu.VMEM((2 * C, C, 288), BF16), pltpu.SemaphoreType.DMA],
-            **({} if adjoint else {"out_specs": [whole(owned_out.shape), pinned()]}),
+            scratch_shapes=scratch
+            + [pltpu.VMEM((2 * C, C, 288), BF16), pltpu.SemaphoreType.DMA]
+            + [pltpu.VMEM(owned_out.shape, F32), pltpu.SemaphoreType.DMA((2,))],
+            out_specs=[pinned()] + (list(map(whole, spec_shapes)) if adjoint else [pinned()]),
             compiler_params=params(52),
             cost_estimate=cost(3),
             name="owner_up" if adjoint else "owner_in",

time: 73 us -> 72.6 us (level)
  no operation moved by 1% of the time
where the time goes in v4:
time: 72.6 us; the launch traced here: 72 us
  starting transfers between devices  27.9 us (38%)
  Pallas kernels  22.3 us (31%)
  waiting for transfers between devices  15.1 us (21%)
  local copies, waits for them, and re-layouts  5.77 us (8%)
  between operations  0.9 us (1%)
    all_to_all x4, starting transfers between devices, exchange(): lax.all_to_all(block, 'space', split_axis=0, concat_axis=0, tiled=True)  20.3 us
    all_to_all x4, waiting for transfers between devices, exchange(): lax.all_to_all(block, 'space', split_axis=0, concat_axis=0, tiled=True)  15.1 us
    ppermute x4, starting transfers between devices, swap(): lax.ppermute(block, 'sample', [(s, s ^ bits) for s in range(SAMPLES)])  7.55 us
    pallas_call x2, Pallas kernels, owner(): pl.pallas_call(functools.partial(owner_kernel, adjoint), out_shape=[owned...  5.99 us
    pallas_call x1, Pallas kernels, shards(): pl.pallas_call(middle_kernel, in_specs=[whole(flat), pinned(), pinned()]...  5.96 us
    unnamed x31, local copies, waits for them, and re-layouts  5.76 us
    pallas_call x1, Pallas kernels, shards(): pl.pallas_call(forward_kernel, in_specs=[pinned()] * 3, out_shape=slab_ou...  3.3 us
    pallas_call x1, Pallas kernels, shards(): pl.pallas_call(last_kernel, in_specs=[whole(flat), pinned()] + inverse_sp...  2.86 us
  transfers between devices with their start and end apart: 8, of which 4 were waited for; matrix products, arithmetic and copies ran while one was open for 1% of the time, Pallas kernels for 8%

profile of v4, /device:TPU:1, one launch (start us, length us, event | category | flops | bytes accessed | tf_op | source)
XLA Modules:
  0.0 72.0 jit_solution(13691041531078262487)
XLA Ops:
  0.6 3.3 %slab_in.1 = f32[512,128]{1,0:T(8,128)} custom-call(bf16[5120,128]{1,0:T(8,128)(2,1)} %bitcast.37, bf16[2,128,256]{2,1,0:T(8,128)(2,1)} %constant.16.clone.ytab_hbm.ytab, bf16[128,256]{1,0:T(8,128)(2,1)} %constant.17.clone.ztab_hbm.ztab), custom_call_target="tpu_custom_call" | custom-call | flops 1200000000 | bytes 9000000 | tf_op jit(solution)/shard_map/slab_in/pallas_call | solution.py:515
  4.0 0.0 copy-start.4
  4.0 0.0 copy-start.5
  4.0 0.0 copy-start.8
  4.0 0.0 copy-start.10
  4.0 7.1 %all-to-all-start = ((f32[16,32,128]{2,1,0:T(8,128)}), f32[16,32,128]{2,1,0:T(8,128)S(1)}, u32[]{:S(2)}, u32[]{:S(2)}) async-start(f32[16,32,128]{2,1,0:T(8,128)} %bitcast.42), calls=%async_computation | async-start | bytes 524288 | tf_op jit(solution)/shard_map/all_to_all | solution.py:451
  11.1 1.0 %copy.17 = bf16[2,20,20,288]{3,2,1,0:T(8,128)(2,1)} copy(bf16[2,20,20,288]{3,0,2,1:T(2,128)(2,1)S(1)} %copy-done.14) | data formatting | bytes 921600 | tf_op args[2]
  12.0 6.2 %all-to-all-done.s_ref = f32[16,32,128]{2,1,0:T(8,128)S(1)} async-done(((f32[16,32,128]{2,1,0:T(8,128)}), f32[16,32,128]{2,1,0:T(8,128)S(1)}, u32[]{:S(2)}, u32[]{:S(2)}) %all-to-all-start) | async-done | bytes 262176 | tf_op jit(solution)/shard_map/all_to_all | solution.py:451
  18.3 0.0 copy-start
  18.3 2.7 %owner_in.1 = (f32[16,32,128]{2,1,0:T(8,128)}, f32[8,40,128]{2,1,0:T(8,128)S(1)}) custom-call(f32[16,32,128]{2,1,0:T(8,128)S(1)} %all-to-all-done.s_ref, bf16[40,20,288]{2,1,0:T(8,128)(2,1)} %bitcast.40, bf16[2,128,512]{2,1,0:T(8,128)(2,1)S(1)} %copy-done.5, bf16[2,128,512]{2,1,0:T(8,128)(2,1)S(1)} %copy-done.4, f32[2,24,512]{2,1,0:T(8,128)S(1)} %copy-done.8, ...), custom_call_target="tpu_custom_call" | custom-call | flops 1200000000 | bytes 9000000 | tf_op jit(solution)/shard_map/owner_in/pallas_call | solution.py:485
  21.0 4.3 %all-to-all-start.1 = ((f32[16,32,128]{2,1,0:T(8,128)}), f32[16,32,128]{2,1,0:T(8,128)S(1)}, u32[]{:S(2)}, u32[]{:S(2)}) async-start(f32[16,32,128]{2,1,0:T(8,128)} %get-tuple-element.19), calls=%async_computation.1 | async-start | bytes 524288 | tf_op jit(solution)/shard_map/all_to_all | solution.py:451
  25.3 0.0 copy-start.3
  25.3 0.0 copy-start.6
  25.3 0.0 copy-start.7
  25.3 0.0 copy-start.9
  25.4 1.1 %point_in.1 = (f32[5120,128]{1,0:T(8,128)S(1)}, f32[8,128]{1,0:T(8,128)}) custom-call(bf16[5120,128]{1,0:T(8,128)(2,1)S(1)} %bitcast.38, bf16[20,20]{1,0:T(8,128)(2,1)S(1)} %copy-done.1, f32[1,20]{1,0:T(1,128)S(1)} %bitcast.39), custom_call_target="tpu_custom_call" | custom-call | flops 1600000000 | bytes 12000000 | tf_op jit(solution)/shard_map/point_in/pallas_call | solution.py:505
  26.5 1.5 %copy-done.13 = f32[5120,128]{1,0:T(8,128)} copy-done((f32[5120,128]{1,0:T(8,128)}, f32[5120,128]{1,0:T(8,128)S(1)}, u32[]{:S(2)}) %copy-start.13) | copy-done | bytes 2621464
  28.0 4.6 %all-to-all-done.1 = f32[16,32,128]{2,1,0:T(8,128)S(1)} async-done(((f32[16,32,128]{2,1,0:T(8,128)}), f32[16,32,128]{2,1,0:T(8,128)S(1)}, u32[]{:S(2)}, u32[]{:S(2)}) %all-to-all-start.1) | async-done | bytes 262176 | tf_op jit(solution)/shard_map/all_to_all | solution.py:451
  32.5 6.0 %slab_mid.1 = (bf16[5120,128]{1,0:T(8,128)(2,1)}, f32[5120,128]{1,0:T(8,128)}, f32[512,128]{1,0:T(8,128)}) custom-call(f32[512,128]{1,0:T(8,128)S(1)} %bitcast.33, f32[5120,128]{1,0:T(8,128)} %copy-done.13, bf16[5120,128]{1,0:T(8,128)(2,1)} %bitcast.43, bf16[2,128,256]{2,1,0:T(8,128)(2,1)S(1)} %copy-done.6, bf16[128,256]{1,0:T(8,128)(2,1)S(1)} %copy-done.9, ...), custom_call_target="tpu_custom_call" | custom-call | flops 3200000000 | bytes 24000000 | tf_op jit(solution)/shard_map/slab_mid/pallas_call | solution.py:529
  38.5 4.3 %all-to-all-start.2 = ((f32[16,32,128]{2,1,0:T(8,128)}), f32[16,32,128]{2,1,0:T(8,128)S(1)}, u32[]{:S(2)}, u32[]{:S(2)}) async-start(f32[16,32,128]{2,1,0:T(8,128)} %bitcast.15), calls=%async_computation.2 | async-start | bytes 524288 | tf_op jit(solution)/shard_map/all_to_all | solution.py:451
  42.8 1.7 %copy-done.12 = f32[5120,128]{1,0:T(8,128)S(1)} copy-done((f32[5120,128]{1,0:T(8,128)S(1)}, f32[5120,128]{1,0:T(8,128)}, u32[]{:S(2)}) %copy-start.12) | copy-done | bytes 2621464
  44.6 1.8 %point_up.1 = (f32[5120,128]{1,0:T(8,128)S(1)}, f32[8,128]{1,0:T(8,128)S(1)}) custom-call(f32[5120,128]{1,0:T(8,128)S(1)} %copy-done.12, bf16[20,20]{1,0:T(8,128)(2,1)S(1)} %copy-done.1), custom_call_target="tpu_custom_call" | custom-call | flops 1600000000 | bytes 12000000 | tf_op jit(solution)/shard_map/point_up/pallas_call | solution.py:505
  46.4 1.5 %copy-done.11 = f32[5120,128]{1,0:T(8,128)} copy-done((f32[5120,128]{1,0:T(8,128)}, f32[5120,128]{1,0:T(8,128)S(1)}, u32[]{:S(2)}) %copy-start.11) | copy-done | bytes 2621464
  47.9 2.2 %all-to-all-done.2.s_ref = f32[16,32,128]{2,1,0:T(8,128)S(1)} async-done(((f32[16,32,128]{2,1,0:T(8,128)}), f32[16,32,128]{2,1,0:T(8,128)S(1)}, u32[]{:S(2)}, u32[]{:S(2)}) %all-to-all-start.2) | async-done | bytes 262176 | tf_op jit(solution)/shard_map/all_to_all | solution.py:451
  50.1 3.3 %owner_up.1 = (f32[16,32,128]{2,1,0:T(8,128)}, f32[40,128]{1,0:T(8,128)S(1)}, f32[40,128]{1,0:T(8,128)S(1)}, f32[40,128]{1,0:T(8,128)S(1)}, f32[40,128]{1,0:T(8,128)S(1)}, /*index=5*/f32[4,40,128]{2,1,0:T(8,128)S(1)}) custom-call(f32[16,32,128]{2,1,0:T(8,128)S(1)} %all-to-all-done.2.s_ref, bf16[40,20,288]{2,1,0:T(8,128)(2,1)} %bitcast.41, ...), custom_call_target="tpu_custom_call" | custom-call | flops 1200000000 | bytes 9000000 | tf_op jit(solution)/shard_map/owner_up/pallas_call | solution.py:485
  53.4 2.5 %collective-permute-start = (f32[4,40,128]{2,1,0:T(8,128)S(1)}, f32[4,40,128]{2,1,0:T(8,128)S(1)}, u32[]{:S(2)}, u32[]{:S(2)}) collective-permute-start(f32[4,40,128]{2,1,0:T(8,128)S(1)} %get-tuple-element.30), channel_id=1, source_target_pairs={{0,1},{1,0},{2,3},{3,2},{4,5},{5,4},{6,7},{7,6},{8,9},{9,8},{10,11... | collective-permute-start | bytes 245768 | tf_op jit(solution)/shard_map/ppermute | solution.py:545
  55.9 4.6 %all-to-all-start.3 = ((f32[16,32,128]{2,1,0:T(8,128)}), f32[16,32,128]{2,1,0:T(8,128)S(1)}, u32[]{:S(2)}, u32[]{:S(2)}) async-start(f32[16,32,128]{2,1,0:T(8,128)} %get-tuple-element.26), calls=%async_computation.3 | async-start | bytes 524288 | tf_op jit(solution)/shard_map/all_to_all | solution.py:451
  60.6 1.7 %collective-permute-start.1 = (f32[2,40,128]{2,1,0:T(8,128)S(1)}, f32[2,40,128]{2,1,0:T(8,128)S(1)}, u32[]{:S(2)}, u32[]{:S(2)}) collective-permute-start(f32[2,40,128]{2,1,0:T(8,128)S(1)} %pad_maximum_fusion), channel_id=1, source_target_pairs={{0,2},{1,3},{2,0},{3,1},{4,6},{5,7},{6,4},{7,5},{8,10},{9,11},{10,... | collective-permute-start | bytes 122888 | tf_op jit(solution)/shard_map/ppermute | solution.py:545
  62.3 3.3 %collective-permute-start.2 = (f32[2,40,128]{2,1,0:T(8,128)S(1)}, f32[2,40,128]{2,1,0:T(8,128)S(1)}, u32[]{:S(2)}, u32[]{:S(2)}) collective-permute-start(f32[2,40,128]{2,1,0:T(8,128)S(1)} %pad_maximum_fusion.1), channel_id=1, source_target_pairs={{0,4},{1,5},{2,6},{3,7},{4,0},{5,1},{6,2},{7,3},{8,12},{9,13},{10,... | collective-permute-start | bytes 122888 | tf_op jit(solution)/shard_map/ppermute | solution.py:545
  65.6 2.2 %all-to-all-done.3 = f32[16,32,128]{2,1,0:T(8,128)S(1)} async-done(((f32[16,32,128]{2,1,0:T(8,128)}), f32[16,32,128]{2,1,0:T(8,128)S(1)}, u32[]{:S(2)}, u32[]{:S(2)}) %all-to-all-start.3) | async-done | bytes 262176 | tf_op jit(solution)/shard_map/all_to_all | solution.py:451
  67.8 2.9 %slab_out.1 = (bf16[5120,128]{1,0:T(8,128)(2,1)}, f32[8,128]{1,0:T(8,128)S(1)}) custom-call(f32[512,128]{1,0:T(8,128)S(1)} %bitcast.32, f32[5120,128]{1,0:T(8,128)} %copy-done.11, bf16[2,256,192]{2,1,0:T(8,128)(2,1)S(1)} %copy-done.3, bf16[192,256]{1,0:T(8,128)(2,1)S(1)} %copy-done.7), custom_call_target="tpu_custom_call" | custom-call | flops 8000000000 | bytes 60000000 | tf_op jit(solution)/shard_map/slab_out/pallas_call | solution.py:549
  70.7 1.4 %weight_grad.1 = f32[800,36]{1,0:T(8,128)} custom-call(f32[40,128]{1,0:T(8,128)S(1)} %get-tuple-element.29.own_ref, f32[4,40,128]{2,1,0:T(8,128)S(1)} %collective-permute-done.far_ref, f32[2,40,128]{2,1,0:T(8,128)S(1)} %collective-permute-done.1.near1_ref, f32[2,40,128]{2,1,0:T(8,128)S(1)} %collective-permute-done.2.near2_ref, ...), custom_call_target="tpu_custom_call" | custom-call | flops 400000000 | bytes 3000000 | tf_op jit(solution)/shard_map/weight_grad/pallas_call | solution.py:559
  (27 shorter events, 0.1 us)
Async XLA Ops:
  0.6 10.4 %copy-start.14 = (bf16[2,20,20,288]{3,0,2,1:T(2,128)(2,1)S(1)}, bf16[2,20,20,288]{3,0,2,1:T(2,128)(2,1)}, u32[]{:S(2)}) copy-start(bf16[2,20,20,288]{3,0,2,1:T(2,128)(2,1)} %param.15) | copy-start | bytes 1382404
  4.0 14.3 %copy-start.4 = (bf16[2,128,512]{2,1,0:T(8,128)(2,1)S(1)}, bf16[2,128,512]{2,1,0:T(8,128)(2,1)}, u32[]{:S(2)}) copy-start(bf16[2,128,512]{2,1,0:T(8,128)(2,1)} %constant.23.clone.xlo) | copy-start | bytes 786436
  4.0 14.3 %copy-start.5 = (bf16[2,128,512]{2,1,0:T(8,128)(2,1)S(1)}, bf16[2,128,512]{2,1,0:T(8,128)(2,1)}, u32[]{:S(2)}) copy-start(bf16[2,128,512]{2,1,0:T(8,128)(2,1)} %constant.22.clone.xhi) | copy-start | bytes 786436
  4.0 14.3 %copy-start.8 = (f32[2,24,512]{2,1,0:T(8,128)S(1)}, f32[2,24,512]{2,1,0:T(8,128)}, u32[]{:S(2)}) copy-start(f32[2,24,512]{2,1,0:T(8,128)} %constant.20.clone.mask_ref) | copy-start | bytes 294916
  4.0 14.3 %copy-start.10 = (bf16[24,240]{1,0:T(8,128)(2,1)S(1)}, bf16[24,240]{1,0:T(8,128)(2,1)}, u32[]{:S(2)}) copy-start(bf16[24,240]{1,0:T(8,128)(2,1)} %constant.21.clone.g_ref) | copy-start | bytes 34564
  4.0 14.2 %all-to-all-start = ((f32[16,32,128]{2,1,0:T(8,128)}), f32[16,32,128]{2,1,0:T(8,128)S(1)}, u32[]{:S(2)}, u32[]{:S(2)}) async-start(f32[16,32,128]{2,1,0:T(8,128)} %bitcast.42), calls=%async_computation | async-start | bytes 524288 | tf_op jit(solution)/shard_map/all_to_all | solution.py:451
  18.3 7.0 %copy-start = (bf16[1,4,20,8192]{3,1,2,0:T(4,128)(2,1)S(1)}, bf16[1,4,20,8192]{3,1,2,0:T(4,128)(2,1)}, u32[]{:S(2)}) copy-start(bf16[1,4,20,8192]{3,1,2,0:T(4,128)(2,1)} %param.13) | copy-start | bytes 3932164
  18.3 7.0 %copy-start.1 = (bf16[20,20]{1,0:T(8,128)(2,1)S(1)}, bf16[20,20]{1,0:T(8,128)(2,1)}, u32[]{:S(2)}) copy-start(bf16[20,20]{1,0:T(8,128)(2,1)} %w_ref.3) | copy-start | bytes 2404
  18.3 7.0 %copy-start.2 = (f32[20]{0:T(128)S(1)}, f32[20]{0:T(128)}, u32[]{:S(2)}) copy-start(f32[20]{0:T(128)} %param.17) | copy-start | bytes 244
  21.0 11.5 %all-to-all-start.1 = ((f32[16,32,128]{2,1,0:T(8,128)}), f32[16,32,128]{2,1,0:T(8,128)S(1)}, u32[]{:S(2)}, u32[]{:S(2)}) async-start(f32[16,32,128]{2,1,0:T(8,128)} %get-tuple-element.19), calls=%async_computation.1 | async-start | bytes 524288 | tf_op jit(solution)/shard_map/all_to_all | solution.py:451
  25.3 7.2 %copy-start.3 = (bf16[2,256,192]{2,1,0:T(8,128)(2,1)S(1)}, bf16[2,256,192]{2,1,0:T(8,128)(2,1)}, u32[]{:S(2)}) copy-start(bf16[2,256,192]{2,1,0:T(8,128)(2,1)} %constant.18.clone.ytab_t) | copy-start | bytes 589828
  25.3 7.2 %copy-start.6 = (bf16[2,128,256]{2,1,0:T(8,128)(2,1)S(1)}, bf16[2,128,256]{2,1,0:T(8,128)(2,1)}, u32[]{:S(2)}) copy-start(bf16[2,128,256]{2,1,0:T(8,128)(2,1)} %constant.16.clone.ytab_hbm.ytab) | copy-start | bytes 393220
  25.3 7.2 %copy-start.7 = (bf16[192,256]{1,0:T(8,128)(2,1)S(1)}, bf16[192,256]{1,0:T(8,128)(2,1)}, u32[]{:S(2)}) copy-start(bf16[192,256]{1,0:T(8,128)(2,1)} %constant.19.clone.ztab_k) | copy-start | bytes 294916
  25.3 7.2 %copy-start.9 = (bf16[128,256]{1,0:T(8,128)(2,1)S(1)}, bf16[128,256]{1,0:T(8,128)(2,1)}, u32[]{:S(2)}) copy-start(bf16[128,256]{1,0:T(8,128)(2,1)} %constant.17.clone.ztab_hbm.ztab) | copy-start | bytes 196612
  26.5 1.5 %copy-start.13 = (f32[5120,128]{1,0:T(8,128)}, f32[5120,128]{1,0:T(8,128)S(1)}, u32[]{:S(2)}) copy-start(f32[5120,128]{1,0:T(8,128)S(1)} %get-tuple-element.20.local_hbm) | copy-start | bytes 7864324
  38.5 11.6 %all-to-all-start.2 = ((f32[16,32,128]{2,1,0:T(8,128)}), f32[16,32,128]{2,1,0:T(8,128)S(1)}, u32[]{:S(2)}, u32[]{:S(2)}) async-start(f32[16,32,128]{2,1,0:T(8,128)} %bitcast.15), calls=%async_computation.2 | async-start | bytes 524288 | tf_op jit(solution)/shard_map/all_to_all | solution.py:451
  42.8 1.7 %copy-start.12 = (f32[5120,128]{1,0:T(8,128)S(1)}, f32[5120,128]{1,0:T(8,128)}, u32[]{:S(2)}) copy-start(f32[5120,128]{1,0:T(8,128)} %get-tuple-element.24.x_ref) | copy-start | bytes 7864324
  46.4 1.5 %copy-start.11 = (f32[5120,128]{1,0:T(8,128)}, f32[5120,128]{1,0:T(8,128)S(1)}, u32[]{:S(2)}) copy-start(f32[5120,128]{1,0:T(8,128)S(1)} %get-tuple-element.27.local_hbm) | copy-start | bytes 7864324
  53.4 7.1 %collective-permute-start = (f32[4,40,128]{2,1,0:T(8,128)S(1)}, f32[4,40,128]{2,1,0:T(8,128)S(1)}, u32[]{:S(2)}, u32[]{:S(2)}) collective-permute-start(f32[4,40,128]{2,1,0:T(8,128)S(1)} %get-tuple-element.30), channel_id=1, source_target_pairs={{0,1},{1,0},{2,3},{3,2},{4,5},{5,4},{6,7},{7,6},{8,9},{9,8},{10,11... | collective-permute-start | bytes 245768 | tf_op jit(solution)/shard_map/ppermute | solution.py:545
  55.9 11.8 %all-to-all-start.3 = ((f32[16,32,128]{2,1,0:T(8,128)}), f32[16,32,128]{2,1,0:T(8,128)S(1)}, u32[]{:S(2)}, u32[]{:S(2)}) async-start(f32[16,32,128]{2,1,0:T(8,128)} %get-tuple-element.26), calls=%async_computation.3 | async-start | bytes 524288 | tf_op jit(solution)/shard_map/all_to_all | solution.py:451
  60.6 10.1 %collective-permute-start.1 = (f32[2,40,128]{2,1,0:T(8,128)S(1)}, f32[2,40,128]{2,1,0:T(8,128)S(1)}, u32[]{:S(2)}, u32[]{:S(2)}) collective-permute-start(f32[2,40,128]{2,1,0:T(8,128)S(1)} %pad_maximum_fusion), channel_id=1, source_target_pairs={{0,2},{1,3},{2,0},{3,1},{4,6},{5,7},{6,4},{7,5},{8,10},{9,11},{10,... | collective-permute-start | bytes 122888 | tf_op jit(solution)/shard_map/ppermute | solution.py:545
  62.3 8.4 %collective-permute-start.2 = (f32[2,40,128]{2,1,0:T(8,128)S(1)}, f32[2,40,128]{2,1,0:T(8,128)S(1)}, u32[]{:S(2)}, u32[]{:S(2)}) collective-permute-start(f32[2,40,128]{2,1,0:T(8,128)S(1)} %pad_maximum_fusion.1), channel_id=1, source_target_pairs={{0,4},{1,5},{2,6},{3,7},{4,0},{5,1},{6,2},{7,3},{8,12},{9,13},{10,... | collective-permute-start | bytes 122888 | tf_op jit(solution)/shard_map/ppermute | solution.py:545
  65.6 5.1 %collective-permute-start.3 = (f32[2,40,128]{2,1,0:T(8,128)S(1)}, f32[2,40,128]{2,1,0:T(8,128)S(1)}, u32[]{:S(2)}, u32[]{:S(2)}) collective-permute-start(f32[2,40,128]{2,1,0:T(8,128)S(1)} %pad_maximum_fusion.2), channel_id=1, source_target_pairs={{0,6},{1,7},{2,4},{3,5},{4,2},{5,3},{6,0},{7,1},{8,14},{9,15},{10,... | collective-permute-start | bytes 122888 | tf_op jit(solution)/shard_map/ppermute | solution.py:545

commit v5 on v4

--- a/solution.py
+++ b/solution.py
@@ -24,6 +24,7 @@
 PAIRS = C // 2
 CHUNK = 64
 STEPS = C // 4
+AHEAD = 3
 FAR = 1
 NEAR = (0, 2, 4, 6)
 ROWS = C * SLAB * NY
@@ -224,6 +225,12 @@
     forward_plane(u_ref, ztab, out_ref)
 
 
+def invert(quad, h_ref, ytab_t, pre_ref):
+    for k, block in enumerate(inverse_y(quad, h_ref, ytab_t)):
+        at = (4 * quad + k) * CELL_ROWS
+        pre_ref[at : at + CELL_ROWS, :] = block
+
+
 def middle_kernel(
     recv_ref, local_hbm, cot_hbm, ytab, ztab, ytab_t, ztab_k,
     act_hbm, up_hbm, out_ref,
@@ -236,15 +243,17 @@
             copy.start()
     stores = []
     inverse_plane(recv_ref, ztab_k, h_ref)
+    for quad in range(AHEAD):
+        invert(quad, h_ref, ytab_t, pre_ref)
     for quad in range(STEPS):
-        for k, block in enumerate(inverse_y(quad, h_ref, ytab_t)):
-            pre_ref[k * CELL_ROWS : (k + 1) * CELL_ROWS, :] = block
+        if quad + AHEAD < STEPS:
+            invert(quad + AHEAD, h_ref, ytab_t, pre_ref)
         local_copies[quad].wait()
         cot_copies[quad].wait()
         for i in range(QUAD_ROWS // CHUNK):
             near = slice(i * CHUNK, (i + 1) * CHUNK)
             rows = slice(quad * QUAD_ROWS + i * CHUNK, quad * QUAD_ROWS + (i + 1) * CHUNK)
-            pre = pre_ref[near, :] + local_ref[rows, :]
+            pre = pre_ref[rows, :] + local_ref[rows, :]
             cdf = 0.5 * (1.0 + lax.erf(pre * (1.0 / math.sqrt(2.0))))
             slope = cdf + pre * jnp.exp(-0.5 * pre * pre) * (1.0 / math.sqrt(2.0 * math.pi))
             act_ref[rows, :] = (pre * cdf).astype(BF16)
@@ -284,20 +293,23 @@
         grad_ref[c * 2 * C : (c + 1) * 2 * C, :] = total[:, :BLOCK_MODES]
 
 
-def last_kernel(recv_ref, local_hbm, ytab_t, ztab_k, out_hbm, token_ref, local_ref, out_ref, h_ref, sems):
+def last_kernel(recv_ref, local_hbm, ytab_t, ztab_k, out_hbm, token_ref, local_ref, out_ref, pre_ref, h_ref, sems):
     token_ref[...] = jnp.zeros_like(token_ref)
     local_copies = fetch(local_hbm, local_ref, sems, 0)
     for copy in local_copies:
         copy.start()
     stores = []
     inverse_plane(recv_ref, ztab_k, h_ref)
+    for quad in range(AHEAD):
+        invert(quad, h_ref, ytab_t, pre_ref)
     for quad in range(STEPS):
-        spectral = inverse_y(quad, h_ref, ytab_t)
+        if quad + AHEAD < STEPS:
+            invert(quad + AHEAD, h_ref, ytab_t, pre_ref)
         local_copies[quad].wait()
         for k in range(4):
             at = (4 * quad + k) * CELL_ROWS
             rows = slice(at, at + CELL_ROWS)
-            out_ref[rows, :] = (spectral[k] + local_ref[rows, :]).astype(BF16)
+            out_ref[rows, :] = (pre_ref[rows, :] + local_ref[rows, :]).astype(BF16)
         store = pltpu.make_async_copy(
             out_ref.at[quad_rows(quad)], out_hbm.at[quad_rows(quad)], sems.at[STEPS + quad]
         )
@@ -532,7 +544,7 @@
         out_specs=[pinned(), pinned(), whole(flat)],
         out_shape=rows_out + [slab_out],
         scratch_shapes=[pltpu.VMEM((ROWS, 128), dtype) for dtype in (F32, BF16, BF16, F32)]
-        + [planes, planes, pltpu.VMEM((QUAD_ROWS, 128), F32)]
+        + [planes, planes, pltpu.VMEM((ROWS, 128), F32)]
         + [pltpu.VMEM((QUAD_ROWS, 128), BF16)] * 2
         + [sems((4 * STEPS,))],
         compiler_params=params(52),
@@ -551,7 +563,7 @@
         in_specs=[whole(flat), pinned()] + inverse_specs,
         out_specs=[pinned(), whole((8, 128))],
         out_shape=[rows_out[0], jax.ShapeDtypeStruct((8, 128), F32)],
-        scratch_shapes=[pltpu.VMEM((ROWS, 128), dtype) for dtype in (F32, BF16)] + [planes, sems((2 * STEPS,))],
+        scratch_shapes=[pltpu.VMEM((ROWS, 128), dtype) for dtype in (F32, BF16, F32)] + [planes, sems((2 * STEPS,))],
         compiler_params=params(52),
         cost_estimate=cost(20),
         name="slab_out",

time: 72.6 us -> 72.2 us (level)
  no operation moved by 1% of the time
where the time goes in v5:
time: 72.2 us; the launch traced here: 71.5 us
  starting transfers between devices  27.9 us (39%)
  Pallas kernels  21.9 us (30%)
  waiting for transfers between devices  15.1 us (21%)
  local copies, waits for them, and re-layouts  5.77 us (8%)
  between operations  0.9 us (1%)
    all_to_all x4, starting transfers between devices, exchange(): lax.all_to_all(block, 'space', split_axis=0, concat_axis=0, tiled=True)  20.3 us
    all_to_all x4, waiting for transfers between devices, exchange(): lax.all_to_all(block, 'space', split_axis=0, concat_axis=0, tiled=True)  15.1 us
    ppermute x4, starting transfers between devices, swap(): lax.ppermute(block, 'sample', [(s, s ^ bits) for s in range(SAMPLES)])  7.55 us
    pallas_call x2, Pallas kernels, owner(): pl.pallas_call(functools.partial(owner_kernel, adjoint), out_shape=[owned...  5.99 us
    unnamed x31, local copies, waits for them, and re-layouts  5.76 us
    pallas_call x1, Pallas kernels, shards(): pl.pallas_call(middle_kernel, in_specs=[whole(flat), pinned(), pinned()]...  5.74 us
    pallas_call x1, Pallas kernels, shards(): pl.pallas_call(forward_kernel, in_specs=[pinned()] * 3, out_shape=slab_ou...  3.3 us
    pallas_call x2, Pallas kernels, point(): pl.pallas_call(functools.partial(point_kernel, transposed), out_shape=[ro...  2.86 us
  transfers between devices with their start and end apart: 8, of which 4 were waited for; matrix products, arithmetic and copies ran while one was open for 1% of the time, Pallas kernels for 8%

profile of v5, /device:TPU:1, one launch (start us, length us, event | category | flops | bytes accessed | tf_op | source)
XLA Modules:
  0.0 71.5 jit_solution(3326423716445289318)
XLA Ops:
  0.6 3.3 %slab_in.1 = f32[512,128]{1,0:T(8,128)} custom-call(bf16[5120,128]{1,0:T(8,128)(2,1)} %bitcast.37, bf16[2,128,256]{2,1,0:T(8,128)(2,1)} %constant.16.clone.ytab_hbm.ytab, bf16[128,256]{1,0:T(8,128)(2,1)} %constant.17.clone.ztab_hbm.ztab), custom_call_target="tpu_custom_call" | custom-call | flops 1200000000 | bytes 9000000 | tf_op jit(solution)/shard_map/slab_in/pallas_call | solution.py:527
  4.0 0.0 copy-start.4
  4.0 0.0 copy-start.5
  4.0 0.0 copy-start.8
  4.0 0.0 copy-start.10
  4.0 7.1 %all-to-all-start = ((f32[16,32,128]{2,1,0:T(8,128)}), f32[16,32,128]{2,1,0:T(8,128)S(1)}, u32[]{:S(2)}, u32[]{:S(2)}) async-start(f32[16,32,128]{2,1,0:T(8,128)} %bitcast.42), calls=%async_computation | async-start | bytes 524288 | tf_op jit(solution)/shard_map/all_to_all | solution.py:463
  11.1 1.0 %copy.17 = bf16[2,20,20,288]{3,2,1,0:T(8,128)(2,1)} copy(bf16[2,20,20,288]{3,0,2,1:T(2,128)(2,1)S(1)} %copy-done.14) | data formatting | bytes 921600 | tf_op args[2]
  12.0 6.2 %all-to-all-done.s_ref = f32[16,32,128]{2,1,0:T(8,128)S(1)} async-done(((f32[16,32,128]{2,1,0:T(8,128)}), f32[16,32,128]{2,1,0:T(8,128)S(1)}, u32[]{:S(2)}, u32[]{:S(2)}) %all-to-all-start) | async-done | bytes 262176 | tf_op jit(solution)/shard_map/all_to_all | solution.py:463
  18.3 0.0 copy-start.1
  18.3 2.7 %owner_in.1 = (f32[16,32,128]{2,1,0:T(8,128)}, f32[8,40,128]{2,1,0:T(8,128)S(1)}) custom-call(f32[16,32,128]{2,1,0:T(8,128)S(1)} %all-to-all-done.s_ref, bf16[40,20,288]{2,1,0:T(8,128)(2,1)} %bitcast.40, bf16[2,128,512]{2,1,0:T(8,128)(2,1)S(1)} %copy-done.5, bf16[2,128,512]{2,1,0:T(8,128)(2,1)S(1)} %copy-done.4, f32[2,24,512]{2,1,0:T(8,128)S(1)} %copy-done.8, ...), custom_call_target="tpu_custom_call" | custom-call | flops 1200000000 | bytes 9000000 | tf_op jit(solution)/shard_map/owner_in/pallas_call | solution.py:497
  21.0 4.3 %all-to-all-start.1 = ((f32[16,32,128]{2,1,0:T(8,128)}), f32[16,32,128]{2,1,0:T(8,128)S(1)}, u32[]{:S(2)}, u32[]{:S(2)}) async-start(f32[16,32,128]{2,1,0:T(8,128)} %get-tuple-element.19), calls=%async_computation.1 | async-start | bytes 524288 | tf_op jit(solution)/shard_map/all_to_all | solution.py:463
  25.3 0.0 copy-start.3
  25.3 0.0 copy-start.6
  25.3 0.0 copy-start.7
  25.3 0.0 copy-start.9
  25.4 1.1 %point_in.1 = (f32[5120,128]{1,0:T(8,128)S(1)}, f32[8,128]{1,0:T(8,128)}) custom-call(bf16[5120,128]{1,0:T(8,128)(2,1)S(1)} %bitcast.38, bf16[20,20]{1,0:T(8,128)(2,1)S(1)} %copy-done.1, f32[1,20]{1,0:T(1,128)S(1)} %bitcast.39), custom_call_target="tpu_custom_call" | custom-call | flops 1600000000 | bytes 12000000 | tf_op jit(solution)/shard_map/point_in/pallas_call | solution.py:517
  26.5 1.5 %copy-done.13 = f32[5120,128]{1,0:T(8,128)} copy-done((f32[5120,128]{1,0:T(8,128)}, f32[5120,128]{1,0:T(8,128)S(1)}, u32[]{:S(2)}) %copy-start.13) | copy-done | bytes 2621464
  28.0 4.6 %all-to-all-done.1 = f32[16,32,128]{2,1,0:T(8,128)S(1)} async-done(((f32[16,32,128]{2,1,0:T(8,128)}), f32[16,32,128]{2,1,0:T(8,128)S(1)}, u32[]{:S(2)}, u32[]{:S(2)}) %all-to-all-start.1) | async-done | bytes 262176 | tf_op jit(solution)/shard_map/all_to_all | solution.py:463
  32.5 5.7 %slab_mid.1 = (bf16[5120,128]{1,0:T(8,128)(2,1)}, f32[5120,128]{1,0:T(8,128)}, f32[512,128]{1,0:T(8,128)}) custom-call(f32[512,128]{1,0:T(8,128)S(1)} %bitcast.33, f32[5120,128]{1,0:T(8,128)} %copy-done.13, bf16[5120,128]{1,0:T(8,128)(2,1)} %bitcast.43, bf16[2,128,256]{2,1,0:T(8,128)(2,1)S(1)} %copy-done.6, bf16[128,256]{1,0:T(8,128)(2,1)S(1)} %copy-done.9, ...), custom_call_target="tpu_custom_call" | custom-call | flops 3200000000 | bytes 24000000 | tf_op jit(solution)/shard_map/slab_mid/pallas_call | solution.py:541
  38.3 4.3 %all-to-all-start.2 = ((f32[16,32,128]{2,1,0:T(8,128)}), f32[16,32,128]{2,1,0:T(8,128)S(1)}, u32[]{:S(2)}, u32[]{:S(2)}) async-start(f32[16,32,128]{2,1,0:T(8,128)} %bitcast.15), calls=%async_computation.2 | async-start | bytes 524288 | tf_op jit(solution)/shard_map/all_to_all | solution.py:463
  42.6 1.7 %copy-done.12 = f32[5120,128]{1,0:T(8,128)S(1)} copy-done((f32[5120,128]{1,0:T(8,128)S(1)}, f32[5120,128]{1,0:T(8,128)}, u32[]{:S(2)}) %copy-start.12) | copy-done | bytes 2621464
  44.4 1.8 %point_up.1 = (f32[5120,128]{1,0:T(8,128)S(1)}, f32[8,128]{1,0:T(8,128)S(1)}) custom-call(f32[5120,128]{1,0:T(8,128)S(1)} %copy-done.12, bf16[20,20]{1,0:T(8,128)(2,1)S(1)} %copy-done.1), custom_call_target="tpu_custom_call" | custom-call | flops 1600000000 | bytes 12000000 | tf_op jit(solution)/shard_map/point_up/pallas_call | solution.py:517
  46.1 1.5 %copy-done.11 = f32[5120,128]{1,0:T(8,128)} copy-done((f32[5120,128]{1,0:T(8,128)}, f32[5120,128]{1,0:T(8,128)S(1)}, u32[]{:S(2)}) %copy-start.11) | copy-done | bytes 2621464
  47.6 2.2 %all-to-all-done.2.s_ref = f32[16,32,128]{2,1,0:T(8,128)S(1)} async-done(((f32[16,32,128]{2,1,0:T(8,128)}), f32[16,32,128]{2,1,0:T(8,128)S(1)}, u32[]{:S(2)}, u32[]{:S(2)}) %all-to-all-start.2) | async-done | bytes 262176 | tf_op jit(solution)/shard_map/all_to_all | solution.py:463
  49.8 3.3 %owner_up.1 = (f32[16,32,128]{2,1,0:T(8,128)}, f32[40,128]{1,0:T(8,128)S(1)}, f32[40,128]{1,0:T(8,128)S(1)}, f32[40,128]{1,0:T(8,128)S(1)}, f32[40,128]{1,0:T(8,128)S(1)}, /*index=5*/f32[4,40,128]{2,1,0:T(8,128)S(1)}) custom-call(f32[16,32,128]{2,1,0:T(8,128)S(1)} %all-to-all-done.2.s_ref, bf16[40,20,288]{2,1,0:T(8,128)(2,1)} %bitcast.41, ...), custom_call_target="tpu_custom_call" | custom-call | flops 1200000000 | bytes 9000000 | tf_op jit(solution)/shard_map/owner_up/pallas_call | solution.py:497
  53.2 2.5 %collective-permute-start = (f32[4,40,128]{2,1,0:T(8,128)S(1)}, f32[4,40,128]{2,1,0:T(8,128)S(1)}, u32[]{:S(2)}, u32[]{:S(2)}) collective-permute-start(f32[4,40,128]{2,1,0:T(8,128)S(1)} %get-tuple-element.30), channel_id=1, source_target_pairs={{0,1},{1,0},{2,3},{3,2},{4,5},{5,4},{6,7},{7,6},{8,9},{9,8},{10,11... | collective-permute-start | bytes 245768 | tf_op jit(solution)/shard_map/ppermute | solution.py:557
  55.7 4.6 %all-to-all-start.3 = ((f32[16,32,128]{2,1,0:T(8,128)}), f32[16,32,128]{2,1,0:T(8,128)S(1)}, u32[]{:S(2)}, u32[]{:S(2)}) async-start(f32[16,32,128]{2,1,0:T(8,128)} %get-tuple-element.26), calls=%async_computation.3 | async-start | bytes 524288 | tf_op jit(solution)/shard_map/all_to_all | solution.py:463
  60.4 1.7 %collective-permute-start.1 = (f32[2,40,128]{2,1,0:T(8,128)S(1)}, f32[2,40,128]{2,1,0:T(8,128)S(1)}, u32[]{:S(2)}, u32[]{:S(2)}) collective-permute-start(f32[2,40,128]{2,1,0:T(8,128)S(1)} %pad_maximum_fusion), channel_id=1, source_target_pairs={{0,2},{1,3},{2,0},{3,1},{4,6},{5,7},{6,4},{7,5},{8,10},{9,11},{10,... | collective-permute-start | bytes 122888 | tf_op jit(solution)/shard_map/ppermute | solution.py:557
  62.1 3.3 %collective-permute-start.2 = (f32[2,40,128]{2,1,0:T(8,128)S(1)}, f32[2,40,128]{2,1,0:T(8,128)S(1)}, u32[]{:S(2)}, u32[]{:S(2)}) collective-permute-start(f32[2,40,128]{2,1,0:T(8,128)S(1)} %pad_maximum_fusion.1), channel_id=1, source_target_pairs={{0,4},{1,5},{2,6},{3,7},{4,0},{5,1},{6,2},{7,3},{8,12},{9,13},{10,... | collective-permute-start | bytes 122888 | tf_op jit(solution)/shard_map/ppermute | solution.py:557
  65.4 2.2 %all-to-all-done.3 = f32[16,32,128]{2,1,0:T(8,128)S(1)} async-done(((f32[16,32,128]{2,1,0:T(8,128)}), f32[16,32,128]{2,1,0:T(8,128)S(1)}, u32[]{:S(2)}, u32[]{:S(2)}) %all-to-all-start.3) | async-done | bytes 262176 | tf_op jit(solution)/shard_map/all_to_all | solution.py:463
  67.5 2.6 %slab_out.1 = (bf16[5120,128]{1,0:T(8,128)(2,1)}, f32[8,128]{1,0:T(8,128)S(1)}) custom-call(f32[512,128]{1,0:T(8,128)S(1)} %bitcast.32, f32[5120,128]{1,0:T(8,128)} %copy-done.11, bf16[2,256,192]{2,1,0:T(8,128)(2,1)S(1)} %copy-done.3, bf16[192,256]{1,0:T(8,128)(2,1)S(1)} %copy-done.7), custom_call_target="tpu_custom_call" | custom-call | flops 8000000000 | bytes 60000000 | tf_op jit(solution)/shard_map/slab_out/pallas_call | solution.py:561
  70.2 1.4 %weight_grad.1 = f32[800,36]{1,0:T(8,128)} custom-call(f32[40,128]{1,0:T(8,128)S(1)} %get-tuple-element.29.own_ref, f32[4,40,128]{2,1,0:T(8,128)S(1)} %collective-permute-done.far_ref, f32[2,40,128]{2,1,0:T(8,128)S(1)} %collective-permute-done.1.near1_ref, f32[2,40,128]{2,1,0:T(8,128)S(1)} %collective-permute-done.2.near2_ref, ...), custom_call_target="tpu_custom_call" | custom-call | flops 400000000 | bytes 3000000 | tf_op jit(solution)/shard_map/weight_grad/pallas_call | solution.py:571
  (27 shorter events, 0.1 us)
Async XLA Ops:
  0.6 10.4 %copy-start.14 = (bf16[2,20,20,288]{3,0,2,1:T(2,128)(2,1)S(1)}, bf16[2,20,20,288]{3,0,2,1:T(2,128)(2,1)}, u32[]{:S(2)}) copy-start(bf16[2,20,20,288]{3,0,2,1:T(2,128)(2,1)} %param.15) | copy-start | bytes 1382404
  4.0 14.3 %copy-start.4 = (bf16[2,128,512]{2,1,0:T(8,128)(2,1)S(1)}, bf16[2,128,512]{2,1,0:T(8,128)(2,1)}, u32[]{:S(2)}) copy-start(bf16[2,128,512]{2,1,0:T(8,128)(2,1)} %constant.23.clone.xlo) | copy-start | bytes 786436
  4.0 14.3 %copy-start.5 = (bf16[2,128,512]{2,1,0:T(8,128)(2,1)S(1)}, bf16[2,128,512]{2,1,0:T(8,128)(2,1)}, u32[]{:S(2)}) copy-start(bf16[2,128,512]{2,1,0:T(8,128)(2,1)} %constant.22.clone.xhi) | copy-start | bytes 786436
  4.0 14.3 %copy-start.8 = (f32[2,24,512]{2,1,0:T(8,128)S(1)}, f32[2,24,512]{2,1,0:T(8,128)}, u32[]{:S(2)}) copy-start(f32[2,24,512]{2,1,0:T(8,128)} %constant.20.clone.mask_ref) | copy-start | bytes 294916
  4.0 14.3 %copy-start.10 = (bf16[24,240]{1,0:T(8,128)(2,1)S(1)}, bf16[24,240]{1,0:T(8,128)(2,1)}, u32[]{:S(2)}) copy-start(bf16[24,240]{1,0:T(8,128)(2,1)} %constant.21.clone.g_ref) | copy-start | bytes 34564
  4.0 14.2 %all-to-all-start = ((f32[16,32,128]{2,1,0:T(8,128)}), f32[16,32,128]{2,1,0:T(8,128)S(1)}, u32[]{:S(2)}, u32[]{:S(2)}) async-start(f32[16,32,128]{2,1,0:T(8,128)} %bitcast.42), calls=%async_computation | async-start | bytes 524288 | tf_op jit(solution)/shard_map/all_to_all | solution.py:463
  18.3 7.0 %copy-start = (bf16[1,4,20,8192]{3,1,2,0:T(4,128)(2,1)S(1)}, bf16[1,4,20,8192]{3,1,2,0:T(4,128)(2,1)}, u32[]{:S(2)}) copy-start(bf16[1,4,20,8192]{3,1,2,0:T(4,128)(2,1)} %param.13) | copy-start | bytes 3932164
  18.3 7.0 %copy-start.1 = (bf16[20,20]{1,0:T(8,128)(2,1)S(1)}, bf16[20,20]{1,0:T(8,128)(2,1)}, u32[]{:S(2)}) copy-start(bf16[20,20]{1,0:T(8,128)(2,1)} %w_ref.3) | copy-start | bytes 2404
  18.3 7.0 %copy-start.2 = (f32[20]{0:T(128)S(1)}, f32[20]{0:T(128)}, u32[]{:S(2)}) copy-start(f32[20]{0:T(128)} %param.17) | copy-start | bytes 244
  21.0 11.5 %all-to-all-start.1 = ((f32[16,32,128]{2,1,0:T(8,128)}), f32[16,32,128]{2,1,0:T(8,128)S(1)}, u32[]{:S(2)}, u32[]{:S(2)}) async-start(f32[16,32,128]{2,1,0:T(8,128)} %get-tuple-element.19), calls=%async_computation.1 | async-start | bytes 524288 | tf_op jit(solution)/shard_map/all_to_all | solution.py:463
  25.3 7.2 %copy-start.3 = (bf16[2,256,192]{2,1,0:T(8,128)(2,1)S(1)}, bf16[2,256,192]{2,1,0:T(8,128)(2,1)}, u32[]{:S(2)}) copy-start(bf16[2,256,192]{2,1,0:T(8,128)(2,1)} %constant.18.clone.ytab_t) | copy-start | bytes 589828
  25.3 7.2 %copy-start.6 = (bf16[2,128,256]{2,1,0:T(8,128)(2,1)S(1)}, bf16[2,128,256]{2,1,0:T(8,128)(2,1)}, u32[]{:S(2)}) copy-start(bf16[2,128,256]{2,1,0:T(8,128)(2,1)} %constant.16.clone.ytab_hbm.ytab) | copy-start | bytes 393220
  25.3 7.2 %copy-start.7 = (bf16[192,256]{1,0:T(8,128)(2,1)S(1)}, bf16[192,256]{1,0:T(8,128)(2,1)}, u32[]{:S(2)}) copy-start(bf16[192,256]{1,0:T(8,128)(2,1)} %constant.19.clone.ztab_k) | copy-start | bytes 294916
  25.3 7.2 %copy-start.9 = (bf16[128,256]{1,0:T(8,128)(2,1)S(1)}, bf16[128,256]{1,0:T(8,128)(2,1)}, u32[]{:S(2)}) copy-start(bf16[128,256]{1,0:T(8,128)(2,1)} %constant.17.clone.ztab_hbm.ztab) | copy-start | bytes 196612
  26.5 1.5 %copy-start.13 = (f32[5120,128]{1,0:T(8,128)}, f32[5120,128]{1,0:T(8,128)S(1)}, u32[]{:S(2)}) copy-start(f32[5120,128]{1,0:T(8,128)S(1)} %get-tuple-element.20.local_hbm) | copy-start | bytes 7864324
  38.3 11.6 %all-to-all-start.2 = ((f32[16,32,128]{2,1,0:T(8,128)}), f32[16,32,128]{2,1,0:T(8,128)S(1)}, u32[]{:S(2)}, u32[]{:S(2)}) async-start(f32[16,32,128]{2,1,0:T(8,128)} %bitcast.15), calls=%async_computation.2 | async-start | bytes 524288 | tf_op jit(solution)/shard_map/all_to_all | solution.py:463
  42.6 1.7 %copy-start.12 = (f32[5120,128]{1,0:T(8,128)S(1)}, f32[5120,128]{1,0:T(8,128)}, u32[]{:S(2)}) copy-start(f32[5120,128]{1,0:T(8,128)} %get-tuple-element.24.x_ref) | copy-start | bytes 7864324
  46.1 1.5 %copy-start.11 = (f32[5120,128]{1,0:T(8,128)}, f32[5120,128]{1,0:T(8,128)S(1)}, u32[]{:S(2)}) copy-start(f32[5120,128]{1,0:T(8,128)S(1)} %get-tuple-element.27.local_hbm) | copy-start | bytes 7864324
  53.2 7.2 %collective-permute-start = (f32[4,40,128]{2,1,0:T(8,128)S(1)}, f32[4,40,128]{2,1,0:T(8,128)S(1)}, u32[]{:S(2)}, u32[]{:S(2)}) collective-permute-start(f32[4,40,128]{2,1,0:T(8,128)S(1)} %get-tuple-element.30), channel_id=1, source_target_pairs={{0,1},{1,0},{2,3},{3,2},{4,5},{5,4},{6,7},{7,6},{8,9},{9,8},{10,11... | collective-permute-start | bytes 245768 | tf_op jit(solution)/shard_map/ppermute | solution.py:557
  55.7 11.8 %all-to-all-start.3 = ((f32[16,32,128]{2,1,0:T(8,128)}), f32[16,32,128]{2,1,0:T(8,128)S(1)}, u32[]{:S(2)}, u32[]{:S(2)}) async-start(f32[16,32,128]{2,1,0:T(8,128)} %get-tuple-element.26), calls=%async_computation.3 | async-start | bytes 524288 | tf_op jit(solution)/shard_map/all_to_all | solution.py:463
  60.4 9.8 %collective-permute-start.1 = (f32[2,40,128]{2,1,0:T(8,128)S(1)}, f32[2,40,128]{2,1,0:T(8,128)S(1)}, u32[]{:S(2)}, u32[]{:S(2)}) collective-permute-start(f32[2,40,128]{2,1,0:T(8,128)S(1)} %pad_maximum_fusion), channel_id=1, source_target_pairs={{0,2},{1,3},{2,0},{3,1},{4,6},{5,7},{6,4},{7,5},{8,10},{9,11},{10,... | collective-permute-start | bytes 122888 | tf_op jit(solution)/shard_map/ppermute | solution.py:557
  62.1 8.1 %collective-permute-start.2 = (f32[2,40,128]{2,1,0:T(8,128)S(1)}, f32[2,40,128]{2,1,0:T(8,128)S(1)}, u32[]{:S(2)}, u32[]{:S(2)}) collective-permute-start(f32[2,40,128]{2,1,0:T(8,128)S(1)} %pad_maximum_fusion.1), channel_id=1, source_target_pairs={{0,4},{1,5},{2,6},{3,7},{4,0},{5,1},{6,2},{7,3},{8,12},{9,13},{10,... | collective-permute-start | bytes 122888 | tf_op jit(solution)/shard_map/ppermute | solution.py:557
  65.4 4.8 %collective-permute-start.3 = (f32[2,40,128]{2,1,0:T(8,128)S(1)}, f32[2,40,128]{2,1,0:T(8,128)S(1)}, u32[]{:S(2)}, u32[]{:S(2)}) collective-permute-start(f32[2,40,128]{2,1,0:T(8,128)S(1)} %pad_maximum_fusion.2), channel_id=1, source_target_pairs={{0,6},{1,7},{2,4},{3,5},{4,2},{5,3},{6,0},{7,1},{8,14},{9,15},{10,... | collective-permute-start | bytes 122888 | tf_op jit(solution)/shard_map/ppermute | solution.py:557
